TPU v7x, 32 devices: a whole 2x2x4 slice. The times are simulated.
32 devices in a mesh: batch: 8 (over z, core), seq: 4 (over y, x).
Axes of the slice: x: 2, y: 2, z: 4, core: 2. Of those that a mesh axis runs over, the one named last changes fastest.
Arguments:
- inputs: bfloat16 [16, 1024, 2048], P('batch', 'seq'), may hold values from -6 to 6
- cotangent: bfloat16 [16, 1024, 2048], P('batch', 'seq'), may hold values from -6 to 6
- max_exit: int32 [16], P('batch'), may hold values from 5 to 24, as said below
- min_exit: int32 [16], P('batch'), may hold values from 1 to 24
- layer: int32 [1], replicated, may hold values from 4 to 19
- wq: bfloat16 [2048, 2048], P(('batch', 'seq')), may hold values from -0.125 to 0.125
- wk: bfloat16 [2048, 2048], P(('batch', 'seq')), may hold values from -0.125 to 0.125
- wv: bfloat16 [2048, 2048], P(('batch', 'seq')), may hold values from -0.125 to 0.125
- wo: bfloat16 [2048, 2048], P(('batch', 'seq')), may hold values from -0.5 to 0.5
- gain_one: bfloat16 [2048], P(('batch', 'seq')), may hold values from 0.25 to 1.75
- shift_one: bfloat16 [2048], P(('batch', 'seq')), may hold values from -3 to 3
- bias_q: bfloat16 [2048], P(('batch', 'seq')), may hold values from -3 to 3
- bias_v: bfloat16 [2048], P(('batch', 'seq')), may hold values from -3 to 3
- bias_o: bfloat16 [2048], P(('batch', 'seq')), may hold values from -3 to 3
- w_in: bfloat16 [2048, 8192], P(('batch', 'seq')), may hold values from -0.125 to 0.125
- w_out: bfloat16 [8192, 2048], P(('batch', 'seq')), may hold values from -0.09375 to 0.09375
- gain_two: bfloat16 [2048], P(('batch', 'seq')), may hold values from 0.25 to 1.75
- shift_two: bfloat16 [2048], P(('batch', 'seq')), may hold values from -3 to 3
- bias_in: bfloat16 [8192], P(('batch', 'seq')), may hold values from -3 to 3
- bias_out: bfloat16 [2048], P(('batch', 'seq')), may hold values from -3 to 3
Outputs:
- output: bfloat16 [16, 1024, 2048], P('batch', 'seq')
- input_grad: bfloat16 [16, 1024, 2048], P('batch', 'seq')
- query_weight_gradient: float32 [2048, 2048], P(('batch', 'seq'))
- key_weight_gradient: float32 [2048, 2048], P(('batch', 'seq'))
- value_weight_gradient: float32 [2048, 2048], P(('batch', 'seq'))
- output_weight_gradient: float32 [2048, 2048], P(('batch', 'seq'))
- grad_gain_one: float32 [2048], P(('batch', 'seq'))
- grad_shift_one: float32 [2048], P(('batch', 'seq'))
- grad_bias_q: float32 [2048], P(('batch', 'seq'))
- grad_bias_v: float32 [2048], P(('batch', 'seq'))
- grad_bias_o: float32 [2048], P(('batch', 'seq'))
- input_weight_gradient: float32 [2048, 8192], P(('batch', 'seq'))
- grad_w_out: float32 [8192, 2048], P(('batch', 'seq'))
- grad_gain_two: float32 [2048], P(('batch', 'seq'))
- grad_shift_two: float32 [2048], P(('batch', 'seq'))
- grad_bias_in: float32 [8192], P(('batch', 'seq'))
- grad_bias_out: float32 [2048], P(('batch', 'seq'))
Inputs may be any that keep to these rules, and one draw needn't show every extreme that they name: Every sequence has max_exit >= min_exit and max_exit > layer[0]; in each of the aligned groups of 2 sequences exactly one has min_exit > layer[0].
All inputs are finite; a program needn't handle non-finite values.
Results may differ from a plain program's by a relative error of at most 0.015.
Values may be sent and summed in bfloat16 or wider, within the bound.
No kernel may reach another device: no remote copies, remote signals or barrier semaphores. Data moves between devices by JAX's collectives and lax.ppermute only.
A program may use at most 448 MiB of HBM per device.

v0:
```python
from functools import partial

import jax
import jax.numpy as jnp
from jax import lax
from jax.sharding import PartitionSpec as P

HEADS = 32
HEAD_DIM = 64


epsilon = 1e-05
head_blocks = 4


def layer_norm(values_in, norm_gain, norm_shift):
    average = jnp.mean(values_in, -1, keepdims=True)
    centered = values_in - average
    spread = jnp.mean(centered * centered, -1, keepdims=True)
    return centered * lax.rsqrt(spread + epsilon) * norm_gain + norm_shift


def by_heads(tensor):
    parted = tensor.reshape(
        tensor.shape[0], tensor.shape[1], head_blocks, HEADS // head_blocks, HEAD_DIM
    )
    return jnp.moveaxis(parted, 2, 0)


def from_heads(tensor):
    moved = jnp.moveaxis(tensor, 0, 2)
    return moved.reshape(moved.shape[0], moved.shape[1], -1)


def masked_logits(query, keys, causal, scaling):
    logits = (
        jnp.einsum("bqhe,bkhe->bhqk", query, keys, preferred_element_type=jnp.float32) * scaling
    )
    return jnp.where(causal[None, None], logits, -1e30)


def attend(causal, scaling, members):
    query, keys, values = members
    logits = masked_logits(query, keys, causal, scaling)
    top = jnp.max(logits, -1, keepdims=True)
    log_total = top + jnp.log(jnp.sum(jnp.exp(logits - top), -1, keepdims=True))
    probs = jnp.exp(logits - log_total).astype(jnp.bfloat16)
    attended_context = jnp.einsum(
        "bhqk,bkhe->bqhe", probs, values, preferred_element_type=jnp.float32
    )
    return (attended_context, log_total)


def attend_back(causal, scaling, members):
    query, keys, values, grad_context, log_total = members
    probs = jnp.exp(masked_logits(query, keys, causal, scaling) - log_total)
    grad_probs = jnp.einsum(
        "bqhe,bkhe->bhqk", grad_context, values, preferred_element_type=jnp.float32
    )
    inner = jnp.sum(grad_probs * probs, -1, keepdims=True)
    grad_raw = (probs * (grad_probs - inner) * scaling).astype(jnp.bfloat16)
    query_gradient = jnp.einsum(
        "bhqk,bkhe->bqhe", grad_raw, keys, preferred_element_type=jnp.float32
    )
    key_gradient = jnp.einsum(
        "bhqk,bqhe->bkhe", grad_raw, query, preferred_element_type=jnp.float32
    )
    value_gradient = jnp.einsum(
        "bhqk,bqhe->bkhe",
        probs.astype(jnp.bfloat16),
        grad_context,
        preferred_element_type=jnp.float32,
    )
    return (query_gradient, key_gradient, value_gradient)


def token_sum(tensor):
    return jnp.sum(tensor.astype(jnp.float32), axis=(0, 1))


def body(
    inputs,
    cotangent,
    max_exit,
    min_exit,
    layer,
    wq,
    wk,
    wv,
    wo,
    gain_one,
    shift_one,
    bias_q,
    bias_v,
    bias_o,
    w_in,
    w_out,
    gain_two,
    shift_two,
    bias_in,
    bias_out,
):
    block_len = inputs.shape[1]
    full_len = block_len * lax.axis_size("seq")
    q_places = lax.axis_index("seq") * block_len + jnp.arange(block_len, dtype=jnp.int32)
    k_places = jnp.arange(full_len, dtype=jnp.int32)
    causal = q_places[:, None] >= k_places[None, :]
    exits = max_exit[:, None] - (max_exit - min_exit)[:, None] * q_places[None, :] // (full_len - 1)
    active = (layer[0] < exits).astype(jnp.float32)[..., None]
    scaling = HEAD_DIM ** (-0.5)
    (
        full_wq,
        full_wk,
        full_wv,
        full_wo,
        full_gain_one,
        full_shift_one,
        full_bias_q,
        full_bias_v,
        full_bias_o,
        full_gain_two,
        full_shift_two,
        full_bias_out,
    ) = (
        lax.all_gather(wq, ("batch", "seq"), axis=0, tiled=True),
        lax.all_gather(wk, ("batch", "seq"), axis=0, tiled=True),
        lax.all_gather(wv, ("batch", "seq"), axis=0, tiled=True),
        lax.all_gather(wo, ("batch", "seq"), axis=0, tiled=True),
        lax.all_gather(gain_one, ("batch", "seq"), axis=0, tiled=True),
        lax.all_gather(shift_one, ("batch", "seq"), axis=0, tiled=True),
        lax.all_gather(bias_q, ("batch", "seq"), axis=0, tiled=True),
        lax.all_gather(bias_v, ("batch", "seq"), axis=0, tiled=True),
        lax.all_gather(bias_o, ("batch", "seq"), axis=0, tiled=True),
        lax.all_gather(gain_two, ("batch", "seq"), axis=0, tiled=True),
        lax.all_gather(shift_two, ("batch", "seq"), axis=0, tiled=True),
        lax.all_gather(bias_out, ("batch", "seq"), axis=0, tiled=True),
    )
    gain_a = full_gain_one.astype(jnp.float32)
    shift_a = full_shift_one.astype(jnp.float32)
    start = inputs.astype(jnp.float32)
    normalized_rows = layer_norm(start, gain_a, shift_a).astype(jnp.bfloat16)
    query = (
        jnp.dot(normalized_rows, full_wq, preferred_element_type=jnp.float32)
        + full_bias_q.astype(jnp.float32)
    ).astype(jnp.bfloat16)
    keys = jnp.dot(normalized_rows, full_wk, preferred_element_type=jnp.float32).astype(
        jnp.bfloat16
    )
    values = (
        jnp.dot(normalized_rows, full_wv, preferred_element_type=jnp.float32)
        + full_bias_v.astype(jnp.float32)
    ).astype(jnp.bfloat16)
    keys_all, values_all = (
        lax.all_gather(keys, "seq", axis=1, tiled=True),
        lax.all_gather(values, "seq", axis=1, tiled=True),
    )
    context_heads, log_total = lax.map(
        partial(attend, causal, scaling),
        (by_heads(query), by_heads(keys_all), by_heads(values_all)),
    )
    attended_context = from_heads(context_heads).astype(jnp.bfloat16)
    branch = jnp.dot(
        attended_context, full_wo, preferred_element_type=jnp.float32
    ) + full_bias_o.astype(jnp.float32)
    middle = start + active * branch
    gain_b = full_gain_two.astype(jnp.float32)
    shift_b = full_shift_two.astype(jnp.float32)
    second_normalized_rows = layer_norm(middle, gain_b, shift_b).astype(jnp.bfloat16)
    complete_input_weight, complete_output_weight, full_bias_in = (
        lax.all_gather(w_in, ("batch", "seq"), axis=0, tiled=True),
        lax.all_gather(w_out, ("batch", "seq"), axis=0, tiled=True),
        lax.all_gather(bias_in, ("batch", "seq"), axis=0, tiled=True),
    )
    hidden_pre = jnp.dot(
        second_normalized_rows, complete_input_weight, preferred_element_type=jnp.float32
    ) + full_bias_in.astype(jnp.float32)
    hidden_state = jax.nn.gelu(hidden_pre, approximate=False).astype(jnp.bfloat16)
    branch_two = jnp.dot(
        hidden_state, complete_output_weight, preferred_element_type=jnp.float32
    ) + full_bias_out.astype(jnp.float32)
    output = (middle + active * branch_two).astype(jnp.bfloat16)
    grad_out = cotangent.astype(jnp.float32)
    second_branch_gradient = (active * grad_out).astype(jnp.bfloat16)
    grad_bias_out = token_sum(second_branch_gradient)
    _, gelu_pull = jax.vjp(partial(jax.nn.gelu, approximate=False), hidden_pre)
    grad_w_out = jnp.einsum(
        "agt,agm->tm", hidden_state, second_branch_gradient, preferred_element_type=jnp.float32
    )
    grad_hidden = jnp.einsum(
        "jgp,mp->jgm",
        second_branch_gradient,
        complete_output_weight,
        preferred_element_type=jnp.float32,
    )
    preactivation_gradient = gelu_pull(grad_hidden)[0].astype(jnp.bfloat16)
    input_weight_gradient = jnp.einsum(
        "zmv,zme->ve",
        second_normalized_rows,
        preactivation_gradient,
        preferred_element_type=jnp.float32,
    )
    grad_bias_in = token_sum(preactivation_gradient)
    grad_normed_two = jnp.einsum(
        "pyk,uk->pyu",
        preactivation_gradient,
        complete_input_weight,
        preferred_element_type=jnp.float32,
    )
    sum_w_in, sum_w_out, sum_bias_in = (
        lax.psum_scatter(input_weight_gradient, ("batch", "seq"), scatter_dimension=0, tiled=True),
        lax.psum_scatter(grad_w_out, ("batch", "seq"), scatter_dimension=0, tiled=True),
        lax.psum_scatter(grad_bias_in, ("batch", "seq"), scatter_dimension=0, tiled=True),
    )
    _, norm_pull_two = jax.vjp(layer_norm, middle, gain_b, shift_b)
    grad_middle_norm, grad_gain_two, grad_shift_two = norm_pull_two(grad_normed_two)
    grad_middle = grad_out + grad_middle_norm
    backward_query_weight, backward_key_weight, backward_value_weight, backward_output_weight = (
        lax.all_gather(wq, ("batch", "seq"), axis=0, tiled=True),
        lax.all_gather(wk, ("batch", "seq"), axis=0, tiled=True),
        lax.all_gather(wv, ("batch", "seq"), axis=0, tiled=True),
        lax.all_gather(wo, ("batch", "seq"), axis=0, tiled=True),
    )
    branch_gradient = (active * grad_middle).astype(jnp.bfloat16)
    output_weight_gradient = jnp.einsum(
        "zhg,zhn->gn", attended_context, branch_gradient, preferred_element_type=jnp.float32
    )
    grad_bias_o = token_sum(branch_gradient)
    grad_context = jnp.einsum(
        "nza,fa->nzf", branch_gradient, backward_output_weight, preferred_element_type=jnp.float32
    ).astype(jnp.bfloat16)
    grad_q_heads, grad_k_heads, grad_v_heads = lax.map(
        partial(attend_back, causal, scaling),
        (
            by_heads(query),
            by_heads(keys_all),
            by_heads(values_all),
            by_heads(grad_context),
            log_total,
        ),
    )
    query_gradient = from_heads(grad_q_heads).astype(jnp.bfloat16)
    grad_keys_sum, grad_values_sum = (
        lax.psum_scatter(
            from_heads(grad_k_heads).astype(jnp.bfloat16), "seq", scatter_dimension=1, tiled=True
        ).astype(jnp.float32),
        lax.psum_scatter(
            from_heads(grad_v_heads).astype(jnp.bfloat16), "seq", scatter_dimension=1, tiled=True
        ).astype(jnp.float32),
    )
    key_gradient = grad_keys_sum.astype(jnp.bfloat16)
    value_gradient = grad_values_sum.astype(jnp.bfloat16)
    query_weight_gradient = jnp.einsum(
        "ywv,ywc->vc", normalized_rows, query_gradient, preferred_element_type=jnp.float32
    )
    key_weight_gradient = jnp.einsum(
        "ywv,ywc->vc", normalized_rows, key_gradient, preferred_element_type=jnp.float32
    )
    value_weight_gradient = jnp.einsum(
        "ywv,ywc->vc", normalized_rows, value_gradient, preferred_element_type=jnp.float32
    )
    grad_bias_q = token_sum(query_gradient)
    grad_bias_v = token_sum(value_gradient)
    normalized_gradient = jnp.einsum(
        "hit,ft->hif", query_gradient, backward_query_weight, preferred_element_type=jnp.float32
    )
    normalized_gradient = normalized_gradient + jnp.einsum(
        "hit,ft->hif", key_gradient, backward_key_weight, preferred_element_type=jnp.float32
    )
    normalized_gradient = normalized_gradient + jnp.einsum(
        "hit,ft->hif", value_gradient, backward_value_weight, preferred_element_type=jnp.float32
    )
    _, norm_pull_one = jax.vjp(layer_norm, start, gain_a, shift_a)
    grad_start_norm, grad_gain_one, grad_shift_one = norm_pull_one(normalized_gradient)
    input_grad = (grad_middle + grad_start_norm).astype(jnp.bfloat16)
    (
        sum_wq,
        sum_wk,
        sum_wv,
        sum_wo,
        sum_gain_one,
        sum_shift_one,
        sum_bias_q,
        sum_bias_v,
        sum_bias_o,
        sum_gain_two,
        sum_shift_two,
        sum_bias_out,
    ) = (
        lax.psum_scatter(query_weight_gradient, ("batch", "seq"), scatter_dimension=0, tiled=True),
        lax.psum_scatter(key_weight_gradient, ("batch", "seq"), scatter_dimension=0, tiled=True),
        lax.psum_scatter(value_weight_gradient, ("batch", "seq"), scatter_dimension=0, tiled=True),
        lax.psum_scatter(output_weight_gradient, ("batch", "seq"), scatter_dimension=0, tiled=True),
        lax.psum_scatter(grad_gain_one, ("batch", "seq"), scatter_dimension=0, tiled=True),
        lax.psum_scatter(grad_shift_one, ("batch", "seq"), scatter_dimension=0, tiled=True),
        lax.psum_scatter(grad_bias_q, ("batch", "seq"), scatter_dimension=0, tiled=True),
        lax.psum_scatter(grad_bias_v, ("batch", "seq"), scatter_dimension=0, tiled=True),
        lax.psum_scatter(grad_bias_o, ("batch", "seq"), scatter_dimension=0, tiled=True),
        lax.psum_scatter(grad_gain_two, ("batch", "seq"), scatter_dimension=0, tiled=True),
        lax.psum_scatter(grad_shift_two, ("batch", "seq"), scatter_dimension=0, tiled=True),
        lax.psum_scatter(grad_bias_out, ("batch", "seq"), scatter_dimension=0, tiled=True),
    )
    return (
        output,
        input_grad,
        sum_wq,
        sum_wk,
        sum_wv,
        sum_wo,
        sum_gain_one,
        sum_shift_one,
        sum_bias_q,
        sum_bias_v,
        sum_bias_o,
        sum_w_in,
        sum_w_out,
        sum_gain_two,
        sum_shift_two,
        sum_bias_in,
        sum_bias_out,
    )


def solution(mesh):
    placed = (
        P("batch", "seq", None),
        P("batch", "seq", None),
        P("batch"),
        P("batch"),
        P(),
        P(("batch", "seq"), None),
        P(("batch", "seq"), None),
        P(("batch", "seq"), None),
        P(("batch", "seq"), None),
        P(("batch", "seq")),
        P(("batch", "seq")),
        P(("batch", "seq")),
        P(("batch", "seq")),
        P(("batch", "seq")),
        P(("batch", "seq"), None),
        P(("batch", "seq"), None),
        P(("batch", "seq")),
        P(("batch", "seq")),
        P(("batch", "seq")),
        P(("batch", "seq")),
    )
    return jax.shard_map(
        body,
        mesh=mesh,
        in_specs=placed,
        out_specs=(
            P("batch", "seq", None),
            P("batch", "seq", None),
            P(("batch", "seq"), None),
            P(("batch", "seq"), None),
            P(("batch", "seq"), None),
            P(("batch", "seq"), None),
            P(("batch", "seq")),
            P(("batch", "seq")),
            P(("batch", "seq")),
            P(("batch", "seq")),
            P(("batch", "seq")),
            P(("batch", "seq"), None),
            P(("batch", "seq"), None),
            P(("batch", "seq")),
            P(("batch", "seq")),
            P(("batch", "seq")),
            P(("batch", "seq")),
        ),
        check_vma=False,
    )
```

profile of v0, /device:TPU:0, one launch (start us, length us, event | category | flops | bytes accessed | tf_op | source)
XLA Modules:
  0.0 5961.0 jit_solution(16203373061464316132)
XLA Ops:
  16.3 43.4 all-reduce.18
  100.6 69.9 %all-gather.16.cloned.1.call-done = bf16[2048,2048]{1,0:T(8,128)(2,1)} async-done(((bf16[64,2048]{1,0:T(8,128)(2,1)}), bf16[2048,2048]{1,0:T(8,128)(2,1)}) %all-gather.16.cloned.1.call-update) | async-done | bytes 8388624 | tf_op jit(solution)/shard_map/all_gather | solution.py:126
  182.5 66.3 %all-gather = bf16[32,1,256]{2,1,0:T(2,128)(2,1)S(1)} all-gather(bf16[1,1,256]{2,1,0:T(2,128)(2,1)S(1)} %reshape.238), channel_id=1, replica_groups=mesh['batch'=8,'seq'=4] {'batch','seq'}, dimensions={0}, use_global_device_ids=true | all-gather | bytes 16896 | tf_op jit(solution)/shard_map/all_gather | solution.py:172
  266.4 72.0 %all-gather.12.cloned.1.call-done = bf16[2,1024,2048]{2,1,0:T(8,128)(2,1)} async-done(((bf16[2,256,2048]{2,1,0:T(8,128)(2,1)}), bf16[2,1024,2048]{2,1,0:T(8,128)(2,1)}) %all-gather.12.cloned.1.call-update) | async-done | bytes 8388624 | tf_op jit(solution)/shard_map/all_gather | solution.py:155
  359.6 68.7 %all-gather.18.cloned.1.call-done = bf16[2,1024,2048]{2,1,0:T(8,128)(2,1)} async-done(((bf16[2,256,2048]{2,1,0:T(8,128)(2,1)}), bf16[2,1024,2048]{2,1,0:T(8,128)(2,1)}) %all-gather.18.cloned.1.call-update) | async-done | bytes 8388624 | tf_op jit(solution)/shard_map/all_gather | solution.py:154
  450.1 65.6 %while.28 = (s32[]{:T(128)}, bf16[4,2,256,8,64]{2,4,3,0,1:T(8,128)(2,1)}, f32[4,2,8,256,1]{3,2,1,4,0:T(8,128)}, bf16[4,2,1024,8,64]{2,4,3,1,0:T(8,128)(2,1)}, bf...) while((s32[]{:T(128)}, ...), condition=%wide.region_5.6_spmd.clone, body=%wide.region_2.5_spmd.clone.sunk | while | flops 1120137216 | bytes 57281632 | solution.py:157
  526.9 178.0 %all-gather.22.cloned.1.call-done = bf16[2048,8192]{1,0:T(8,128)(2,1)} async-done(((bf16[64,8192]{1,0:T(8,128)(2,1)}), bf16[2048,8192]{1,0:T(8,128)(2,1)}) %all-gather.22.cloned.1.call-update) | async-done | bytes 33554448 | tf_op jit(solution)/shard_map/all_gather | solution.py:170
  737.4 41.7 multiply_convert_fusion.1
  779.0 121.7 %all-gather.24.cloned.1.call-done = bf16[8192,2048]{1,0:T(8,128)(2,1)} async-done(((bf16[256,2048]{1,0:T(8,128)(2,1)}), bf16[8192,2048]{1,0:T(8,128)(2,1)}) %all-gather.24.cloned.1.call-update) | async-done | bytes 33554448 | tf_op jit(solution)/shard_map/all_gather | solution.py:171
  900.8 33.4 convert_reduce_fusion
  982.3 392.1 %while.29 = (s32[]{:T(128)}, bf16[4,2,256,8,64]{2,4,3,0,1:T(8,128)(2,1)}, bf16[4,2,1024,8,64]{2,4,3,0,1:T(8,128)(2,1)}, bf16[4,2,1024,8,64]{2,4,3,0,1:T(8,128)(2...) while((s32[]{:T(128)}, ...), condition=%wide.region_12.13_spmd.clone, body=%wide.region_10.12_spmd.clone.sunk | while | flops 2793678848 | bytes 204069008 | solution.py:231
  1033.7 35.6 bitcast_dynamic-update-slice_fusion.7
  1131.5 35.6 bitcast_dynamic-update-slice_fusion.7
  1229.4 35.6 bitcast_dynamic-update-slice_fusion.7
  1327.3 35.6 bitcast_dynamic-update-slice_fusion.7
  1387.5 71.8 %reduce-scatter.9.cloned.1.call-done = bf16[2,256,2048]{1,2,0:T(8,128)(2,1)} async-done(((bf16[2,1024,2048]{1,2,0:T(8,128)(2,1)}), bf16[2,256,2048]{1,2,0:T(8,128)(2,1)}) %reduce-scatter.9.cloned.1.call-update) | async-done | bytes 2097168 | tf_op jit(solution)/shard_map/reduce_scatter | solution.py:243
  1469.9 78.9 %reduce-scatter.11.cloned.1.call-done = bf16[2,256,2048]{1,2,0:T(8,128)(2,1)} async-done(((bf16[2,1024,2048]{1,2,0:T(8,128)(2,1)}), bf16[2,256,2048]{1,2,0:T(8,128)(2,1)}) %reduce-scatter.11.cloned.1.call-update) | async-done | bytes 2097168 | tf_op jit(solution)/shard_map/reduce_scatter | solution.py:246
  1610.0 32.5 convolution_bitcast_fusion.1
  1714.9 337.2 %reduce-scatter.13.cloned.1.call-done = f32[64,2048]{1,0:T(8,128)} async-done(((f32[2048,2048]{1,0:T(8,128)}), f32[64,2048]{1,0:T(8,128)}) %reduce-scatter.13.cloned.1.call-update) | async-done | bytes 524304 | tf_op jit(solution)/shard_map/reduce_scatter | solution.py:289
  2052.1 362.0 %reduce-scatter.19.cloned.1.call-done = f32[64,2048]{1,0:T(8,128)} async-done(((f32[2048,2048]{1,0:T(8,128)}), f32[64,2048]{1,0:T(8,128)}) %reduce-scatter.19.cloned.1.call-update) | async-done | bytes 524304 | tf_op jit(solution)/shard_map/reduce_scatter | solution.py:292
  2414.1 361.9 %reduce-scatter.15.cloned.1.call-done = f32[64,2048]{1,0:T(8,128)} async-done(((f32[2048,2048]{1,0:T(8,128)}), f32[64,2048]{1,0:T(8,128)}) %reduce-scatter.15.cloned.1.call-update) | async-done | bytes 524304 | tf_op jit(solution)/shard_map/reduce_scatter | solution.py:290
  2776.1 361.9 %reduce-scatter.17.cloned.1.call-done = f32[64,2048]{1,0:T(8,128)} async-done(((f32[2048,2048]{1,0:T(8,128)}), f32[64,2048]{1,0:T(8,128)}) %reduce-scatter.17.cloned.1.call-update) | async-done | bytes 524304 | tf_op jit(solution)/shard_map/reduce_scatter | solution.py:291
  3138.0 1408.7 %reduce-scatter.21.cloned.1.call-done = f32[64,8192]{1,0:T(8,128)} async-done(((f32[2048,8192]{1,0:T(8,128)}), f32[64,8192]{1,0:T(8,128)}) %reduce-scatter.21.cloned.1.call-update) | async-done | bytes 2097168 | tf_op jit(solution)/shard_map/reduce_scatter | solution.py:210
  4546.7 1407.5 %reduce-scatter.23.cloned.1.call-done = f32[256,2048]{1,0:T(8,128)} async-done(((f32[8192,2048]{1,0:T(8,128)}), f32[256,2048]{1,0:T(8,128)}) %reduce-scatter.23.cloned.1.call-update) | async-done | bytes 2097168 | tf_op jit(solution)/shard_map/reduce_scatter | solution.py:211
  (256 shorter events, 685.0 us)
Async XLA Ops:
  7.2 84.2 %all-gather.10.cloned.1.call-start = ((), (), s32[]{:S(2)}) async-start(), calls=%async_computation.8 | async-start | bytes 8650752 | tf_op jit(solution)/shard_map/all_gather | solution.py:127
  7.9 162.5 %all-gather.16.cloned.1.call-start = ((), (), s32[]{:S(2)}) async-start(), calls=%async_computation.11 | async-start | bytes 8650752 | tf_op jit(solution)/shard_map/all_gather | solution.py:126
  8.7 241.0 %all-gather.14.cloned.1.call-start = ((), (), s32[]{:S(2)}) async-start(), calls=%async_computation.10 | async-start | bytes 8650752 | tf_op jit(solution)/shard_map/all_gather | solution.py:125
  9.4 328.9 %all-gather.12.cloned.1.call-start = ((), (), s32[]{:S(2)}) async-start(), calls=%async_computation.9 | async-start | bytes 10485760 | tf_op jit(solution)/shard_map/all_gather | solution.py:155
  59.6 190.1 %copy-start.37 = (f32[2048]{0:T(1024)}, f32[2048]{0:T(1024)S(1)}, u32[]{:S(2)}) copy-start(f32[2048]{0:T(1024)S(1)} %convert_element_type.147) | copy-start | bytes 24580
  59.6 190.1 %copy-start.24 = (f32[2048]{0:T(1024)}, f32[2048]{0:T(1024)S(1)}, u32[]{:S(2)}) copy-start(f32[2048]{0:T(1024)S(1)} %convert_element_type.146) | copy-start | bytes 24580
  100.5 327.7 %all-gather.18.cloned.1.call-start = ((), (), s32[]{:S(2)}) async-start(), calls=%async_computation.12 | async-start | bytes 10485760 | tf_op jit(solution)/shard_map/all_gather | solution.py:154
  179.7 336.0 %all-gather.20.cloned.1.call-start = ((), (), s32[]{:S(2)}) async-start(), calls=%async_computation.13 | async-start | bytes 8650752 | tf_op jit(solution)/shard_map/all_gather | solution.py:128
  180.2 524.7 %all-gather.22.cloned.1.call-start = ((), (), s32[]{:S(2)}) async-start(), calls=%async_computation.14 | async-start | bytes 34603008 | tf_op jit(solution)/shard_map/all_gather | solution.py:170
  181.0 719.8 %all-gather.24.cloned.1.call-start = ((), (), s32[]{:S(2)}) async-start(), calls=%async_computation.15 | async-start | bytes 34603008 | tf_op jit(solution)/shard_map/all_gather | solution.py:171
  181.7 1277.5 %reduce-scatter.9.cloned.1.call-start = ((), (), s32[]{:S(2)}) async-start(), calls=%async_computation.16 | async-start | bytes 10485760 | tf_op jit(solution)/shard_map/reduce_scatter | solution.py:243
  248.9 456.0 %copy-start.20 = (f32[2048]{0:T(1024)}, f32[2048]{0:T(1024)S(1)}, u32[]{:S(2)}) copy-start(f32[2048]{0:T(1024)S(1)} %convert_element_type.159) | copy-start | bytes 24580
  248.9 711.8 %copy-start.14 = (f32[2048]{0:T(1024)}, f32[2048]{0:T(1024)S(1)}, u32[]{:S(2)}) copy-start(f32[2048]{0:T(1024)S(1)} %convert_element_type.158) | copy-start | bytes 24580
  249.1 715.2 %copy-start.39 = (f32[2,256]{1,0:T(2,128)}, f32[2,256]{1,0:T(2,128)S(1)}, u32[]{:S(2)}) copy-start(f32[2,256]{1,0:T(2,128)S(1)} %compare_convert_fusion) | copy-start | bytes 6148
  524.4 436.3 %copy-start.16 = (f32[2,256]{1,0:T(2,128)}, f32[2,256]{1,0:T(2,128)S(1)}, u32[]{:S(2)}) copy-start(f32[2,256]{1,0:T(2,128)S(1)} %broadcast_multiply_fusion) | copy-start | bytes 6148
  526.9 433.8 %copy-start.18 = (f32[2,256]{1,0:T(2,128)}, f32[2,256]{1,0:T(2,128)S(1)}, u32[]{:S(2)}) copy-start(f32[2,256]{1,0:T(2,128)S(1)} %fusion.168) | copy-start | bytes 6148
  1374.5 174.3 %reduce-scatter.11.cloned.1.call-start = ((), (), s32[]{:S(2)}) async-start(), calls=%async_computation.17 | async-start | bytes 10485760 | tf_op jit(solution)/shard_map/reduce_scatter | solution.py:246
  1375.1 328.4 %all-reduce.21.cloned.1.call-start = ((), (), s32[]{:S(2)}) async-start(), calls=%async_computation.24 | async-start | bytes 196608
  1565.2 486.9 %reduce-scatter.13.cloned.1.call-start = ((), (), s32[]{:S(2)}) async-start(), calls=%async_computation.18 | async-start | bytes 17301504 | tf_op jit(solution)/shard_map/reduce_scatter | solution.py:289
  1575.8 838.3 %reduce-scatter.19.cloned.1.call-start = ((), (), s32[]{:S(2)}) async-start(), calls=%async_computation.21 | async-start | bytes 17301504 | tf_op jit(solution)/shard_map/reduce_scatter | solution.py:292
  1588.4 1187.7 %reduce-scatter.15.cloned.1.call-start = ((), (), s32[]{:S(2)}) async-start(), calls=%async_computation.19 | async-start | bytes 17301504 | tf_op jit(solution)/shard_map/reduce_scatter | solution.py:290
  1598.9 1539.1 %reduce-scatter.17.cloned.1.call-start = ((), (), s32[]{:S(2)}) async-start(), calls=%async_computation.20 | async-start | bytes 17301504 | tf_op jit(solution)/shard_map/reduce_scatter | solution.py:291
  1609.4 2937.4 %reduce-scatter.21.cloned.1.call-start = ((), (), s32[]{:S(2)}) async-start(), calls=%async_computation.22 | async-start | bytes 69206016 | tf_op jit(solution)/shard_map/reduce_scatter | solution.py:210
  1642.6 4311.7 %reduce-scatter.23.cloned.1.call-start = ((), (), s32[]{:S(2)}) async-start(), calls=%async_computation.23 | async-start | bytes 69206016 | tf_op jit(solution)/shard_map/reduce_scatter | solution.py:211
  (38 other events, 1512.5 us)
Sparse Core Ops, SparseCore 0:
  10.9 80.4 all-gather.9
  94.2 76.2 all-gather.15
  173.4 76.3 all-gather.13
  252.0 86.2 all-gather.11
  340.6 87.5 all-gather.17
  431.0 77.5 all-gather.19
  511.4 193.4 all-gather.21
  707.8 192.9 all-gather.23
  1374.6 84.5 reduce-scatter.8
  1462.4 86.3 reduce-scatter.10
  1565.4 125.2 all-reduce.20
  1693.5 358.5 reduce-scatter.12
  2055.1 359.0 reduce-scatter.18
  2417.0 359.0 reduce-scatter.14
  2778.9 359.0 reduce-scatter.16
  3140.9 1405.7 reduce-scatter.20
  4549.6 1404.5 reduce-scatter.22
where the time goes:
time: 5970 us; the launch traced here: 5960 us
  waiting for transfers between devices  4930 us (83%)
  matrix products  736 us (12%)
  blocking collectives  110 us (2%)
  local copies, waits for them, and re-layouts  84.5 us (1%)
  other arithmetic  79.1 us (1%)
    reduce_scatter x1, waiting for transfers between devices, body(): lax.psum_scatter(input_weight_gradient, ('batch', 'seq'), scatter_dimensi...  1410 us
    reduce_scatter x1, waiting for transfers between devices, body(): lax.psum_scatter(grad_w_out, ('batch', 'seq'), scatter_dimension=0, tiled...  1410 us
    reduce_scatter x1, waiting for transfers between devices, body(): lax.psum_scatter(output_weight_gradient, ('batch', 'seq'), scatter_dimens...  362 us
    reduce_scatter x1, waiting for transfers between devices, body(): lax.psum_scatter(value_weight_gradient, ('batch', 'seq'), scatter_dimensi...  362 us
    reduce_scatter x1, waiting for transfers between devices, body(): lax.psum_scatter(key_weight_gradient, ('batch', 'seq'), scatter_dimension...  362 us
    reduce_scatter x1, waiting for transfers between devices, body(): lax.psum_scatter(query_weight_gradient, ('batch', 'seq'), scatter_dimensi...  337 us
    all_gather x1, waiting for transfers between devices, body(): lax.all_gather(w_in, ('batch', 'seq'), axis=0, tiled=True)  178 us
    dot_general x4, matrix products, attend_back(): jnp.einsum('bhqk,bqhe->bkhe', grad_raw, query, preferred_element_type=jnp...  142 us
  transfers between devices with their start and end apart: 17, of which 15 were waited for; matrix products, arithmetic and copies ran while one was open for 7% of the time, Pallas kernels for 0%

commit v1 on v0

v1 whole, which is shorter than its diff:
```python
from functools import partial

import jax
import jax.numpy as jnp
import numpy as np
from jax import lax
from jax.experimental import pallas as pl
from jax.experimental.pallas import tpu as pltpu
from jax.sharding import PartitionSpec as P

HEAD_DIM = 64
PAIR = 2 * HEAD_DIM
epsilon = 1e-05
LOG2E = 1.4426950408889634
bf16, f32 = jnp.bfloat16, jnp.float32
ALL = ("batch", "seq")
VMEM_LIMIT = 56 * 1024 * 1024


def dot_nn(a, b):
    return jnp.dot(a, b, preferred_element_type=f32)


def dot_nt(a, b):
    return lax.dot_general(a, b, (((1,), (1,)), ((), ())), preferred_element_type=f32)


def dot_tn(a, b):
    return lax.dot_general(a, b, (((0,), (0,)), ((), ())), preferred_element_type=f32)


class Ring:
    def __init__(self, size):
        self.size = size
        self.order = [i ^ (i >> 1) for i in range(size)]
        self.place = [self.order.index(i) for i in range(size)]
        self.up = [(self.order[i], self.order[(i + 1) % size]) for i in range(size)]
        self.down = [(self.order[i], self.order[i - 1]) for i in range(size)]

    def mine(self):
        return jnp.array(self.place, jnp.int32)[lax.axis_index("seq")]

    def steps_to(self):
        return lax.rem(jnp.array(self.place, jnp.int32) - self.mine() + self.size, self.size)

    def gather(self, block):
        n, half = self.size, block.shape[0] // 2
        out = [None] * n
        out[0] = rising = falling = block
        for k in range(1, n // 2):
            rising = lax.ppermute(rising, "seq", self.up)
            falling = lax.ppermute(falling, "seq", self.down)
            out[n - k], out[k] = rising, falling
        first = lax.ppermute(rising[:half], "seq", self.up)
        last = lax.ppermute(falling[half:], "seq", self.down)
        out[n // 2] = jnp.concatenate([first, last])
        return jnp.concatenate(out)

    def scatter(self, total):
        n = self.size
        rows = total.shape[0] // n
        half = rows // 2
        part = [total[k * rows : (k + 1) * rows] for k in range(n)]
        rising = lax.ppermute(part[n // 2][:half], "seq", self.up)
        falling = lax.ppermute(part[n // 2][half:], "seq", self.down)
        if n == 2:
            return part[0].astype(f32) + jnp.concatenate([rising, falling]).astype(f32)
        for k in range(n // 2 - 1, 0, -1):
            up, down = part[k], part[n - k]
            if k == n // 2 - 1:
                up = jnp.concatenate([add16(up[:half], rising), up[half:]])
                down = jnp.concatenate([down[:half], add16(down[half:], falling)])
            else:
                up, down = add16(up, rising), add16(down, falling)
            rising = lax.ppermute(up, "seq", self.up)
            falling = lax.ppermute(down, "seq", self.down)
        return part[0].astype(f32) + rising.astype(f32) + falling.astype(f32)


def add16(a, b):
    return (a.astype(f32) + b.astype(f32)).astype(bf16)


def gather_small(block, devices):
    place = lax.axis_index(ALL)
    have, bit = block[None], 1
    while bit < devices:
        other = lax.ppermute(have, ALL, [(i, i ^ bit) for i in range(devices)])
        low = (place & bit) == 0
        have = jnp.concatenate([jnp.where(low, have, other), jnp.where(low, other, have)])
        bit *= 2
    return have


def scatter_small(total, devices):
    place = lax.axis_index(ALL)
    bit = devices // 2
    while bit >= 1:
        low = (place & bit) == 0
        keep = jnp.where(low, total[:bit], total[bit:])
        send = jnp.where(low, total[bit:], total[:bit])
        total = keep + lax.ppermute(send, ALL, [(i, i ^ bit) for i in range(devices)])
        bit //= 2
    return total[0]


def attend_kernel(blocks, rows, steps, q_ref, k_ref, v_ref, o_ref, lse_ref, keys, values_t):
    for a in range(blocks):
        here = pl.ds(pl.multiple_of(steps[a] * rows, rows), rows)
        keys[a * rows : (a + 1) * rows, :] = k_ref[here, :]
        values_t[:, a * rows : (a + 1) * rows] = v_ref[here, :].astype(f32).T.astype(bf16)
    lane = lax.broadcasted_iota(jnp.int32, (1, PAIR), 1)
    causal = lax.broadcasted_iota(jnp.int32, (rows, rows), 0) <= lax.broadcasted_iota(
        jnp.int32, (rows, rows), 1
    )
    scale = HEAD_DIM ** (-0.5) * LOG2E
    for i in range(blocks):
        here = pl.ds(pl.multiple_of(steps[i] * rows, rows), rows)
        query = q_ref[here, :]
        ahead = i * rows
        parts = []
        for head in range(2):
            own = (lane // HEAD_DIM == head).astype(bf16)
            lines = slice(head * HEAD_DIM, (head + 1) * HEAD_DIM)
            q_head = query * own
            diag = dot_nt(keys[ahead : ahead + rows, :], q_head) * scale
            diag = jnp.where(causal, diag, -1e30)
            top = jnp.max(diag, 0, keepdims=True)
            if i > 0:
                full = dot_nt(keys[:ahead, :], q_head) * scale
                top = jnp.maximum(top, jnp.max(full, 0, keepdims=True))
            diag = jnp.exp2(diag - top)
            total = jnp.sum(diag, 0, keepdims=True)
            mixed = dot_nn(values_t[lines, ahead : ahead + rows], diag.astype(bf16))
            if i > 0:
                full = jnp.exp2(full - top)
                total = total + jnp.sum(full, 0, keepdims=True)
                mixed = mixed + dot_nn(values_t[lines, :ahead], full.astype(bf16))
            parts.append(mixed / total)
            lse_ref[0, head : head + 1, ahead : ahead + rows] = top + jnp.log2(total)
        o_ref[here, :] = jnp.concatenate(parts).T.astype(bf16)


def attend(qkv, steps, blocks):
    tokens, width = qkv.shape[0], qkv.shape[1] // 3
    pairs, rows = width // PAIR, tokens // blocks
    column = lambda c: pl.BlockSpec((tokens, PAIR), lambda h, steps: (0, c * pairs + h))
    return pl.pallas_call(
        partial(attend_kernel, blocks, rows),
        out_shape=(
            jax.ShapeDtypeStruct((tokens, width), bf16),
            jax.ShapeDtypeStruct((pairs, 2, tokens), f32),
        ),
        grid_spec=pltpu.PrefetchScalarGridSpec(
            num_scalar_prefetch=1,
            grid=(pairs,),
            in_specs=[column(0), column(1), column(2)],
            out_specs=(column(0), pl.BlockSpec((1, 2, tokens), lambda h, steps: (h, 0, 0))),
            scratch_shapes=[pltpu.VMEM((tokens, PAIR), bf16), pltpu.VMEM((PAIR, tokens), bf16)],
        ),
        compiler_params=pltpu.CompilerParams(vmem_limit_bytes=VMEM_LIMIT),
        cost_estimate=pl.CostEstimate(
            flops=4 * tokens * tokens * width, bytes_accessed=8 * tokens * width,
            transcendentals=tokens * tokens * pairs,
        ),
        name="attend",
    )(steps, qkv, qkv, qkv)


def attend_back_kernel(
    blocks, rows, steps, q_ref, k_ref, v_ref, g_ref, lse_ref, d_ref, keys, keys_t, values, dk, dv, dk16, dv16
):
    @pl.when(pl.program_id(1) == 0)
    def _():
        for a in range(blocks):
            here = pl.ds(pl.multiple_of(steps[a] * rows, rows), rows)
            place = slice(a * rows, (a + 1) * rows)
            keys[place, :] = k_ref[here, :]
            keys_t[:, place] = k_ref[here, :].astype(f32).T.astype(bf16)
            values[place, :] = v_ref[here, :]
        dk[...] = jnp.zeros_like(dk)
        dv[...] = jnp.zeros_like(dv)
        lane = lax.broadcasted_iota(jnp.int32, (1, PAIR), 1)
        scaling = HEAD_DIM ** (-0.5)
        for i in range(blocks):
            here = pl.ds(pl.multiple_of(steps[i] * rows, rows), rows)
            query, grad = q_ref[here, :], g_ref[here, :]
            length = (i + 1) * rows
            causal = lax.broadcasted_iota(jnp.int32, (length, rows), 0) <= (
                lax.broadcasted_iota(jnp.int32, (length, rows), 1) + i * rows
            )
            parts = []
            for head in range(2):
                own = (lane // HEAD_DIM == head).astype(bf16)
                lines = slice(head * HEAD_DIM, (head + 1) * HEAD_DIM)
                q_head, g_head = query * own, grad * own
                lse = lse_ref[0, head : head + 1, i * rows : (i + 1) * rows]
                logits = dot_nt(keys[:length, :], q_head) * (scaling * LOG2E)
                probs = jnp.where(causal, jnp.exp2(logits - lse), 0.0)
                grad_probs = dot_nt(values[:length, :], g_head)
                inner = jnp.sum(grad_probs * probs, 0, keepdims=True)
                grad_raw = (probs * (grad_probs - inner) * scaling).astype(bf16)
                parts.append(dot_nn(keys_t[lines, :length], grad_raw))
                dk[:length, :] += dot_nn(grad_raw, q_head)
                dv[:length, :] += dot_nn(probs.astype(bf16), g_head)
            d_ref[here, :] = jnp.concatenate(parts).T.astype(bf16)
        for a in range(blocks):
            here = pl.ds(pl.multiple_of(steps[a] * rows, rows), rows)
            dk16[here, :] = dk[a * rows : (a + 1) * rows, :].astype(bf16)
            dv16[here, :] = dv[a * rows : (a + 1) * rows, :].astype(bf16)

    @pl.when(pl.program_id(1) == 1)
    def _():
        d_ref[...] = dk16[...]

    @pl.when(pl.program_id(1) == 2)
    def _():
        d_ref[...] = dv16[...]


def attend_back(qkv, grad_context, lse, steps, blocks):
    tokens, width = grad_context.shape
    pairs, rows = width // PAIR, tokens // blocks
    column = lambda c: pl.BlockSpec((tokens, PAIR), lambda h, c_out, steps: (0, c * pairs + h))
    wide = lambda dtype: pltpu.VMEM((tokens, PAIR), dtype)
    return pl.pallas_call(
        partial(attend_back_kernel, blocks, rows),
        out_shape=jax.ShapeDtypeStruct((tokens, 3 * width), bf16),
        grid_spec=pltpu.PrefetchScalarGridSpec(
            num_scalar_prefetch=1,
            grid=(pairs, 3),
            in_specs=[
                column(0), column(1), column(2), column(0),
                pl.BlockSpec((1, 2, tokens), lambda h, c_out, steps: (h, 0, 0)),
            ],
            out_specs=pl.BlockSpec((tokens, PAIR), lambda h, c_out, steps: (0, c_out * pairs + h)),
            scratch_shapes=[
                wide(bf16), pltpu.VMEM((PAIR, tokens), bf16), wide(bf16),
                wide(f32), wide(f32), wide(bf16), wide(bf16),
            ],
        ),
        compiler_params=pltpu.CompilerParams(vmem_limit_bytes=VMEM_LIMIT),
        cost_estimate=pl.CostEstimate(
            flops=10 * tokens * tokens * width, bytes_accessed=14 * tokens * width,
            transcendentals=tokens * tokens * pairs,
        ),
        name="attend_back",
    )(steps, qkv, qkv, qkv, grad_context, lse)


def norm_parts(rows):
    centered = rows - jnp.mean(rows, -1, keepdims=True)
    spread = jnp.mean(centered * centered, -1, keepdims=True)
    inverse = lax.rsqrt(spread + epsilon)
    return centered * inverse, inverse


def norm_back(grad, gain, unit, inverse):
    scaled = grad * gain
    return inverse * (
        scaled - jnp.mean(scaled, -1, keepdims=True) - unit * jnp.mean(scaled * unit, -1, keepdims=True)
    )


def gelu_both(pre):
    below = 0.5 * (1.0 + lax.erf(pre * (0.5**0.5)))
    density = jnp.exp(-0.5 * pre * pre) * ((2.0 * np.pi) ** -0.5)
    return pre * below, below + pre * density


def body(
    inputs, cotangent, max_exit, min_exit, layer, wq, wk, wv, wo, gain_one, shift_one, bias_q, bias_v,
    bias_o, w_in, w_out, gain_two, shift_two, bias_in, bias_out,
):
    B, S = lax.axis_size("batch"), lax.axis_size("seq")
    devices = B * S
    s = lax.axis_index("seq")
    slots, T, D = inputs.shape
    r, rw = wq.shape[0], w_out.shape[0]
    Dl, Fl = D // S, rw * B
    whole_heads = r % HEAD_DIM == 0
    ring = Ring(S)
    steps = ring.steps_to()

    places = s * T + jnp.arange(T, dtype=jnp.int32)
    exits = max_exit[:, None] - (max_exit - min_exit)[:, None] * places[None, :] // (S * T - 1)
    active = (layer[0] < exits).astype(f32)[..., None]

    small = (gain_one, shift_one, bias_q, bias_v, bias_o, gain_two, shift_two, bias_out)
    packed = gather_small(jnp.concatenate(small + (bias_in,)), devices)
    full = lambda k: packed[:, k * r : (k + 1) * r].reshape(D).astype(f32)
    mine = lambda k: (
        lax.dynamic_index_in_dim(packed.reshape(B, S, -1), s, 1, False)[:, k * r : (k + 1) * r]
        if whole_heads
        else lax.dynamic_slice(packed[:, k * r : (k + 1) * r].reshape(D), (s * Dl,), (Dl,))
    ).reshape(Dl).astype(f32)
    gain_a, shift_a, bias_o_full, gain_b, shift_b, bias_out_full = (full(k) for k in (0, 1, 4, 5, 6, 7))
    bias_qkv = jnp.concatenate([mine(2), jnp.zeros((Dl,), f32), mine(3)])
    bias_hidden = (
        lax.dynamic_index_in_dim(packed.reshape(B, S, -1), s, 1, False)[:, len(small) * r :]
        .reshape(Fl).astype(f32)
    )

    def heads_out(w):
        if whole_heads:
            return w.reshape(r, B, S, r).transpose(2, 0, 1, 3).reshape(S, r, Dl)
        return w.reshape(r, S, Dl).transpose(1, 0, 2)

    def heads_back(w):
        if whole_heads:
            return w.reshape(S, r, B, r).transpose(1, 2, 0, 3).reshape(r, D)
        return w.transpose(1, 0, 2).reshape(r, D)

    swap = lambda x: lax.all_to_all(x, "seq", split_axis=0, concat_axis=0, tiled=True)
    gather = lambda x: lax.all_gather(x, "batch", axis=0, tiled=True)
    scatter = lambda x: lax.psum_scatter(x, "batch", scatter_dimension=0, tiled=True)
    qkv_pieces = jnp.concatenate([heads_out(w) for w in (wq, wk, wv)], -1)
    w_qkv = gather(swap(qkv_pieces).reshape(S * r, 3 * Dl))
    if whole_heads:
        w_o = gather(wo)
    else:
        w_o = lax.dynamic_slice(lax.all_gather(wo, ALL, axis=0, tiled=True), (s * Dl, 0), (Dl, D))
    in_pieces = w_in.reshape(r, B, S, rw).transpose(2, 0, 1, 3).reshape(S, r, Fl)
    w_1 = gather(swap(in_pieces).reshape(S * r, Fl))
    w_2 = gather(w_out)

    start = inputs.astype(f32)
    grad_out = cotangent.astype(f32)
    grad_two = (active * grad_out).astype(bf16)

    normed, qkv, context, lse, middle, normed_two = [], [], [], [], [], []
    for i in range(slots):
        rows = ring.gather(inputs[i]).astype(f32)
        unit, _ = norm_parts(rows)
        normed.append((unit * gain_a + shift_a).astype(bf16))
        qkv.append((dot_nn(normed[i], w_qkv) + bias_qkv).astype(bf16))
        mixed, log_total = attend(qkv[i], steps, S)
        context.append(mixed)
        lse.append(log_total)
        branch = ring.scatter(dot_nn(mixed, w_o).astype(bf16)) + bias_o_full
        middle.append(start[i] + active[i] * branch)
    unit_two, inverse_two = [], []
    for i in range(slots):
        unit, inverse = norm_parts(middle[i])
        unit_two.append(unit)
        inverse_two.append(inverse)
        normed_two.append(ring.gather((unit * gain_b + shift_b).astype(bf16)))
    grad_branch_two = [ring.gather(grad_two[i]) for i in range(slots)]

    hidden, grad_pre, output, grad_middle, grad_branch = [], [], [], [], []
    sum_gain_two = sum_shift_two = 0.0
    own_grad_branch = []
    for i in range(slots):
        value, slope = gelu_both(dot_nn(normed_two[i], w_1) + bias_hidden)
        hidden.append(value.astype(bf16))
        grad_pre.append((dot_nt(grad_branch_two[i], w_2) * slope).astype(bf16))
        back = ring.scatter(dot_nt(grad_pre[i], w_1).astype(bf16))
        sum_gain_two += jnp.sum(back * unit_two[i], 0)
        sum_shift_two += jnp.sum(back, 0)
        grad_middle.append(grad_out[i] + norm_back(back, gain_b, unit_two[i], inverse_two[i]))
        own_grad_branch.append((active[i] * grad_middle[i]).astype(bf16))
        grad_branch.append(ring.gather(own_grad_branch[i]))
        branch_two = ring.scatter(dot_nn(hidden[i], w_2).astype(bf16)) + bias_out_full
        output.append((middle[i] + active[i] * branch_two).astype(bf16))

    both = lambda left, right: sum(dot_tn(a, b) for a, b in zip(left, right))
    sum_w_1 = scatter(both(normed_two, grad_pre).astype(bf16))
    sum_w_1 = swap(sum_w_1.reshape(S, r, Fl)).reshape(S, r, B, rw).transpose(1, 2, 0, 3).reshape(r, -1)
    sum_w_2 = scatter(both(hidden, grad_branch_two).astype(bf16))

    grad_qkv, input_grad = [], []
    sum_gain_one = sum_shift_one = 0.0
    for i in range(slots):
        grad_context = dot_nt(grad_branch[i], w_o).astype(bf16)
        grad_qkv.append(attend_back(qkv[i], grad_context, lse[i], steps, S))
        back = ring.scatter(dot_nt(grad_qkv[i], w_qkv).astype(bf16))
        unit, inverse = norm_parts(start[i])
        sum_gain_one += jnp.sum(back * unit, 0)
        sum_shift_one += jnp.sum(back, 0)
        input_grad.append((grad_middle[i] + norm_back(back, gain_a, unit, inverse)).astype(bf16))

    sum_o = both(context, grad_branch)
    if whole_heads:
        sum_o = scatter(sum_o.astype(bf16))
    else:
        sum_o = lax.dynamic_update_slice(jnp.zeros((D, D), f32), sum_o, (s * Dl, 0))
        sum_o = lax.psum_scatter(sum_o.astype(bf16), ALL, scatter_dimension=0, tiled=True)
    sum_qkv = scatter(both(normed, grad_qkv).astype(bf16))
    sum_qkv = swap(sum_qkv.reshape(S, r, 3 * Dl))
    sum_q, sum_k, sum_v = (heads_back(sum_qkv[:, :, c * Dl : (c + 1) * Dl]) for c in range(3))

    tokens = lambda parts: sum(jnp.sum(p.astype(f32), 0) for p in parts)
    bias_sums = tokens(grad_qkv)
    plain = lambda v: v.reshape(devices, r)

    def own_heads(v):
        if whole_heads:
            spread = jnp.zeros((B, S, r), f32)
            return lax.dynamic_update_slice(spread, v.reshape(B, 1, r), (0, s, 0)).reshape(devices, r)
        return lax.dynamic_update_slice(jnp.zeros((D,), f32), v, (s * Dl,)).reshape(devices, r)

    own_hidden = lax.dynamic_update_slice(
        jnp.zeros((B, S, rw), f32), tokens(grad_pre).reshape(B, 1, rw), (0, s, 0)
    ).reshape(devices, rw)
    sums = scatter_small(
        jnp.concatenate(
            [
                plain(sum_gain_one), plain(sum_shift_one), own_heads(bias_sums[:Dl]),
                own_heads(bias_sums[2 * Dl :]), plain(tokens(own_grad_branch)), plain(sum_gain_two),
                plain(sum_shift_two), plain(tokens([grad_two[i] for i in range(slots)])), own_hidden,
            ],
            -1,
        ),
        devices,
    )
    g1, s1, bq, bv, bo, g2, s2, b2 = (sums[k * r : (k + 1) * r] for k in range(8))
    wide = lambda v: v.astype(f32)
    return (
        jnp.stack(output), jnp.stack(input_grad), wide(sum_q), wide(sum_k), wide(sum_v), wide(sum_o),
        g1, s1, bq, bv, bo, wide(sum_w_1), wide(sum_w_2), g2, s2, sums[8 * r :], b2,
    )


def solution(mesh):
    tokens, rows, vector = P("batch", "seq", None), P(ALL, None), P(ALL)
    placed = (
        (tokens, tokens, P("batch"), P("batch"), P())
        + (rows,) * 4 + (vector,) * 5 + (rows,) * 2 + (vector,) * 4
    )
    out = (tokens, tokens) + (rows,) * 4 + (vector,) * 5 + (rows,) * 2 + (vector,) * 4
    return jax.shard_map(body, mesh=mesh, in_specs=placed, out_specs=out, check_vma=False)
```

time: 5970 us -> 1140 us (0.19)
  waiting for transfers between devices: 4930 us -> 481 us
  matrix products: 736 us -> 261 us
  Pallas kernels: 0 us -> 97.1 us
  starting transfers between devices: 0.68 us -> 82.8 us
  blocking collectives: 110 us -> 33.8 us
    reduce_scatter x8 -> x4, waiting for transfers between devices: 4390 us -> 80.4 us  [body(): lax.psum_scatter(x, 'batch', scatter_dimension=0, tiled=True)]
    all_gather x8 -> x4, waiting for transfers between devices: 540 us -> 0.01 us  [body(): gather = lambda x: lax.all_gather(x, 'batch', axis=0, tiled=True)]
    dot_general x46 -> x24, matrix products: 736 us -> 261 us  [the longest x8 95.5 us: dot_tn(): lax.dot_general(a, b, (((0,), (0,)), ((), ())), preferred_element_type=f32)]
    ppermute x0 -> x74, waiting for transfers between devices: none -> 394 us  [the longest x8 147 us: scatter(): falling = lax.ppermute(down, 'seq', self.down)]
    pallas_call x0 -> x4, Pallas kernels: none -> 97.1 us  [the longest x2 64.2 us: attend_back(): pl.pallas_call(partial(attend_back_kernel, blocks, rows), out_shape=jax.S...]
    ppermute x0 -> x74, starting transfers between devices: none -> 74.4 us  [the longest x8 9.58 us: gather(): rising = lax.ppermute(rising, 'seq', self.up)]
    all_gather x1 -> x0, blocking collectives: 66.3 us -> none  [body(): lax.all_gather(bias_in, ('batch', 'seq'), axis=0, tiled=True)]
  transfers between devices with their start and end apart: 17 -> 84, of which waited for: 15 -> 37; matrix products, arithmetic and copies ran while one was open for 7% -> 31% of each run, Pallas kernels for 0% -> 6%
where the time goes in v1:
time: 1140 us; the launch traced here: 1130 us
  waiting for transfers between devices  481 us (42%)
  matrix products  261 us (23%)
  Pallas kernels  97.1 us (9%)
  local copies, waits for them, and re-layouts  86 us (8%)
  starting transfers between devices  82.8 us (7%)
  other arithmetic  75.6 us (7%)
  blocking collectives  33.8 us (3%)
  between operations  17.3 us (2%)
    ppermute x8, waiting for transfers between devices, scatter(): falling = lax.ppermute(down, 'seq', self.down)  147 us
    dot_general x8, matrix products, dot_tn(): lax.dot_general(a, b, (((0,), (0,)), ((), ())), preferred_element_type=f32)  95.5 us
    dot_general x8, matrix products, dot_nt(): lax.dot_general(a, b, (((1,), (1,)), ((), ())), preferred_element_type=f32)  83.3 us
    dot_general x8, matrix products, dot_nn(): return jnp.dot(a, b, preferred_element_type=f32)  82.3 us
    reduce_scatter x4, waiting for transfers between devices, body(): lax.psum_scatter(x, 'batch', scatter_dimension=0, tiled=True)  80.4 us
    pallas_call x2, Pallas kernels, attend_back(): pl.pallas_call(partial(attend_back_kernel, blocks, rows), out_shape=jax.S...  64.2 us
    ppermute x8, waiting for transfers between devices, gather(): rising = lax.ppermute(rising, 'seq', self.up)  57.7 us
    ppermute x8, waiting for transfers between devices, gather(): last = lax.ppermute(falling[half:], 'seq', self.down)  40.5 us
  transfers between devices with their start and end apart: 84, of which 37 were waited for; matrix products, arithmetic and copies ran while one was open for 31% of the time, Pallas kernels for 6%

profile of v1, /device:TPU:0, one launch (start us, length us, event | category | flops | bytes accessed | tf_op | source)
XLA Modules:
  0.0 1134.7 jit_solution(7419800838303343633)
XLA Ops:
  12.0 16.4 %all_to_all.20 = bf16[4,64,1536]{2,1,0:T(8,128)(2,1)} all-to-all(bf16[4,64,1536]{2,1,0:T(8,128)(2,1)S(1)} %pad_maximum_fusion.18), channel_id=1, replica_groups=mesh['batch'=8,'seq'=4] {'seq'}, dimensions={0} | all-to-all | bytes 1572864 | tf_op jit(solution)/shard_map/all_to_all | solution.py:314
  33.8 17.4 %all_to_all.21 = bf16[4,64,2048]{2,1,0:T(8,128)(2,1)} all-to-all(bf16[4,64,2048]{2,1,0:T(8,128)(2,1)} %reshape.424), channel_id=1, replica_groups=mesh['batch'=8,'seq'=4] {'seq'}, dimensions={0} | all-to-all | bytes 2097152 | tf_op jit(solution)/shard_map/all_to_all | solution.py:314
  62.5 35.1 %collective-permute-done.4 = bf16[1,768]{1,0:T(2,128)(2,1)S(1)} collective-permute-done((bf16[1,768]{1,0:T(2,128)(2,1)S(1)}, bf16[1,768]{1,0:T(2,128)(2,1)S(1)}, u32[]{:S(2)}, u32[]{:S(2)}) %collective-permute-start.4) | collective-permute-done | bytes 1568 | tf_op jit(solution)/shard_map/ppermute | solution.py:88
  138.4 15.2 %collective-permute-done.3 = bf16[128,2048]{1,0:T(8,128)(2,1)S(1)} collective-permute-done((bf16[128,2048]{1,0:T(8,128)(2,1)S(1)}, bf16[128,2048]{1,0:T(8,128)(2,1)S(1)}, u32[]{:S(2)}, u32[]{:S(2)}) %collective-permute-start.3) | collective-permute-done | bytes 524320 | tf_op jit(solution)/shard_map/ppermute | solution.py:55
  163.4 27.5 %collective-permute-done.23 = bf16[128,2048]{1,0:T(8,128)(2,1)S(1)} collective-permute-done((bf16[128,2048]{1,0:T(8,128)(2,1)S(1)}, bf16[128,2048]{1,0:T(8,128)(2,1)S(1)}, u32[]{:S(2)}, u32[]{:S(2)}) %collective-permute-start.23) | collective-permute-done | bytes 524320 | tf_op jit(solution)/shard_map/ppermute | solution.py:54
  206.2 16.4 %attend.2 = (bf16[1024,512]{1,0:T(8,128)(2,1)}, f32[4,2,1024]{2,1,0:T(2,128)}) custom-call(s32[4]{0:T(128)} %compare_select_fusion.steps, bf16[1024,1536]{1,0:T(8,128)(2,1)} %add_convert_fusion.4.q_ref.k_ref.v_ref, bf16[1024,1536]{1,0:T(8,128)(2,1)} %add_convert_fusion.4.q_ref.k_ref.v_ref, bf16[1024,1536]{1,0:T(8,128)(2,1)} %add_convert_fusion.4.q_ref.k_ref.v_ref), custom_call_target="tpu_custom_call" | custom-call | flops 2147483648 | bytes 4194304 | tf_op jit(solution)/shard_map/attend/pallas_call | solution.py:148
  242.5 16.5 %attend.3 = (bf16[1024,512]{1,0:T(8,128)(2,1)}, f32[4,2,1024]{2,1,0:T(2,128)}) custom-call(s32[4]{0:T(128)} %compare_select_fusion.steps, bf16[1024,1536]{1,0:T(8,128)(2,1)} %add_convert_fusion.3.q_ref.k_ref.v_ref, bf16[1024,1536]{1,0:T(8,128)(2,1)} %add_convert_fusion.3.q_ref.k_ref.v_ref, bf16[1024,1536]{1,0:T(8,128)(2,1)} %add_convert_fusion.3.q_ref.k_ref.v_ref), custom_call_target="tpu_custom_call" | custom-call | flops 2147483648 | bytes 4194304 | tf_op jit(solution)/shard_map/attend/pallas_call | solution.py:148
  287.3 15.5 %collective-permute-done.53 = bf16[256,2048]{1,0:T(8,128)(2,1)} collective-permute-done((bf16[256,2048]{1,0:T(8,128)(2,1)}, bf16[256,2048]{1,0:T(8,128)(2,1)}, u32[]{:S(2)}, u32[]{:S(2)}) %collective-permute-start.53) | collective-permute-done | bytes 1048608 | tf_op jit(solution)/shard_map/ppermute | solution.py:52
  307.6 17.7 %collective-permute-done.12 = bf16[256,2048]{1,0:T(8,128)(2,1)} collective-permute-done((bf16[256,2048]{1,0:T(8,128)(2,1)}, bf16[256,2048]{1,0:T(8,128)(2,1)}, u32[]{:S(2)}, u32[]{:S(2)}) %collective-permute-start.12) | collective-permute-done | bytes 1048608 | tf_op jit(solution)/shard_map/ppermute | solution.py:76
  327.3 20.4 %collective-permute-done.28 = bf16[256,2048]{1,0:T(8,128)(2,1)} collective-permute-done((bf16[256,2048]{1,0:T(8,128)(2,1)}, bf16[256,2048]{1,0:T(8,128)(2,1)}, u32[]{:S(2)}, u32[]{:S(2)}) %collective-permute-start.28) | collective-permute-done | bytes 1048608 | tf_op jit(solution)/shard_map/ppermute | solution.py:76
  469.9 17.0 %convert_reduce_fusion.3 = (f32[2048]{0:T(1024)}, bf16[1024,2048]{1,0:T(8,128)(2,1)S(1)}) fusion(f32[1024,2048]{1,0:T(8,128)} %get-tuple-element.163, f32[2048]{0:T(1024)S(1)} %bitcast.210, bf16[1024,2048]{1,0:T(8,128)(2,1)} %constant_dynamic-update-slice_fusion.20, bf16[2048,2048]{1,0:T(8,128)(2,1)} %all-gather.11.cloned.1.call-done), kind=kOutput, calls=%fused_computation.34 | convolution fusion | flops 8617195520 | bytes 25182208 | tf_op jit(solution)/shard_map/dot_general | solution.py:25
  500.7 17.0 %convert_reduce_fusion.2 = (f32[2048]{0:T(1024)}, bf16[1024,2048]{1,0:T(8,128)(2,1)}) fusion(f32[1024,2048]{1,0:T(8,128)} %copy-done.96, f32[2048]{0:T(1024)S(1)} %bitcast.211, bf16[1024,2048]{1,0:T(8,128)(2,1)S(1)} %copy-done.38, bf16[2048,2048]{1,0:T(8,128)(2,1)} %all-gather.11.cloned.1.call-done), kind=kOutput, calls=%fused_computation.33 | convolution fusion | flops 8617195520 | bytes 25182208 | tf_op jit(solution)/shard_map/dot_general | solution.py:25
  585.3 21.2 %collective-permute-done.44 = bf16[256,2048]{1,0:T(8,128)(2,1)S(1)} collective-permute-done((bf16[256,2048]{1,0:T(8,128)(2,1)S(1)}, bf16[256,2048]{1,0:T(8,128)(2,1)S(1)}, u32[]{:S(2)}, u32[]{:S(2)}) %collective-permute-start.44) | collective-permute-done | bytes 1048608 | tf_op jit(solution)/shard_map/ppermute | solution.py:76
  608.5 20.4 %collective-permute-done.60 = bf16[256,2048]{1,0:T(8,128)(2,1)S(1)} collective-permute-done((bf16[256,2048]{1,0:T(8,128)(2,1)S(1)}, bf16[256,2048]{1,0:T(8,128)(2,1)S(1)}, u32[]{:S(2)}, u32[]{:S(2)}) %collective-permute-start.60) | collective-permute-done | bytes 1048608 | tf_op jit(solution)/shard_map/ppermute | solution.py:76
  633.0 36.8 %collective-permute-done.20 = bf16[256,2048]{1,0:T(8,128)(2,1)S(1)} collective-permute-done((bf16[256,2048]{1,0:T(8,128)(2,1)S(1)}, bf16[256,2048]{1,0:T(8,128)(2,1)S(1)}, u32[]{:S(2)}, u32[]{:S(2)}) %collective-permute-start.20) | collective-permute-done | bytes 1048608 | tf_op jit(solution)/shard_map/ppermute | solution.py:76
  681.8 19.0 %collective-permute-done.46 = bf16[256,2048]{1,0:T(8,128)(2,1)S(1)} collective-permute-done((bf16[256,2048]{1,0:T(8,128)(2,1)S(1)}, bf16[256,2048]{1,0:T(8,128)(2,1)S(1)}, u32[]{:S(2)}, u32[]{:S(2)}) %collective-permute-start.46) | collective-permute-done | bytes 1048608 | tf_op jit(solution)/shard_map/ppermute | solution.py:51
  704.1 19.2 %collective-permute-done.62 = bf16[256,2048]{1,0:T(8,128)(2,1)S(1)} collective-permute-done((bf16[256,2048]{1,0:T(8,128)(2,1)S(1)}, bf16[256,2048]{1,0:T(8,128)(2,1)S(1)}, u32[]{:S(2)}, u32[]{:S(2)}) %collective-permute-start.62) | collective-permute-done | bytes 1048608 | tf_op jit(solution)/shard_map/ppermute | solution.py:51
  738.2 32.1 %attend_back.2 = bf16[1024,1536]{1,0:T(8,128)(2,1)} custom-call(s32[4]{0:T(128)} %compare_select_fusion.steps, bf16[1024,1536]{1,0:T(8,128)(2,1)} %add_convert_fusion.4.q_ref.k_ref.v_ref, bf16[1024,1536]{1,0:T(8,128)(2,1)} %add_convert_fusion.4.q_ref.k_ref.v_ref, bf16[1024,1536]{1,0:T(8,128)(2,1)} %add_convert_fusion.4.q_ref.k_ref.v_ref, ...), custom_call_target="tpu_custom_call" | custom-call | flops 5368709120 | bytes 7340032 | tf_op jit(solution)/shard_map/attend_back/pallas_call | solution.py:226
  790.8 32.2 %attend_back.3 = bf16[1024,1536]{1,0:T(8,128)(2,1)} custom-call(s32[4]{0:T(128)} %compare_select_fusion.steps, bf16[1024,1536]{1,0:T(8,128)(2,1)} %add_convert_fusion.3.q_ref.k_ref.v_ref, bf16[1024,1536]{1,0:T(8,128)(2,1)} %add_convert_fusion.3.q_ref.k_ref.v_ref, bf16[1024,1536]{1,0:T(8,128)(2,1)} %add_convert_fusion.3.q_ref.k_ref.v_ref, ...), custom_call_target="tpu_custom_call" | custom-call | flops 5368709120 | bytes 7340032 | tf_op jit(solution)/shard_map/attend_back/pallas_call | solution.py:226
  836.2 15.6 %fusion.72 = f32[2048,2048]{1,0:T(8,128)} fusion(bf16[1024,2048]{1,0:T(8,128)(2,1)} %copy-done.40, bf16[1024,2048]{1,0:T(8,128)(2,1)} %get-tuple-element.167), kind=kOutput, calls=%fused_computation.308 | convolution fusion | flops 8589934592 | bytes 25165824 | tf_op jit(solution)/shard_map/dot_general | solution.py:29
  851.8 16.0 %add_convert_fusion.1 = bf16[2048,2048]{1,0:T(8,128)(2,1)} fusion(f32[2048,2048]{1,0:T(8,128)} %fusion.72, bf16[1024,2048]{1,0:T(8,128)(2,1)} %constant_dynamic-update-slice_fusion.5, bf16[1024,2048]{1,0:T(8,128)(2,1)S(1)} %copy-done.101), kind=kOutput, calls=%fused_computation.1 | convolution fusion | flops 8598323200 | bytes 33554432 | tf_op jit(solution)/shard_map/dot_general | solution.py:29
  877.8 15.5 %fusion.73 = f32[2048,2048]{1,0:T(8,128)} fusion(bf16[1024,2048]{1,0:T(8,128)(2,1)} %get-tuple-element.148, bf16[1024,2048]{1,0:T(8,128)(2,1)} %constant_dynamic-update-slice_fusion.30), kind=kOutput, calls=%fused_computation.309 | convolution fusion | flops 8589934592 | bytes 25165824 | tf_op jit(solution)/shard_map/dot_general | solution.py:29
  954.4 18.1 %collective-permute-done.52 = bf16[256,2048]{1,0:T(8,128)(2,1)S(1)} collective-permute-done((bf16[256,2048]{1,0:T(8,128)(2,1)}, bf16[256,2048]{1,0:T(8,128)(2,1)S(1)}, u32[]{:S(2)}, u32[]{:S(2)}) %collective-permute-start.52) | collective-permute-done | bytes 1048608 | tf_op jit(solution)/shard_map/ppermute | solution.py:76
  1044.2 77.0 %reduce-scatter.11.cloned.1.call-done = bf16[256,2048]{1,0:T(8,128)(2,1)} async-done(((bf16[2048,2048]{1,0:T(8,128)(2,1)}), bf16[256,2048]{1,0:T(8,128)(2,1)}) %reduce-scatter.11.cloned.1.call-update) | async-done | bytes 1048592 | tf_op jit(solution)/shard_map/reduce_scatter | solution.py:316
  (614 shorter events, 562.3 us)
Async XLA Ops:
  7.2 187.1 %all-gather.5.cloned.1.call-start = ((), (), s32[]{:S(2)}) async-start(), calls=%async_computation.8 | async-start | bytes 7077888 | tf_op jit(solution)/shard_map/all_gather | solution.py:315
  28.5 194.1 %all-gather.7.cloned.1.call-start = ((), (), s32[]{:S(2)}) async-start(), calls=%async_computation.9 | async-start | bytes 2359296 | tf_op jit(solution)/shard_map/all_gather | solution.py:315
  29.2 409.6 %all-gather.9.cloned.1.call-start = ((), (), s32[]{:S(2)}) async-start(), calls=%async_computation.10 | async-start | bytes 9437184 | tf_op jit(solution)/shard_map/all_gather | solution.py:315
  51.2 418.8 %all-gather.11.cloned.1.call-start = ((), (), s32[]{:S(2)}) async-start(), calls=%async_computation.11 | async-start | bytes 9437184 | tf_op jit(solution)/shard_map/all_gather | solution.py:315
  52.7 68.8 %collective-permute-start = (bf16[256,2048]{1,0:T(8,128)(2,1)}, bf16[256,2048]{1,0:T(8,128)(2,1)}, u32[]{:S(2)}, u32[]{:S(2)}) collective-permute-start(bf16[256,2048]{1,0:T(8,128)(2,1)} %get-tuple-element.118), channel_id=1, source_target_pairs={{0,2},{1,0},{3,1},{2,3},{4,6},{5,4},{7,5},{6,7},{8,10},{9,8},{11,9... | collective-permute-start | bytes 3145736 | tf_op jit(solution)/shard_map/ppermute | solution.py:52
  53.6 65.3 %collective-permute-start.1 = (bf16[256,2048]{1,0:T(8,128)(2,1)}, bf16[256,2048]{1,0:T(8,128)(2,1)}, u32[]{:S(2)}, u32[]{:S(2)}) collective-permute-start(bf16[256,2048]{1,0:T(8,128)(2,1)} %get-tuple-element.118), channel_id=1, source_target_pairs={{0,1},{1,3},{3,2},{2,0},{4,5},{5,7},{7,6},{6,4},{8,9},{9,11},{11,1... | collective-permute-start | bytes 3145736 | tf_op jit(solution)/shard_map/ppermute | solution.py:51
  54.7 73.6 %collective-permute-start.21 = (bf16[256,2048]{1,0:T(8,128)(2,1)}, bf16[256,2048]{1,0:T(8,128)(2,1)}, u32[]{:S(2)}, u32[]{:S(2)}) collective-permute-start(bf16[256,2048]{1,0:T(8,128)(2,1)} %get-tuple-element.119), channel_id=1, source_target_pairs={{0,2},{1,0},{3,1},{2,3},{4,6},{5,4},{7,5},{6,7},{8,10},{9,8},{11,9... | collective-permute-start | bytes 3145736 | tf_op jit(solution)/shard_map/ppermute | solution.py:52
  55.6 71.1 %collective-permute-start.22 = (bf16[256,2048]{1,0:T(8,128)(2,1)}, bf16[256,2048]{1,0:T(8,128)(2,1)}, u32[]{:S(2)}, u32[]{:S(2)}) collective-permute-start(bf16[256,2048]{1,0:T(8,128)(2,1)} %get-tuple-element.119), channel_id=1, source_target_pairs={{0,1},{1,3},{3,2},{2,0},{4,5},{5,7},{7,6},{6,4},{8,9},{9,11},{11,1... | collective-permute-start | bytes 3145736 | tf_op jit(solution)/shard_map/ppermute | solution.py:51
  57.9 946.2 %reduce-scatter.5.cloned.1.call-start = ((), (), s32[]{:S(2)}) async-start(), calls=%async_computation.12 | async-start | bytes 7077888 | tf_op jit(solution)/shard_map/reduce_scatter | solution.py:316
  117.0 163.9 %collective-permute-start.37 = (bf16[256,2048]{1,0:T(8,128)(2,1)}, bf16[256,2048]{1,0:T(8,128)(2,1)S(1)}, u32[]{:S(2)}, u32[]{:S(2)}) collective-permute-start(bf16[256,2048]{1,0:T(8,128)(2,1)} %get-tuple-element.114), channel_id=1, source_target_pairs={{0,2},{1,0},{3,1},{2,3},{4,6},{5,4},{7,5},{6,7},{8,10},{9,8},{11,9... | collective-permute-start | bytes 3145736 | tf_op jit(solution)/shard_map/ppermute | solution.py:52
  126.7 155.1 %collective-permute-start.38 = (bf16[256,2048]{1,0:T(8,128)(2,1)}, bf16[256,2048]{1,0:T(8,128)(2,1)S(1)}, u32[]{:S(2)}, u32[]{:S(2)}) collective-permute-start(bf16[256,2048]{1,0:T(8,128)(2,1)} %get-tuple-element.114), channel_id=1, source_target_pairs={{0,1},{1,3},{3,2},{2,0},{4,5},{5,7},{7,6},{6,4},{8,9},{9,11},{11,1... | collective-permute-start | bytes 3145736 | tf_op jit(solution)/shard_map/ppermute | solution.py:51
  128.3 154.7 %collective-permute-start.54 = (bf16[256,2048]{1,0:T(8,128)(2,1)}, bf16[256,2048]{1,0:T(8,128)(2,1)S(1)}, u32[]{:S(2)}, u32[]{:S(2)}) collective-permute-start(bf16[256,2048]{1,0:T(8,128)(2,1)} %get-tuple-element.115), channel_id=1, source_target_pairs={{0,1},{1,3},{3,2},{2,0},{4,5},{5,7},{7,6},{6,4},{8,9},{9,11},{11,1... | collective-permute-start | bytes 3145736 | tf_op jit(solution)/shard_map/ppermute | solution.py:51
  281.7 66.0 %collective-permute-start.28 = (bf16[256,2048]{1,0:T(8,128)(2,1)}, bf16[256,2048]{1,0:T(8,128)(2,1)}, u32[]{:S(2)}, u32[]{:S(2)}) collective-permute-start(bf16[256,2048]{1,0:T(8,128)(2,1)} %pad_maximum_fusion.7), channel_id=1, source_target_pairs={{0,2},{1,0},{3,1},{2,3},{4,6},{5,4},{7,5},{6,7},{8,10},{9,8},{11,9... | collective-permute-start | bytes 3145736 | tf_op jit(solution)/shard_map/ppermute | solution.py:76
  283.0 65.3 %collective-permute-start.26 = (bf16[256,2048]{1,0:T(8,128)(2,1)}, bf16[256,2048]{1,0:T(8,128)(2,1)}, u32[]{:S(2)}, u32[]{:S(2)}) collective-permute-start(bf16[256,2048]{1,0:T(8,128)(2,1)} %pad_maximum_fusion.6), channel_id=1, source_target_pairs={{0,1},{1,3},{3,2},{2,0},{4,5},{5,7},{7,6},{6,4},{8,9},{9,11},{11,1... | collective-permute-start | bytes 3145736 | tf_op jit(solution)/shard_map/ppermute | solution.py:75
  498.6 59.2 %collective-permute-start.41 = (bf16[128,2048]{1,0:T(8,128)(2,1)S(1)}, bf16[128,2048]{1,0:T(8,128)(2,1)S(1)}, u32[]{:S(2)}, u32[]{:S(2)}) collective-permute-start(bf16[128,2048]{1,0:T(8,128)(2,1)S(1)} %get-tuple-element.77), channel_id=1, source_target_pairs={{0,1},{1,3},{3,2},{2,0},{4,5},{5,7},{7,6},{6,4},{8,9},{9,11},{11,1... | collective-permute-start | bytes 1572872 | tf_op jit(solution)/shard_map/ppermute | solution.py:64
  499.3 59.3 %collective-permute-start.43 = (bf16[128,2048]{1,0:T(8,128)(2,1)S(1)}, bf16[128,2048]{1,0:T(8,128)(2,1)S(1)}, u32[]{:S(2)}, u32[]{:S(2)}) collective-permute-start(bf16[128,2048]{1,0:T(8,128)(2,1)S(1)} %get-tuple-element.78), channel_id=1, source_target_pairs={{0,2},{1,0},{3,1},{2,3},{4,6},{5,4},{7,5},{6,7},{8,10},{9,8},{11,9... | collective-permute-start | bytes 1572872 | tf_op jit(solution)/shard_map/ppermute | solution.py:65
  584.0 91.8 %collective-permute-start.36 = (bf16[256,2048]{1,0:T(8,128)(2,1)S(1)}, bf16[256,2048]{1,0:T(8,128)(2,1)S(1)}, u32[]{:S(2)}, u32[]{:S(2)}) collective-permute-start(bf16[256,2048]{1,0:T(8,128)(2,1)S(1)} %pad_maximum_fusion.9), channel_id=1, source_target_pairs={{0,2},{1,0},{3,1},{2,3},{4,6},{5,4},{7,5},{6,7},{8,10},{9,8},{11,9... | collective-permute-start | bytes 3145736 | tf_op jit(solution)/shard_map/ppermute | solution.py:76
  606.4 69.3 %collective-permute-start.34 = (bf16[256,2048]{1,0:T(8,128)(2,1)S(1)}, bf16[256,2048]{1,0:T(8,128)(2,1)S(1)}, u32[]{:S(2)}, u32[]{:S(2)}) collective-permute-start(bf16[256,2048]{1,0:T(8,128)(2,1)S(1)} %pad_maximum_fusion.8), channel_id=1, source_target_pairs={{0,1},{1,3},{3,2},{2,0},{4,5},{5,7},{7,6},{6,4},{8,9},{9,11},{11,1... | collective-permute-start | bytes 3145736 | tf_op jit(solution)/shard_map/ppermute | solution.py:75
  607.1 62.7 %collective-permute-start.20 = (bf16[256,2048]{1,0:T(8,128)(2,1)S(1)}, bf16[256,2048]{1,0:T(8,128)(2,1)S(1)}, u32[]{:S(2)}, u32[]{:S(2)}) collective-permute-start(bf16[256,2048]{1,0:T(8,128)(2,1)S(1)} %pad_maximum_fusion.5), channel_id=1, source_target_pairs={{0,2},{1,0},{3,1},{2,3},{4,6},{5,4},{7,5},{6,7},{8,10},{9,8},{11,9... | collective-permute-start | bytes 3145736 | tf_op jit(solution)/shard_map/ppermute | solution.py:76
  723.3 59.1 %collective-permute-start.63 = (bf16[128,2048]{1,0:T(8,128)(2,1)S(1)}, bf16[128,2048]{1,0:T(8,128)(2,1)S(1)}, u32[]{:S(2)}, u32[]{:S(2)}) collective-permute-start(bf16[128,2048]{1,0:T(8,128)(2,1)S(1)} %slice.684), channel_id=1, source_target_pairs={{0,1},{1,3},{3,2},{2,0},{4,5},{5,7},{7,6},{6,4},{8,9},{9,11},{11,1... | collective-permute-start | bytes 1572872 | tf_op jit(solution)/shard_map/ppermute | solution.py:54
  836.1 183.4 %reduce-scatter.9.cloned.1.call-start = ((), (), s32[]{:S(2)}) async-start(), calls=%async_computation.14 | async-start | bytes 9437184 | tf_op jit(solution)/shard_map/reduce_scatter | solution.py:316
  867.8 162.8 %reduce-scatter.7.cloned.1.call-start = ((), (), s32[]{:S(2)}) async-start(), calls=%async_computation.13 | async-start | bytes 2359296 | tf_op jit(solution)/shard_map/reduce_scatter | solution.py:316
  877.5 243.7 %reduce-scatter.11.cloned.1.call-start = ((), (), s32[]{:S(2)}) async-start(), calls=%async_computation.15 | async-start | bytes 9437184 | tf_op jit(solution)/shard_map/reduce_scatter | solution.py:316
  1019.5 104.4 %all-to-all-start.3 = ((bf16[4,64,2048]{2,1,0:T(8,128)(2,1)}), bf16[4,64,2048]{2,1,0:T(8,128)(2,1)S(1)}, u32[]{:S(2)}, u32[]{:S(2)}) async-start(bf16[4,64,2048]{2,1,0:T(8,128)(2,1)} %bitcast.198), calls=%async_computation.6 | async-start | bytes 2097152 | tf_op jit(solution)/shard_map/all_to_all | solution.py:314
  (162 other events, 4098.2 us)
Sparse Core Ops, SparseCore 0:
  28.6 64.4 all-gather.4
  94.7 29.3 all-gather.6
  125.7 80.9 all-gather.8
  208.1 80.5 all-gather.10
  836.2 67.1 reduce-scatter.4
  905.5 88.5 reduce-scatter.8
  996.4 34.1 reduce-scatter.6
  1032.9 88.2 reduce-scatter.10

commit v2 on v1

v2 whole, which is shorter than its diff:
```python
from functools import partial

import jax
import jax.numpy as jnp
import numpy as np
from jax import lax
from jax.experimental import pallas as pl
from jax.experimental.pallas import tpu as pltpu
from jax.sharding import PartitionSpec as P

HEAD_DIM = 64
PAIR = 2 * HEAD_DIM
epsilon = 1e-05
LOG2E = 1.4426950408889634
bf16, f32 = jnp.bfloat16, jnp.float32
ALL = ("batch", "seq")
VMEM_LIMIT = 56 * 1024 * 1024


def dot_nn(a, b):
    return jnp.dot(a, b, preferred_element_type=f32)


def dot_nt(a, b):
    return lax.dot_general(a, b, (((1,), (1,)), ((), ())), preferred_element_type=f32)


def dot_tn(a, b):
    return lax.dot_general(a, b, (((0,), (0,)), ((), ())), preferred_element_type=f32)


PARAMS = pltpu.CompilerParams(vmem_limit_bytes=VMEM_LIMIT)
PACE = 0.5


def cost(flops):
    return pl.CostEstimate(flops=int(PACE * flops), bytes_accessed=int(PACE * flops / 320), transcendentals=0)


def tile_of(width, most=512):
    return next(t for t in (most, 256, 128, width) if width % t == 0)


def listed(value):
    return list(value) if isinstance(value, (list, tuple)) else [value]


def rows_of(pieces):
    return sum(p.shape[0] for p in pieces)


def fixed(shape):
    return pl.BlockSpec(shape, lambda j: (0,) * len(shape))


def join(refs, whole):
    at = 0
    for ref in refs:
        whole[at : at + ref.shape[0], :] = ref[...]
        at += ref.shape[0]


def first_step(body):
    pl.when(pl.program_id(0) == 0)(body)


def matmul(left, right, dot, parts=None):
    left = listed(left)
    n, rows, depth = len(left), rows_of(left), left[0].shape[1]
    width = right.shape[1] if dot is dot_nn else right.shape[0]
    tile, ranges = tile_of(width), parts or [[(0, rows)]]
    sizes = [sum(stop - begin for begin, stop in part) for part in ranges]

    def kernel(*refs):
        whole = refs[0]
        if n > 1:
            whole = refs[-1]
            first_step(lambda: join(refs[:n], whole))
        total = dot(whole[...], refs[n][...]).astype(bf16)
        for ref, part in zip(refs[n + 1 :], ranges):
            at = 0
            for begin, stop in part:
                ref[at : at + stop - begin, :] = total[begin:stop]
                at += stop - begin

    strip = (
        pl.BlockSpec((depth, tile), lambda j: (0, j)) if dot is dot_nn else pl.BlockSpec((tile, depth), lambda j: (j, 0))
    )
    out = pl.pallas_call(
        kernel,
        out_shape=tuple(jax.ShapeDtypeStruct((size, width), bf16) for size in sizes),
        grid=(width // tile,),
        in_specs=[fixed(p.shape) for p in left] + [strip],
        out_specs=tuple(pl.BlockSpec((size, tile), lambda j: (0, j)) for size in sizes),
        scratch_shapes=[pltpu.VMEM((rows, depth), bf16)] if n > 1 else [],
        compiler_params=PARAMS, cost_estimate=cost(3.5 * rows * depth * width), name="matmul",
    )(*left, right)
    return out if parts else out[0]


def weight_sum(lefts, rights):
    lefts, rights = [listed(v) for v in lefts], [listed(v) for v in rights]
    tokens = [rows_of(v) for v in lefts]
    rows, width = lefts[0][0].shape[1], rights[0][0].shape[1]
    tile = tile_of(rows, 256)
    sizes = [len(v) for v in lefts + rights]
    spots = [pltpu.VMEM((t, tile), bf16) for t in tokens] + [pltpu.VMEM((t, width), bf16) for t in tokens]
    spots = [spot if size > 1 else pltpu.VMEM((16, 128), bf16) for spot, size in zip(spots, sizes)]
    n = len(lefts)

    def kernel(*refs):
        out, spot, at, wholes = refs[sum(sizes)], refs[sum(sizes) + 1 :], 0, []
        for k, size in enumerate(sizes):
            group = refs[at : at + size]
            at += size
            if size == 1:
                wholes.append(group[0])
                continue
            wholes.append(spot[k])
            if k < n:
                join(group, spot[k])
            else:
                first_step(partial(join, group, spot[k]))
        total = sum(dot_tn(wholes[k][...], wholes[n + k][...]) for k in range(n))
        out[...] = total.astype(bf16)

    return pl.pallas_call(
        kernel,
        out_shape=jax.ShapeDtypeStruct((rows, width), bf16),
        grid=(rows // tile,),
        in_specs=[pl.BlockSpec((p.shape[0], tile), lambda j: (0, j)) for v in lefts for p in v]
        + [fixed(p.shape) for v in rights for p in v],
        out_specs=pl.BlockSpec((tile, width), lambda j: (j, 0)),
        scratch_shapes=spots,
        compiler_params=PARAMS, cost_estimate=cost(3.3 * sum(tokens) * rows * width), name="weight_sum",
    )(*(p for v in lefts + rights for p in v))


def norm_parts(rows):
    centered = rows - jnp.mean(rows, -1, keepdims=True)
    spread = jnp.mean(centered * centered, -1, keepdims=True)
    inverse = lax.rsqrt(spread + epsilon)
    return centered * inverse, inverse


def norm_back(grad, gain, unit, inverse):
    scaled = grad * gain
    return inverse * (
        scaled - jnp.mean(scaled, -1, keepdims=True) - unit * jnp.mean(scaled * unit, -1, keepdims=True)
    )


def project(pieces, gain, shift, w_qkv, bias):
    n, rows, (depth, width) = len(pieces), rows_of(pieces), w_qkv.shape
    tile = tile_of(width)

    def kernel(*refs):
        gain_ref, shift_ref, w_ref, bias_ref, normed, out = refs[n:]

        def norm():
            at = 0
            for ref in refs[:n]:
                for k in range(0, ref.shape[0], 64):
                    unit, _ = norm_parts(ref[k : k + 64, :].astype(f32))
                    normed[at + k : at + k + 64, :] = (unit * gain_ref[...] + shift_ref[...]).astype(bf16)
                at += ref.shape[0]

        first_step(norm)
        out[...] = (dot_nn(normed[...], w_ref[...]) + bias_ref[...]).astype(bf16)

    return pl.pallas_call(
        kernel,
        out_shape=(jax.ShapeDtypeStruct((rows, depth), bf16), jax.ShapeDtypeStruct((rows, width), bf16)),
        grid=(width // tile,),
        in_specs=[fixed(p.shape) for p in pieces]
        + [fixed((1, depth)), fixed((1, depth)), pl.BlockSpec((depth, tile), lambda j: (0, j)), pl.BlockSpec((1, tile), lambda j: (0, j))],
        out_specs=(fixed((rows, depth)), pl.BlockSpec((rows, tile), lambda j: (0, j))),
        compiler_params=PARAMS, cost_estimate=cost(5 * rows * depth * width), name="project",
    )(*pieces, gain, shift, w_qkv, bias)


def gelu_both(pre):
    below = 0.5 * (1.0 + lax.erf(pre * (0.5**0.5)))
    density = jnp.exp(-0.5 * pre * pre) * ((2.0 * np.pi) ** -0.5)
    return pre * below, below + pre * density


def hidden_both(normed, grad_hidden, w_1, bias):
    n, rows, (depth, width) = len(normed), rows_of(normed), w_1.shape
    tile = tile_of(width)

    def kernel(*refs):
        g_ref, w1_ref, b_ref, h_ref, p_ref, s_ref, whole = refs[n:]
        first_step(lambda: join(refs[:n], whole))
        value, slope = gelu_both(dot_nn(whole[...], w1_ref[...]) + b_ref[...])
        h_ref[...] = value.astype(bf16)
        grad_pre = (g_ref[...].astype(f32) * slope).astype(bf16)
        p_ref[...] = grad_pre
        s_ref[...] = jnp.sum(grad_pre.astype(f32), 0, keepdims=True)

    part = pl.BlockSpec((rows, tile), lambda j: (0, j))
    line = pl.BlockSpec((1, tile), lambda j: (0, j))
    return pl.pallas_call(
        kernel,
        out_shape=(jax.ShapeDtypeStruct((rows, width), bf16),) * 2 + (jax.ShapeDtypeStruct((1, width), f32),),
        grid=(width // tile,),
        in_specs=[fixed(p.shape) for p in normed] + [part, pl.BlockSpec((depth, tile), lambda j: (0, j)), line],
        out_specs=(part, part, line),
        scratch_shapes=[pltpu.VMEM((rows, depth), bf16)],
        compiler_params=PARAMS, cost_estimate=cost(5 * rows * depth * width), name="hidden_both",
    )(*normed, grad_hidden, w_1, bias)


STEP = 64


def own_rows(depth):
    return pl.BlockSpec((STEP, depth), lambda j: (j, 0))


def slot_rows(slot, depth):
    return pl.BlockSpec((1, STEP, depth), lambda j: (slot, j, 0))


def summed_rows(rows, depth):
    half = rows // 2 // STEP
    spec = lambda place: pl.BlockSpec((STEP, depth), lambda j: (place(j), 0))
    return [
        own_rows(depth), spec(lambda j: jnp.maximum(j, half)), spec(lambda j: jnp.minimum(j, half - 1) + half),
        spec(lambda j: jnp.minimum(j, half - 1)), spec(lambda j: jnp.maximum(j - half, 0)),
    ]


def summed(refs, steps):
    own, up, down, far_up, far_down = (ref[...].astype(f32) for ref in refs)
    early = pl.program_id(0) < steps // 2
    return own + jnp.where(early, far_up, up) + jnp.where(early, down, far_down)


def second_norm(slot, branch, inputs, active, bias, gain, shift):
    rows, depth = branch[0].shape

    def kernel(*refs):
        x, act, bias_ref, gain_ref, shift_ref, middle, normed = refs[5:]
        total = summed(refs[:5], rows // STEP) + bias_ref[...]
        total = x[0].astype(f32) + act[...] * total
        middle[...] = total
        normed[...] = (norm_parts(total)[0] * gain_ref[...] + shift_ref[...]).astype(bf16)

    return pl.pallas_call(
        kernel,
        out_shape=(jax.ShapeDtypeStruct((rows, depth), f32), jax.ShapeDtypeStruct((rows, depth), bf16)),
        grid=(rows // STEP,),
        in_specs=summed_rows(rows, depth) + [slot_rows(slot, depth), own_rows(1)] + [fixed((1, depth))] * 3,
        out_specs=(own_rows(depth), own_rows(depth)),
        compiler_params=PARAMS, cost_estimate=cost(6e9), name="second_norm",
    )(*branch, inputs, active, bias, gain, shift)


def add_line(sums, line, value):
    sums[line : line + 1, :] += jnp.sum(value, 0, keepdims=True)


def second_norm_back(slot, back, middle, cotangent, active, gain):
    rows, depth = middle.shape

    def kernel(*refs):
        mid, cot, act, gain_ref, grad_middle, grad_branch, sums = refs[5:]

        @first_step
        def _():
            sums[...] = jnp.zeros_like(sums)

        grad = summed(refs[:5], rows // STEP)
        unit, inverse = norm_parts(mid[...])
        outer = cot[0].astype(f32)
        total = outer + norm_back(grad, gain_ref[...], unit, inverse)
        grad_middle[...] = total
        branch = (act[...] * total).astype(bf16)
        grad_branch[...] = branch
        add_line(sums, 0, grad * unit)
        add_line(sums, 1, grad)
        add_line(sums, 2, branch.astype(f32))
        add_line(sums, 3, (act[...] * outer).astype(bf16).astype(f32))

    return pl.pallas_call(
        kernel,
        out_shape=(
            jax.ShapeDtypeStruct((rows, depth), f32), jax.ShapeDtypeStruct((rows, depth), bf16),
            jax.ShapeDtypeStruct((8, depth), f32),
        ),
        grid=(rows // STEP,),
        in_specs=summed_rows(rows, depth) + [own_rows(depth), slot_rows(slot, depth), own_rows(1), fixed((1, depth))],
        out_specs=(own_rows(depth), own_rows(depth), fixed((8, depth))),
        compiler_params=PARAMS, cost_estimate=cost(7e9), name="second_norm_back",
    )(*back, middle, cotangent, active, gain)


def first_norm_back(slot, back, inputs, grad_middle, gain, others):
    (rows, depth), slots = grad_middle.shape, inputs.shape[0]
    more = [] if others is None else [others]

    def kernel(*refs):
        x, grad_mid, gain_ref = refs[5:8]
        out, sums = refs[-2:]

        @first_step
        def _():
            sums[...] = jnp.zeros_like(sums)

        grad = summed(refs[:5], rows // STEP)
        unit, inverse = norm_parts(x[0].astype(f32))
        out[0] = (grad_mid[...] + norm_back(grad, gain_ref[...], unit, inverse)).astype(bf16)
        add_line(sums, 0, grad * unit)
        add_line(sums, 1, grad)

    return pl.pallas_call(
        kernel,
        out_shape=(jax.ShapeDtypeStruct((slots, rows, depth), bf16), jax.ShapeDtypeStruct((8, depth), f32)),
        grid=(rows // STEP,),
        in_specs=summed_rows(rows, depth) + [slot_rows(slot, depth), own_rows(depth), fixed((1, depth))]
        + [pl.BlockSpec(memory_space=pl.ANY)] * len(more),
        out_specs=(slot_rows(slot, depth), fixed((8, depth))),
        input_output_aliases={8: 0} if more else {},
        compiler_params=PARAMS, cost_estimate=cost(7e9), name="first_norm_back",
    )(*back, inputs, grad_middle, gain, *more)


def final_sum(slot, slots, branch, middle, active, bias, others):
    rows, depth = middle.shape
    more = [] if others is None else [others]

    def kernel(*refs):
        mid, act, bias_ref = refs[5:8]
        total = summed(refs[:5], rows // STEP) + bias_ref[...]
        refs[-1][0] = (mid[...] + act[...] * total).astype(bf16)

    return pl.pallas_call(
        kernel,
        out_shape=jax.ShapeDtypeStruct((slots, rows, depth), bf16),
        grid=(rows // STEP,),
        in_specs=summed_rows(rows, depth) + [own_rows(depth), own_rows(1), fixed((1, depth))] + [pl.BlockSpec(memory_space=pl.ANY)] * len(more),
        out_specs=slot_rows(slot, depth),
        input_output_aliases={8: 0} if more else {},
        compiler_params=PARAMS, cost_estimate=cost(6e9), name="final_sum",
    )(*branch, middle, active, bias, *more)


def head_pieces(weights, groups, blocks):
    rows = weights[0].shape[0]

    def kernel(*refs):
        for k in range(blocks):
            strips = [ref[:, (g * blocks + k) * rows : (g * blocks + k + 1) * rows] for ref in refs[:-1] for g in range(groups)]
            refs[-1][k] = jnp.concatenate(strips, 1)

    return pl.pallas_call(
        kernel,
        out_shape=jax.ShapeDtypeStruct((blocks, rows, 3 * groups * rows), bf16),
        compiler_params=PARAMS, cost_estimate=cost(2e9), name="head_pieces",
    )(*weights)


def unit_pieces(weight, groups, blocks):
    (rows, width), n = weight.shape, weight.shape[1] // (groups * blocks)

    def kernel(ref, out):
        for k in range(blocks):
            for g in range(groups):
                out[k, :, g * n : (g + 1) * n] = ref[:, (g * blocks + k) * n : (g * blocks + k + 1) * n]

    return pl.pallas_call(
        kernel,
        out_shape=jax.ShapeDtypeStruct((blocks, rows, groups * n), bf16),
        compiler_params=PARAMS, cost_estimate=cost(2e9), name="unit_pieces",
    )(weight) if n % 128 == 0 else weight.reshape(rows, groups, blocks, n).transpose(2, 0, 1, 3).reshape(blocks, rows, groups * n)


def unit_rows(pieces, groups):
    blocks, rows, width = pieces.shape
    n = width // groups

    def kernel(ref, out):
        for k in range(blocks):
            for g in range(groups):
                out[:, (g * blocks + k) * n : (g * blocks + k + 1) * n] = ref[k, :, g * n : (g + 1) * n].astype(f32)

    return pl.pallas_call(
        kernel,
        out_shape=jax.ShapeDtypeStruct((rows, blocks * width), f32),
        compiler_params=PARAMS, cost_estimate=cost(2e9), name="unit_rows",
    )(pieces) if n % 128 == 0 else pieces.reshape(blocks, rows, groups, n).transpose(1, 2, 0, 3).reshape(rows, -1).astype(f32)


def head_rows(pieces, groups):
    blocks, rows, width = pieces.shape

    def kernel(ref, *outs):
        for c, out in enumerate(outs):
            strips = [
                ref[k, :, (c * groups + g) * rows : (c * groups + g + 1) * rows] for g in range(groups) for k in range(blocks)
            ]
            out[...] = jnp.concatenate(strips, 1).astype(f32)

    return pl.pallas_call(
        kernel,
        out_shape=(jax.ShapeDtypeStruct((rows, blocks * width // 3), f32),) * 3,
        compiler_params=PARAMS, cost_estimate=cost(2e9), name="head_rows",
    )(pieces)


def after(value, others):
    return value if others is None else lax.optimization_barrier((value, others))[0]


class Clock:
    def __init__(self):
        self.last = None

    def now(self, value):
        return after(value, self.last)

    def did(self, value):
        self.last = jax.tree.leaves(value)
        return value


class Ring:
    def __init__(self, size):
        self.size = size
        self.order = [i ^ (i >> 1) for i in range(size)]
        self.place = [self.order.index(i) for i in range(size)]

    def parts(self, rows):
        n, half = self.size, rows // 2
        first = lambda k: (k * rows, k * rows + half)
        second = lambda k: (k * rows + half, (k + 1) * rows)
        far = n // 2
        out = [[(0, rows)], [first(far), second(far - 1)], [second(far), first(far + 1)]]
        for k in range(far - 1, 1, -1):
            out += [[first(k)], [second(k - 1)], [second(n - k)], [first(n - k + 1)]]
        return out + [[first(1)], [second(n - 1)]]

    def send(self, value, steps):
        n = self.size
        return lax.ppermute(value, "seq", [(self.order[i], self.order[(i + steps) % n]) for i in range(n)])

    def mine(self):
        place, shift = lax.axis_index("seq"), 1
        while shift < self.size:
            place = place ^ (place >> shift)
            shift *= 2
        return place

    def at(self, steps):
        place = (self.mine() + steps) & (self.size - 1)
        return place ^ (place >> 1)

    def steps_to(self):
        return (jnp.array(self.place, jnp.int32) - self.mine()) & (self.size - 1)

    def swap(self, pieces):
        take = lambda k: lax.dynamic_slice_in_dim(pieces, self.at(k), 1)
        out = lax.dynamic_update_slice_in_dim(jnp.zeros_like(pieces), take(0), self.at(0), 0)
        for k in range(1, self.size):
            came = self.send(take(k), k)
            out = lax.dynamic_update_slice_in_dim(out, came, self.at(-k), 0)
        return out


class Gather:
    def __init__(self, ring, clock, block):
        self.ring, self.clock = ring, clock
        self.half = block.shape[0] // 2
        self.near, self.far = [block], []
        block = clock.now(block)
        self.rising, self.falling = ring.send(block, 1), ring.send(block, -1)

    def go(self):
        ring = self.ring
        for _ in range(2, ring.size // 2):
            self.far.append(self.rising)
            self.near.append(self.falling)
            self.rising, self.falling = ring.send(self.rising, 1), ring.send(self.falling, -1)
        rising, falling = self.clock.did(self.clock.now((self.rising, self.falling)))
        self.far.append(rising)
        self.near.append(falling)
        first, second = self.clock.did((rising[: self.half], falling[self.half :]))
        self.middle = [ring.send(first, 1), ring.send(second, -1)]

    def arrive(self):
        self.middle = list(self.clock.did(self.clock.now(tuple(self.middle))))

    def result(self):
        return self.clock.now(self.near + self.middle + self.far[::-1])


class Scatter:
    def __init__(self, ring, clock, part):
        self.ring, self.clock, self.part = ring, clock, part
        self.up, self.down = ring.send(part[1], 1), ring.send(part[2], -1)

    def go(self):
        n, send, now, did = self.ring.size, self.ring.send, self.clock.now, self.clock.did
        half = self.part[1].shape[0] // 2
        rest = self.part[3:]
        for k in range(0, 4 * (n // 2 - 2), 4):
            up = jnp.concatenate([add16(rest[k], self.up[:half]), add16(rest[k + 1], self.up[half:])])
            down = jnp.concatenate([add16(rest[k + 2], self.down[:half]), add16(rest[k + 3], self.down[half:])])
            self.up, self.down = send(up, 1), send(down, -1)
        up, down = did(now((self.up, self.down)))
        far_up, far_down = did((add16(rest[-2], up[:half]), add16(rest[-1], down[:half])))
        self.up, self.down = up, down
        self.far_up, self.far_down = send(far_up, 1), send(far_down, -1)

    def arrive(self):
        self.far_up, self.far_down = self.clock.did(self.clock.now((self.far_up, self.far_down)))

    def result(self):
        return (self.part[0], self.up, self.down) + self.clock.now((self.far_up, self.far_down))


def add16(a, b):
    return (a.astype(f32) + b.astype(f32)).astype(bf16)


def gather_small(block, devices):
    place = lax.axis_index(ALL)
    have, bit = block[None], 1
    while bit < devices:
        other = lax.ppermute(have, ALL, [(i, i ^ bit) for i in range(devices)])
        low = (place & bit) == 0
        have = jnp.concatenate([jnp.where(low, have, other), jnp.where(low, other, have)])
        bit *= 2
    return have


class SmallScatter:
    def __init__(self, clock, total):
        self.clock, self.keep, self.came, self.devices = clock, total, None, total.shape[0]

    def gathered(self):
        total = self.clock.now(self.keep)
        return total if self.came is None else self.clock.did(total + self.clock.now(self.came))

    def step(self):
        bit = self.keep.shape[0] // 2
        if bit == 0:
            return
        total = self.gathered()
        low = (lax.axis_index(ALL) & bit) == 0
        self.keep = jnp.where(low, total[:bit], total[bit:])
        send = jnp.where(low, total[bit:], total[:bit])
        self.came = lax.ppermute(send, ALL, [(i, i ^ bit) for i in range(self.devices)])

    def result(self):
        while self.keep.shape[0] > 1:
            self.step()
        return self.gathered()[0]


def attend_kernel(blocks, rows, steps, q_ref, k_ref, v_ref, o_ref, lse_ref, keys, values_t):
    for a in range(blocks):
        here = pl.ds(pl.multiple_of(steps[a] * rows, rows), rows)
        keys[a * rows : (a + 1) * rows, :] = k_ref[here, :]
        values_t[:, a * rows : (a + 1) * rows] = v_ref[here, :].astype(f32).T.astype(bf16)
    lane = lax.broadcasted_iota(jnp.int32, (1, PAIR), 1)
    causal = lax.broadcasted_iota(jnp.int32, (rows, rows), 0) <= lax.broadcasted_iota(
        jnp.int32, (rows, rows), 1
    )
    scale = HEAD_DIM ** (-0.5) * LOG2E
    for i in range(blocks):
        here = pl.ds(pl.multiple_of(steps[i] * rows, rows), rows)
        query = q_ref[here, :]
        ahead = i * rows
        parts = []
        for head in range(2):
            own = (lane // HEAD_DIM == head).astype(bf16)
            lines = slice(head * HEAD_DIM, (head + 1) * HEAD_DIM)
            q_head = query * own
            diag = dot_nt(keys[ahead : ahead + rows, :], q_head) * scale
            diag = jnp.where(causal, diag, -1e30)
            top = jnp.max(diag, 0, keepdims=True)
            if i > 0:
                full = dot_nt(keys[:ahead, :], q_head) * scale
                top = jnp.maximum(top, jnp.max(full, 0, keepdims=True))
            diag = jnp.exp2(diag - top)
            total = jnp.sum(diag, 0, keepdims=True)
            mixed = dot_nn(values_t[lines, ahead : ahead + rows], diag.astype(bf16))
            if i > 0:
                full = jnp.exp2(full - top)
                total = total + jnp.sum(full, 0, keepdims=True)
                mixed = mixed + dot_nn(values_t[lines, :ahead], full.astype(bf16))
            parts.append(mixed / total)
            lse_ref[0, head : head + 1, ahead : ahead + rows] = top + jnp.log2(total)
        o_ref[here, :] = jnp.concatenate(parts).T.astype(bf16)


def attend(qkv, steps, blocks):
    tokens, width = qkv.shape[0], qkv.shape[1] // 3
    pairs, rows = width // PAIR, tokens // blocks
    column = lambda c: pl.BlockSpec((tokens, PAIR), lambda h, steps: (0, c * pairs + h))
    return pl.pallas_call(
        partial(attend_kernel, blocks, rows),
        out_shape=(
            jax.ShapeDtypeStruct((tokens, width), bf16),
            jax.ShapeDtypeStruct((pairs, 2, tokens), f32),
        ),
        grid_spec=pltpu.PrefetchScalarGridSpec(
            num_scalar_prefetch=1,
            grid=(pairs,),
            in_specs=[column(0), column(1), column(2)],
            out_specs=(column(0), pl.BlockSpec((1, 2, tokens), lambda h, steps: (h, 0, 0))),
            scratch_shapes=[pltpu.VMEM((tokens, PAIR), bf16), pltpu.VMEM((PAIR, tokens), bf16)],
        ),
        compiler_params=pltpu.CompilerParams(vmem_limit_bytes=VMEM_LIMIT),
        cost_estimate=cost(32 * tokens * tokens * width),
        name="attend",
    )(steps, qkv, qkv, qkv)


def attend_back_kernel(
    blocks, rows, steps, q_ref, k_ref, v_ref, g_ref, lse_ref, d_ref, keys, keys_t, values, dk, dv, dk16, dv16
):
    @pl.when(pl.program_id(1) == 0)
    def _():
        for a in range(blocks):
            here = pl.ds(pl.multiple_of(steps[a] * rows, rows), rows)
            place = slice(a * rows, (a + 1) * rows)
            keys[place, :] = k_ref[here, :]
            keys_t[:, place] = k_ref[here, :].astype(f32).T.astype(bf16)
            values[place, :] = v_ref[here, :]
        dk[...] = jnp.zeros_like(dk)
        dv[...] = jnp.zeros_like(dv)
        lane = lax.broadcasted_iota(jnp.int32, (1, PAIR), 1)
        scaling = HEAD_DIM ** (-0.5)
        for i in range(blocks):
            here = pl.ds(pl.multiple_of(steps[i] * rows, rows), rows)
            query, grad = q_ref[here, :], g_ref[here, :]
            length = (i + 1) * rows
            causal = lax.broadcasted_iota(jnp.int32, (length, rows), 0) <= (
                lax.broadcasted_iota(jnp.int32, (length, rows), 1) + i * rows
            )
            parts = []
            for head in range(2):
                own = (lane // HEAD_DIM == head).astype(bf16)
                lines = slice(head * HEAD_DIM, (head + 1) * HEAD_DIM)
                q_head, g_head = query * own, grad * own
                lse = lse_ref[0, head : head + 1, i * rows : (i + 1) * rows]
                logits = dot_nt(keys[:length, :], q_head) * (scaling * LOG2E)
                probs = jnp.where(causal, jnp.exp2(logits - lse), 0.0)
                grad_probs = dot_nt(values[:length, :], g_head)
                inner = jnp.sum(grad_probs * probs, 0, keepdims=True)
                grad_raw = (probs * (grad_probs - inner) * scaling).astype(bf16)
                parts.append(dot_nn(keys_t[lines, :length], grad_raw))
                dk[:length, :] += dot_nn(grad_raw, q_head)
                dv[:length, :] += dot_nn(probs.astype(bf16), g_head)
            d_ref[here, :] = jnp.concatenate(parts).T.astype(bf16)
        for a in range(blocks):
            here = pl.ds(pl.multiple_of(steps[a] * rows, rows), rows)
            dk16[here, :] = dk[a * rows : (a + 1) * rows, :].astype(bf16)
            dv16[here, :] = dv[a * rows : (a + 1) * rows, :].astype(bf16)

    @pl.when(pl.program_id(1) == 1)
    def _():
        d_ref[...] = dk16[...]

    @pl.when(pl.program_id(1) == 2)
    def _():
        d_ref[...] = dv16[...]


def attend_back(qkv, grad_context, lse, steps, blocks):
    tokens, width = grad_context.shape
    pairs, rows = width // PAIR, tokens // blocks
    column = lambda c: pl.BlockSpec((tokens, PAIR), lambda h, c_out, steps: (0, c * pairs + h))
    wide = lambda dtype: pltpu.VMEM((tokens, PAIR), dtype)
    return pl.pallas_call(
        partial(attend_back_kernel, blocks, rows),
        out_shape=jax.ShapeDtypeStruct((tokens, 3 * width), bf16),
        grid_spec=pltpu.PrefetchScalarGridSpec(
            num_scalar_prefetch=1,
            grid=(pairs, 3),
            in_specs=[
                column(0), column(1), column(2), column(0),
                pl.BlockSpec((1, 2, tokens), lambda h, c_out, steps: (h, 0, 0)),
            ],
            out_specs=pl.BlockSpec((tokens, PAIR), lambda h, c_out, steps: (0, c_out * pairs + h)),
            scratch_shapes=[
                wide(bf16), pltpu.VMEM((PAIR, tokens), bf16), wide(bf16),
                wide(f32), wide(f32), wide(bf16), wide(bf16),
            ],
        ),
        compiler_params=pltpu.CompilerParams(vmem_limit_bytes=VMEM_LIMIT),
        cost_estimate=cost(64 * tokens * tokens * width),
        name="attend_back",
    )(steps, qkv, qkv, qkv, grad_context, lse)


def body(
    inputs, cotangent, max_exit, min_exit, layer, wq, wk, wv, wo, gain_one, shift_one, bias_q, bias_v,
    bias_o, w_in, w_out, gain_two, shift_two, bias_in, bias_out,
):
    B, S = lax.axis_size("batch"), lax.axis_size("seq")
    devices = B * S
    s = lax.axis_index("seq")
    slots, T, D = inputs.shape
    r, rw = wq.shape[0], w_out.shape[0]
    Dl, Fl = D // S, rw * B
    whole_heads = r % HEAD_DIM == 0
    ring = Ring(S)
    steps = ring.steps_to()

    places = s * T + jnp.arange(T, dtype=jnp.int32)
    exits = max_exit[:, None] - (max_exit - min_exit)[:, None] * places[None, :] // (S * T - 1)
    active = (layer[0] < exits).astype(f32)[..., None]

    clock = Clock()
    grad_two = [(active[i] * cotangent[i].astype(f32)).astype(bf16) for i in range(slots)]
    gather = lambda x: lax.all_gather(x, "batch", axis=0, tiled=True)
    scatter = lambda x: lax.psum_scatter(x, "batch", scatter_dimension=0, tiled=True)
    qkv_pieces = (
        head_pieces((wq, wk, wv), B, S)
        if whole_heads
        else jnp.concatenate([w.reshape(r, S, Dl).transpose(1, 0, 2) for w in (wq, wk, wv)], -1)
    )
    in_pieces = unit_pieces(w_in, B, S)
    def start_layer(i, rows):
        normed[i], qkv[i] = clock.did(project(clock.now(rows), gain_a, shift_a, w_qkv, bias_qkv))

    def attention(i):
        context[i], lse[i] = clock.did(attend(clock.now(qkv[i]), steps, S))

    def branch_out(i):
        return clock.did(matmul(clock.now(context[i]), w_o, dot_nn, parts_out))

    def middle_of(i, branch):
        middle[i], own_normed = clock.did(
            second_norm(i, clock.now(branch), inputs, active[i], bias_o_full, gain_b, shift_b)
        )
        return own_normed

    def hidden_units(i):
        hidden[i], grad_pre[i], sum_pre[i] = clock.did(
            hidden_both(clock.now(normed_two[i]), grad_hidden[i], w_1, bias_hidden)
        )

    def hidden_back(i):
        grad_hidden[i] = clock.did(matmul(clock.now(grad_branch_two[i]), w_2, dot_nt))

    def normed_two_back(i):
        return clock.did(matmul(clock.now(grad_pre[i]), w_1, dot_nt, parts_out))

    def middle_back(i, back):
        grad_middle[i], own_grad_branch[i], sums_two[i] = clock.did(
            second_norm_back(i, clock.now(back), middle[i], cotangent, active[i], gain_b)
        )

    def context_back(i):
        grad_context[i] = clock.did(matmul(clock.now(grad_branch[i]), w_o, dot_nt))

    def attention_back(i):
        grad_qkv[i] = clock.did(attend_back(qkv[i], clock.now(grad_context[i]), lse[i], steps, S))

    def normed_back(i):
        return clock.did(matmul(clock.now(grad_qkv[i]), w_qkv, dot_nt, parts_out))

    def start_back(i, back):
        input_grad[i], sums_one[i] = clock.did(
            first_norm_back(i, clock.now(back), inputs, grad_middle[i], gain_a, input_grad[i - 1] if i else None)
        )

    def branch_two_out(i):
        return clock.did(matmul(clock.now(hidden[i]), w_2, dot_nn, parts_out))

    def finish(i, branch_two):
        output[i] = clock.did(
            final_sum(i, slots, clock.now(branch_two), middle[i], active[i], bias_out_full, output[i - 1] if i else None)
        )

    def gradient(lefts, rights):
        return clock.did(weight_sum(clock.now(lefts), rights))

    parts_out = ring.parts(T)

    tokens = lambda parts: sum(jnp.sum(p.astype(f32), 0) for p in parts)
    plain = lambda v: v.reshape(devices, r)
    pair_sum = lambda pairs, k: plain(pairs[0][k] + pairs[1][k])

    def own_heads(v):
        if whole_heads:
            spread = jnp.zeros((B, S, r), f32)
            return lax.dynamic_update_slice(spread, v.reshape(B, 1, r), (0, s, 0)).reshape(devices, r)
        return lax.dynamic_update_slice(jnp.zeros((D,), f32), v, (s * Dl,)).reshape(devices, r)

    def early_pack():
        own_hidden = lax.dynamic_update_slice(
            jnp.zeros((B, S, rw), f32), sum(sum_pre).reshape(B, 1, rw), (0, s, 0)
        ).reshape(devices, rw)
        parts = (
            pair_sum(sums_two, 2), pair_sum(sums_two, 0), pair_sum(sums_two, 1), pair_sum(sums_two, 3), own_hidden,
        )
        return jnp.concatenate(parts, -1)

    def late_pack():
        bias_sums = tokens(grad_qkv)
        parts = (
            pair_sum(sums_one, 0), pair_sum(sums_one, 1), own_heads(bias_sums[:Dl]),
            own_heads(bias_sums[2 * Dl :]),
        )
        return jnp.concatenate(parts, -1)

    fresh = lambda: [None] * slots
    normed, qkv, context, lse, middle, normed_two, sums_one, sums_two = (fresh() for _ in range(8))
    hidden, sum_pre, grad_pre, output, grad_middle, grad_branch = (fresh() for _ in range(6))
    own_grad_branch, grad_branch_two, grad_hidden, grad_context, grad_qkv, input_grad = (fresh() for _ in range(6))
    assert slots == 2
    begin, bring = partial(Scatter, ring, clock), partial(Gather, ring, clock)

    qkv_rows = clock.did(ring.swap(qkv_pieces).reshape(S * r, 3 * Dl))
    w_qkv = gather(qkv_rows)
    in_rows = ring.swap(clock.now(in_pieces)).reshape(S * r, Fl)
    in0 = bring(inputs[0])
    in_rows = clock.did(clock.now(in_rows))
    in0.go()
    if whole_heads:
        w_o = gather(clock.now(wo))
    else:
        w_o = lax.all_gather(clock.now(wo), ALL, axis=0, tiled=True)
        w_o = lax.dynamic_slice(w_o, (s * Dl, 0), (Dl, D))
    in1 = bring(inputs[1])

    small = (gain_one, shift_one, bias_q, bias_v, bias_o, gain_two, shift_two, bias_out)
    packed = clock.did(gather_small(clock.now(jnp.concatenate(small + (bias_in,))), devices))
    full = lambda k: packed[:, k * r : (k + 1) * r].reshape(1, D).astype(f32)
    mine = lambda k: (
        lax.dynamic_index_in_dim(packed.reshape(B, S, -1), s, 1, False)[:, k * r : (k + 1) * r]
        if whole_heads
        else lax.dynamic_slice(packed[:, k * r : (k + 1) * r].reshape(D), (s * Dl,), (Dl,))
    ).reshape(Dl).astype(f32)
    gain_a, shift_a, bias_o_full, gain_b, shift_b, bias_out_full = (full(k) for k in (0, 1, 4, 5, 6, 7))
    bias_qkv = jnp.concatenate([mine(2), jnp.zeros((Dl,), f32), mine(3)])[None]
    bias_hidden = (
        lax.dynamic_index_in_dim(packed.reshape(B, S, -1), s, 1, False)[:, len(small) * r :]
        .reshape(1, Fl).astype(f32)
    )

    in0.arrive()
    start_layer(0, in0.result())
    in1.go()
    w_2 = gather(clock.now(w_out))
    cot0 = bring(grad_two[0])
    attention(0)
    in1.arrive()
    br0 = begin(branch_out(0))
    w_1 = gather(clock.now(in_rows))
    start_layer(1, in1.result())
    cot0.go()
    attention(1)
    br0.go()
    cot0.arrive()
    cot1 = bring(grad_two[1])
    br1 = begin(branch_out(1))
    br0.arrive()
    nt0 = bring(middle_of(0, br0.result()))
    br1.go()
    grad_branch_two[0] = cot0.result()
    hidden_back(0)
    nt0.go()
    br1.arrive()
    nt1 = bring(middle_of(1, br1.result()))
    nt0.arrive()
    cot1.go()
    normed_two[0] = nt0.result()
    hidden_units(0)
    nt1.go()
    cot1.arrive()
    grad_branch_two[1] = cot1.result()
    hidden_back(1)
    gn0 = begin(normed_two_back(0))
    nt1.arrive()
    normed_two[1] = nt1.result()
    hidden_units(1)
    gn0.go()
    sum_w_2 = gradient(hidden, grad_branch_two)
    sum_w_2 = scatter(sum_w_2)
    gn0.arrive()
    middle_back(0, gn0.result())
    gb0 = bring(own_grad_branch[0])
    gn1 = begin(normed_two_back(1))
    sum_w_1 = gradient(normed_two, grad_pre)
    gb0.go()
    gn1.go()
    part = branch_two_out(0)
    gb0.arrive()
    out0 = begin(part)
    grad_branch[0] = gb0.result()
    context_back(0)
    gn1.arrive()
    middle_back(1, gn1.result())
    gb1 = bring(own_grad_branch[1])
    early = SmallScatter(clock, early_pack())
    early.step()
    sum_w_1 = scatter(after(clock.now(sum_w_1), sum_w_2))
    attention_back(0)
    gb1.go()
    out0.go()
    early.step()
    gx0 = begin(normed_back(0))
    part = branch_two_out(1)
    gb1.arrive()
    grad_branch[1] = gb1.result()
    context_back(1)
    out0.arrive()
    gx0.go()
    early.step()
    sum_o = gradient(context, grad_branch)
    if whole_heads:
        sum_o = scatter(after(clock.now(sum_o), sum_w_1))
    else:
        sum_o = lax.dynamic_update_slice(jnp.zeros((D, D), bf16), sum_o, (s * Dl, 0))
        sum_o = lax.psum_scatter(sum_o, ALL, scatter_dimension=0, tiled=True)
    out1 = begin(part)
    attention_back(1)
    gx0.arrive()
    out1.go()
    gx1 = begin(normed_back(1))
    sum_qkv = gradient(normed, grad_qkv)
    sum_qkv = scatter(after(clock.now(sum_qkv), sum_o))
    gx1.go()
    early.step()
    start_back(0, gx0.result())
    finish(0, out0.result())
    out1.arrive()
    finish(1, out1.result())
    sum_w_1 = ring.swap(clock.now(sum_w_1).reshape(S, r, Fl))
    gx1.arrive()
    start_back(1, gx1.result())
    sum_w_1 = clock.did(unit_rows(clock.now(sum_w_1), B))
    late = SmallScatter(clock, late_pack())
    early, late = early.result(), late.result()
    clock.did(late)

    sum_qkv = ring.swap(clock.now(sum_qkv).reshape(S, r, 3 * Dl))
    if whole_heads:
        sum_q, sum_k, sum_v = head_rows(sum_qkv, B)
    else:
        sum_q, sum_k, sum_v = (
            sum_qkv[:, :, c * Dl : (c + 1) * Dl].transpose(1, 0, 2).reshape(r, D) for c in range(3)
        )

    bo, g2, s2, b2 = (early[k * r : (k + 1) * r] for k in range(4))
    g1, s1, bq, bv = (late[k * r : (k + 1) * r] for k in range(4))
    wide = lambda v: v.astype(f32)
    return (
        output[-1], input_grad[-1], wide(sum_q), wide(sum_k), wide(sum_v), wide(sum_o),
        g1, s1, bq, bv, bo, sum_w_1, wide(sum_w_2), g2, s2, early[4 * r :], b2,
    )


def solution(mesh):
    tokens, rows, vector = P("batch", "seq", None), P(ALL, None), P(ALL)
    placed = (
        (tokens, tokens, P("batch"), P("batch"), P())
        + (rows,) * 4 + (vector,) * 5 + (rows,) * 2 + (vector,) * 4
    )
    out = (tokens, tokens) + (rows,) * 4 + (vector,) * 5 + (rows,) * 2 + (vector,) * 4
    return jax.shard_map(body, mesh=mesh, in_specs=placed, out_specs=out, check_vma=False)
```

time: 1140 us -> 826 us (0.72)
  Pallas kernels: 97.1 us -> 422 us
  waiting for transfers between devices: 481 us -> 211 us
  matrix products: 261 us -> 0 us
  other arithmetic: 75.6 us -> 20.4 us
  local copies, waits for them, and re-layouts: 86 us -> 39.3 us
  blocking collectives: 33.8 us -> 0 us
  starting transfers between devices: 82.8 us -> 106 us
    pallas_call x0 -> x32, Pallas kernels: none -> 326 us  [the longest x12 126 us: matmul(): pl.pallas_call(kernel, out_shape=tuple((jax.ShapeDtypeStruct((size, width...]
    dot_general x24 -> x0, matrix products: 261 us -> none  [the longest x8 95.5 us: dot_tn(): lax.dot_general(a, b, (((0,), (0,)), ((), ())), preferred_element_type=f32)]
    ppermute x69 -> x86, waiting for transfers between devices: 358 us -> 201 us  [the longest x76 190 us: send(): lax.ppermute(value, 'seq', [(self.order[i], self.order[(i + steps) % n])...]
    reduce_scatter x4, waiting for transfers between devices: 80.4 us -> 0.04 us  [body(): lax.psum_scatter(x, 'batch', scatter_dimension=0, tiled=True)]
    all_to_all x2 -> x0, blocking collectives: 33.8 us -> none  [body(): lax.all_to_all(x, 'seq', split_axis=0, concat_axis=0, tiled=True)]
    ppermute x69 -> x86, starting transfers between devices: 67.4 us -> 99.1 us  [the longest x76 83.1 us: send(): lax.ppermute(value, 'seq', [(self.order[i], self.order[(i + steps) % n])...]
    ppermute x5, waiting for transfers between devices: 36.5 us -> 9.86 us  [gather_small(): other = lax.ppermute(have, ALL, [(i, i ^ bit) for i in range(devices)])]
    unnamed x235 -> x172, local copies, waits for them, and re-layouts: 38.5 us -> 12.7 us
  transfers between devices with their start and end apart: 84 -> 99, of which waited for: 37 -> 45; matrix products, arithmetic and copies ran while one was open for 31% -> 5% of each run, Pallas kernels for 6% -> 48%
where the time goes in v2:
time: 826 us; the launch traced here: 815 us
  Pallas kernels  422 us (51%)
  waiting for transfers between devices  211 us (26%)
  starting transfers between devices  106 us (13%)
  local copies, waits for them, and re-layouts  39.3 us (5%)
  other arithmetic  20.4 us (2%)
  between operations  16.6 us (2%)
    ppermute x76, waiting for transfers between devices, send(): lax.ppermute(value, 'seq', [(self.order[i], self.order[(i + steps) % n])...  190 us
    pallas_call x12, Pallas kernels, matmul(): pl.pallas_call(kernel, out_shape=tuple((jax.ShapeDtypeStruct((size, width...  126 us
    ppermute x76, starting transfers between devices, send(): lax.ppermute(value, 'seq', [(self.order[i], self.order[(i + steps) % n])...  83.1 us
    pallas_call x4, Pallas kernels, weight_sum(): pl.pallas_call(kernel, out_shape=jax.ShapeDtypeStruct((rows, width), bf16...  78.3 us
    pallas_call x2, Pallas kernels, attend_back(): pl.pallas_call(partial(attend_back_kernel, blocks, rows), out_shape=jax.S...  63.2 us
    pallas_call x2, Pallas kernels, hidden_both(): pl.pallas_call(kernel, out_shape=(jax.ShapeDtypeStruct((rows, width), bf1...  38.1 us
    pallas_call x2, Pallas kernels, attend(): pl.pallas_call(partial(attend_kernel, blocks, rows), out_shape=(jax.Shape...  32.9 us
    pallas_call x2, Pallas kernels, project(): pl.pallas_call(kernel, out_shape=(jax.ShapeDtypeStruct((rows, depth), bf1...  28.1 us
  transfers between devices with their start and end apart: 99, of which 45 were waited for; matrix products, arithmetic and copies ran while one was open for 5% of the time, Pallas kernels for 48%

profile of v2, /device:TPU:0, one launch (start us, length us, event | category | flops | bytes accessed | tf_op | source)
XLA Modules:
  0.0 815.3 jit_solution(11850197086574466808)
XLA Ops:
  37.2 24.1 %collective-permute-done.5 = bf16[1,64,2048]{2,1,0:T(8,128)(2,1)S(1)} collective-permute-done((bf16[1,64,2048]{2,1,0:T(8,128)(2,1)S(1)}, bf16[1,64,2048]{2,1,0:T(8,128)(2,1)S(1)}, u32[]{:S(2)}, u32[]{:S(2)}) %collective-permute-start.5) | collective-permute-done | bytes 262176 | tf_op jit(solution)/shard_map/ppermute | solution.py:446
  102.2 14.0 %project.2 = (bf16[1024,2048]{1,0:T(8,128)(2,1)}, bf16[1024,1536]{1,0:T(8,128)(2,1)}) custom-call(bf16[256,2048]{1,0:T(8,128)(2,1)} %get-tuple-element.374.refs_0_, bf16[256,2048]{1,0:T(8,128)(2,1)} %collective-permute-done.4.refs_1_, bf16[128,2048]{1,0:T(8,128)(2,1)} %collective-permute-done.10.refs_2_, bf16[128,2048]{1,0:T(8,128)(2,1)} %collective-permute-done.11.refs_3_, ...), custom_call_target="tpu_custom_call" | custom-call | flops 8053063680 | bytes 25165824 | tf_op jit(solution)/shard_map/project/pallas_call | solution.py:171
  127.1 16.4 %attend.2 = (bf16[1024,512]{1,0:T(8,128)(2,1)}, f32[4,2,1024]{2,1,0:T(2,128)}) custom-call(s32[4]{0:T(128)} %subtract_and_fusion.steps, bf16[1024,1536]{1,0:T(8,128)(2,1)} %get-tuple-element.383.q_ref.k_ref.v_ref, bf16[1024,1536]{1,0:T(8,128)(2,1)} %get-tuple-element.383.q_ref.k_ref.v_ref, bf16[1024,1536]{1,0:T(8,128)(2,1)} %get-tuple-element.383.q_ref.k_ref.v_ref), custom_call_target="tpu_custom_call" | custom-call | flops 8589934592 | bytes 26843544 | tf_op jit(solution)/shard_map/attend/pallas_call | solution.py:603
  156.1 14.1 %project.3 = (bf16[1024,2048]{1,0:T(8,128)(2,1)}, bf16[1024,1536]{1,0:T(8,128)(2,1)}) custom-call(bf16[256,2048]{1,0:T(8,128)(2,1)} %get-tuple-element.400.refs_0_, bf16[256,2048]{1,0:T(8,128)(2,1)} %collective-permute-done.9.refs_1_, bf16[128,2048]{1,0:T(8,128)(2,1)} %copy-done.75, bf16[128,2048]{1,0:T(8,128)(2,1)} %copy-done.76, ...), custom_call_target="tpu_custom_call" | custom-call | flops 8053063680 | bytes 25165824 | tf_op jit(solution)/shard_map/project/pallas_call | solution.py:171
  182.1 16.5 %attend.3 = (bf16[1024,512]{1,0:T(8,128)(2,1)}, f32[4,2,1024]{2,1,0:T(2,128)}) custom-call(s32[4]{0:T(128)} %subtract_and_fusion.steps, bf16[1024,1536]{1,0:T(8,128)(2,1)} %get-tuple-element.410.q_ref.k_ref.v_ref, bf16[1024,1536]{1,0:T(8,128)(2,1)} %get-tuple-element.410.q_ref.k_ref.v_ref, bf16[1024,1536]{1,0:T(8,128)(2,1)} %get-tuple-element.410.q_ref.k_ref.v_ref), custom_call_target="tpu_custom_call" | custom-call | flops 8589934592 | bytes 26843544 | tf_op jit(solution)/shard_map/attend/pallas_call | solution.py:603
  222.1 26.1 %collective-permute-done.28.refs_4_ = bf16[128,2048]{1,0:T(8,128)(2,1)} collective-permute-done((bf16[128,2048]{1,0:T(8,128)(2,1)S(1)}, bf16[128,2048]{1,0:T(8,128)(2,1)}, u32[]{:S(2)}, u32[]{:S(2)}) %collective-permute-start.28) | collective-permute-done | bytes 524320 | tf_op jit(solution)/shard_map/ppermute | solution.py:446
  259.8 19.8 %collective-permute-done.31.refs_4_ = bf16[256,2048]{1,0:T(8,128)(2,1)} collective-permute-done((bf16[256,2048]{1,0:T(8,128)(2,1)}, bf16[256,2048]{1,0:T(8,128)(2,1)}, u32[]{:S(2)}, u32[]{:S(2)}) %collective-permute-start.31) | collective-permute-done | bytes 1048608 | tf_op jit(solution)/shard_map/ppermute | solution.py:446
  280.8 13.7 %matmul.14.refs_5_ = bf16[1024,2048]{1,0:T(8,128)(2,1)} custom-call(bf16[256,2048]{1,0:T(8,128)(2,1)} %copy-done.16, bf16[256,2048]{1,0:T(8,128)(2,1)} %copy-done.47, bf16[128,2048]{1,0:T(8,128)(2,1)} %copy-done.66, bf16[128,2048]{1,0:T(8,128)(2,1)} %collective-permute-done.22.refs_3_.refs_5_, bf16[256,2048]{1,0:T(8,128)(2,1)} %copy-done.46, ...), custom_call_target="tpu_custom_call" | custom-call | flops 7516192768 | bytes 23488102 | tf_op jit(solution)/shard_map/matmul/pallas_call | solution.py:89
  331.3 19.0 %hidden_both.2 = (bf16[1024,2048]{1,0:T(8,128)(2,1)}, bf16[1024,2048]{1,0:T(8,128)(2,1)}, f32[1,2048]{1,0:T(1,128)}) custom-call(bf16[256,2048]{1,0:T(8,128)(2,1)} %get-tuple-element.539.refs_0_, bf16[256,2048]{1,0:T(8,128)(2,1)} %collective-permute-done.32.refs_1_, bf16[128,2048]{1,0:T(8,128)(2,1)} %collective-permute-done.35.refs_2_, ...), custom_call_target="tpu_custom_call" | custom-call | flops 10737418240 | bytes 33554432 | tf_op jit(solution)/shard_map/hidden_both/pallas_call | solution.py:203
  361.0 13.7 %matmul.15.refs_5_ = bf16[1024,2048]{1,0:T(8,128)(2,1)} custom-call(bf16[256,2048]{1,0:T(8,128)(2,1)} %copy-done.15, bf16[256,2048]{1,0:T(8,128)(2,1)} %collective-permute-done.38.refs_1_.refs_8_, bf16[128,2048]{1,0:T(8,128)(2,1)} %copy-done.71, bf16[128,2048]{1,0:T(8,128)(2,1)} %copy-done.72, bf16[256,2048]{1,0:T(8,128)(2,1)} %collective-permute-done.37.refs_4_.refs_11_, ...), custom_call_target="tpu_custom_call" | custom-call | flops 7516192768 | bytes 23488102 | tf_op jit(solution)/shard_map/matmul/pallas_call | solution.py:89
  374.6 13.2 %matmul.16 = (bf16[256,2048]{1,0:T(8,128)(2,1)}, bf16[256,2048]{1,0:T(8,128)(2,1)}, bf16[256,2048]{1,0:T(8,128)(2,1)}, bf16[128,2048]{1,0:T(8,128)(2,1)}, bf16[128,2048]{1,0:T(8,128)(2,1)}) custom-call(bf16[1024,2048]{1,0:T(8,128)(2,1)} %get-tuple-element.495.refs_0_.refs_10_, bf16[2048,2048]{1,0:T(8,128)(2,1)} %all-gather.11.cloned.1.call-done.refs_6_.refs_1_), custom_call_target="tpu_custom_call" | custom-call | flops 7516192768 | bytes 23488102 | tf_op jit(solution)/shard_map/matmul/pallas_call | solution.py:89
  391.0 19.1 %hidden_both.3 = (bf16[1024,2048]{1,0:T(8,128)(2,1)}, bf16[1024,2048]{1,0:T(8,128)(2,1)}, f32[1,2048]{1,0:T(1,128)}) custom-call(bf16[256,2048]{1,0:T(8,128)(2,1)} %get-tuple-element.544.refs_0_.refs_5_, bf16[256,2048]{1,0:T(8,128)(2,1)} %collective-permute-done.34.refs_1_.refs_6_, bf16[128,2048]{1,0:T(8,128)(2,1)} %copy-done.69, ...), custom_call_target="tpu_custom_call" | custom-call | flops 10737418240 | bytes 33554432 | tf_op jit(solution)/shard_map/hidden_both/pallas_call | solution.py:203
  410.4 24.8 %weight_sum.4 = bf16[2048,2048]{1,0:T(8,128)(2,1)} custom-call(bf16[1024,2048]{1,0:T(8,128)(2,1)} %get-tuple-element.553.refs_0_, bf16[1024,2048]{1,0:T(8,128)(2,1)} %get-tuple-element.598.refs_1_.refs_0_, bf16[256,2048]{1,0:T(8,128)(2,1)} %copy-done.16, bf16[256,2048]{1,0:T(8,128)(2,1)} %copy-done.47, bf16[128,2048]{1,0:T(8,128)(2,1)} %copy-done.66, ...), custom_call_target="tpu_custom_call" | custom-call | flops 14173391872 | bytes 44291848 | tf_op jit(solution)/shard_map/weight_sum/pallas_call | solution.py:127
  458.7 13.2 %matmul.17 = (bf16[256,2048]{1,0:T(8,128)(2,1)}, bf16[256,2048]{1,0:T(8,128)(2,1)}, bf16[256,2048]{1,0:T(8,128)(2,1)}, bf16[128,2048]{1,0:T(8,128)(2,1)}, bf16[128,2048]{1,0:T(8,128)(2,1)}) custom-call(bf16[1024,2048]{1,0:T(8,128)(2,1)} %get-tuple-element.533.refs_0_.refs_11_, bf16[2048,2048]{1,0:T(8,128)(2,1)} %all-gather.11.cloned.1.call-done.refs_6_.refs_1_), custom_call_target="tpu_custom_call" | custom-call | flops 7516192768 | bytes 23488102 | tf_op jit(solution)/shard_map/matmul/pallas_call | solution.py:89
  474.0 24.5 %weight_sum.5 = bf16[2048,2048]{1,0:T(8,128)(2,1)} custom-call(bf16[256,2048]{1,0:T(8,128)(2,1)} %get-tuple-element.539.refs_0_, bf16[256,2048]{1,0:T(8,128)(2,1)} %collective-permute-done.32.refs_1_, bf16[128,2048]{1,0:T(8,128)(2,1)} %collective-permute-done.35.refs_2_, bf16[128,2048]{1,0:T(8,128)(2,1)} %collective-permute-done.36.refs_3_, ...), custom_call_target="tpu_custom_call" | custom-call | flops 14173391872 | bytes 44291848 | tf_op jit(solution)/shard_map/weight_sum/pallas_call | solution.py:127
  505.6 13.2 %matmul.18 = (bf16[256,2048]{1,0:T(8,128)(2,1)}, bf16[256,2048]{1,0:T(8,128)(2,1)}, bf16[256,2048]{1,0:T(8,128)(2,1)}, bf16[128,2048]{1,0:T(8,128)(2,1)}, bf16[128,2048]{1,0:T(8,128)(2,1)}) custom-call(bf16[1024,2048]{1,0:T(8,128)(2,1)} %get-tuple-element.553.refs_0_, bf16[2048,2048]{1,0:T(8,128)(2,1)} %all-gather.9.cloned.1.call-done.refs_5_.refs_1_), custom_call_target="tpu_custom_call" | custom-call | flops 7516192768 | bytes 23488102 | tf_op jit(solution)/shard_map/matmul/pallas_call | solution.py:89
  543.8 31.6 %attend_back.2.refs_0_.refs_2_ = bf16[1024,1536]{1,0:T(8,128)(2,1)} custom-call(s32[4]{0:T(128)} %subtract_and_fusion.steps, bf16[1024,1536]{1,0:T(8,128)(2,1)} %get-tuple-element.383.q_ref.k_ref.v_ref, bf16[1024,1536]{1,0:T(8,128)(2,1)} %get-tuple-element.383.q_ref.k_ref.v_ref, bf16[1024,1536]{1,0:T(8,128)(2,1)} %get-tuple-element.383.q_ref.k_ref.v_ref, ...), custom_call_target="tpu_custom_call" | custom-call | flops 17179869184 | bytes 53687092 | tf_op jit(solution)/shard_map/attend_back/pallas_call | solution.py:678
  587.9 10.7 %matmul.20 = (bf16[256,2048]{1,0:T(8,128)(2,1)}, bf16[256,2048]{1,0:T(8,128)(2,1)}, bf16[256,2048]{1,0:T(8,128)(2,1)}, bf16[128,2048]{1,0:T(8,128)(2,1)}, bf16[128,2048]{1,0:T(8,128)(2,1)}) custom-call(bf16[1024,1536]{1,0:T(8,128)(2,1)} %attend_back.2.refs_0_.refs_2_, bf16[2048,1536]{1,0:T(8,128)(2,1)} %all-gather.5.cloned.1.call-done.refs_7_.refs_1_), custom_call_target="tpu_custom_call" | custom-call | flops 5637144576 | bytes 17616076 | tf_op jit(solution)/shard_map/matmul/pallas_call | solution.py:89
  600.7 13.3 %matmul.21 = (bf16[256,2048]{1,0:T(8,128)(2,1)}, bf16[256,2048]{1,0:T(8,128)(2,1)}, bf16[256,2048]{1,0:T(8,128)(2,1)}, bf16[128,2048]{1,0:T(8,128)(2,1)}, bf16[128,2048]{1,0:T(8,128)(2,1)}) custom-call(bf16[1024,2048]{1,0:T(8,128)(2,1)} %get-tuple-element.598.refs_1_.refs_0_, bf16[2048,2048]{1,0:T(8,128)(2,1)} %all-gather.9.cloned.1.call-done.refs_5_.refs_1_), custom_call_target="tpu_custom_call" | custom-call | flops 7516192768 | bytes 23488102 | tf_op jit(solution)/shard_map/matmul/pallas_call | solution.py:89
  627.0 10.1 %weight_sum.6 = bf16[512,2048]{1,0:T(8,128)(2,1)} custom-call(bf16[1024,512]{1,0:T(8,128)(2,1)} %get-tuple-element.622.refs_0_, bf16[1024,512]{1,0:T(8,128)(2,1)} %get-tuple-element.623.refs_0_.refs_1_, bf16[256,2048]{1,0:T(8,128)(2,1)} %get-tuple-element.566.refs_0_.refs_2_, bf16[256,2048]{1,0:T(8,128)(2,1)} %copy-done.4, bf16[128,2048]{1,0:T(8,128)(2,1)} %copy-done.18, ...), custom_call_target="tpu_custom_call" | custom-call | flops 3543347968 | bytes 11072962 | tf_op jit(solution)/shard_map/weight_sum/pallas_call | solution.py:127
  641.4 31.6 %attend_back.3.refs_0_.refs_3_ = bf16[1024,1536]{1,0:T(8,128)(2,1)} custom-call(s32[4]{0:T(128)} %subtract_and_fusion.steps, bf16[1024,1536]{1,0:T(8,128)(2,1)} %get-tuple-element.410.q_ref.k_ref.v_ref, bf16[1024,1536]{1,0:T(8,128)(2,1)} %get-tuple-element.410.q_ref.k_ref.v_ref, bf16[1024,1536]{1,0:T(8,128)(2,1)} %get-tuple-element.410.q_ref.k_ref.v_ref, ...), custom_call_target="tpu_custom_call" | custom-call | flops 17179869184 | bytes 53687092 | tf_op jit(solution)/shard_map/attend_back/pallas_call | solution.py:678
  675.1 10.6 %matmul.23 = (bf16[256,2048]{1,0:T(8,128)(2,1)}, bf16[256,2048]{1,0:T(8,128)(2,1)}, bf16[256,2048]{1,0:T(8,128)(2,1)}, bf16[128,2048]{1,0:T(8,128)(2,1)}, bf16[128,2048]{1,0:T(8,128)(2,1)}) custom-call(bf16[1024,1536]{1,0:T(8,128)(2,1)} %attend_back.3.refs_0_.refs_3_, bf16[2048,1536]{1,0:T(8,128)(2,1)} %all-gather.5.cloned.1.call-done.refs_7_.refs_1_), custom_call_target="tpu_custom_call" | custom-call | flops 5637144576 | bytes 17616076 | tf_op jit(solution)/shard_map/matmul/pallas_call | solution.py:89
  685.8 18.9 %weight_sum.7 = bf16[2048,1536]{1,0:T(8,128)(2,1)} custom-call(bf16[1024,2048]{1,0:T(8,128)(2,1)} %get-tuple-element.635.refs_0_, bf16[1024,2048]{1,0:T(8,128)(2,1)} %get-tuple-element.636.refs_1_, bf16[1024,1536]{1,0:T(8,128)(2,1)} %attend_back.2.refs_0_.refs_2_, bf16[1024,1536]{1,0:T(8,128)(2,1)} %attend_back.3.refs_0_.refs_3_), custom_call_target="tpu_custom_call" | custom-call | flops 10630043648 | bytes 33218888 | tf_op jit(solution)/shard_map/weight_sum/pallas_call | solution.py:127
  713.2 11.7 %collective-permute-done.73.refs_1_ = bf16[256,2048]{1,0:T(8,128)(2,1)} collective-permute-done((bf16[256,2048]{1,0:T(8,128)(2,1)}, bf16[256,2048]{1,0:T(8,128)(2,1)}, u32[]{:S(2)}, u32[]{:S(2)}) %collective-permute-start.73) | collective-permute-done | bytes 1048608 | tf_op jit(solution)/shard_map/ppermute | solution.py:446
  (527 shorter events, 375.0 us)
Async XLA Ops:
  7.2 95.0 %all-gather.5.cloned.1.call-start = ((), (), s32[]{:S(2)}) async-start(), calls=%async_computation.4 | async-start | bytes 7077888 | tf_op jit(solution)/shard_map/all_gather | solution.py:720
  27.1 117.4 %all-gather.7.cloned.1.call-start = ((), (), s32[]{:S(2)}) async-start(), calls=%async_computation.5 | async-start | bytes 2359296 | tf_op jit(solution)/shard_map/all_gather | solution.py:720
  70.8 210.0 %all-gather.9.cloned.1.call-start = ((), (), s32[]{:S(2)}) async-start(), calls=%async_computation.6 | async-start | bytes 9437184 | tf_op jit(solution)/shard_map/all_gather | solution.py:720
  124.5 206.8 %all-gather.11.cloned.1.call-start = ((), (), s32[]{:S(2)}) async-start(), calls=%async_computation.7 | async-start | bytes 9437184 | tf_op jit(solution)/shard_map/all_gather | solution.py:720
  150.5 384.1 %reduce-scatter.5.cloned.1.call-start = ((), (), s32[]{:S(2)}) async-start(), calls=%async_computation.8 | async-start | bytes 9437184 | tf_op jit(solution)/shard_map/reduce_scatter | solution.py:721
  154.1 46.5 %collective-permute-start.23 = (bf16[256,2048]{1,0:T(8,128)(2,1)}, bf16[256,2048]{1,0:T(8,128)(2,1)S(1)}, u32[]{:S(2)}, u32[]{:S(2)}) collective-permute-start(bf16[256,2048]{1,0:T(8,128)(2,1)} %get-tuple-element.391), channel_id=1, source_target_pairs={{0,1},{1,3},{3,2},{2,0},{4,5},{5,7},{7,6},{6,4},{8,9},{9,11},{11,1... | collective-permute-start | bytes 3145736 | tf_op jit(solution)/shard_map/ppermute | solution.py:446
  155.8 46.5 %collective-permute-start.24 = (bf16[256,2048]{1,0:T(8,128)(2,1)}, bf16[256,2048]{1,0:T(8,128)(2,1)S(1)}, u32[]{:S(2)}, u32[]{:S(2)}) collective-permute-start(bf16[256,2048]{1,0:T(8,128)(2,1)} %get-tuple-element.392), channel_id=1, source_target_pairs={{0,2},{1,0},{3,1},{2,3},{4,6},{5,4},{7,5},{6,7},{8,10},{9,8},{11,9... | collective-permute-start | bytes 3145736 | tf_op jit(solution)/shard_map/ppermute | solution.py:446
  215.1 40.9 %collective-permute-start.25 = (bf16[256,2048]{1,0:T(8,128)(2,1)}, bf16[256,2048]{1,0:T(8,128)(2,1)S(1)}, u32[]{:S(2)}, u32[]{:S(2)}) collective-permute-start(bf16[256,2048]{1,0:T(8,128)(2,1)} %get-tuple-element.419), channel_id=1, source_target_pairs={{0,1},{1,3},{3,2},{2,0},{4,5},{5,7},{7,6},{6,4},{8,9},{9,11},{11,1... | collective-permute-start | bytes 3145736 | tf_op jit(solution)/shard_map/ppermute | solution.py:446
  215.8 41.5 %collective-permute-start.26 = (bf16[256,2048]{1,0:T(8,128)(2,1)}, bf16[256,2048]{1,0:T(8,128)(2,1)}, u32[]{:S(2)}, u32[]{:S(2)}) collective-permute-start(bf16[256,2048]{1,0:T(8,128)(2,1)} %get-tuple-element.420), channel_id=1, source_target_pairs={{0,2},{1,0},{3,1},{2,3},{4,6},{5,4},{7,5},{6,7},{8,10},{9,8},{11,9... | collective-permute-start | bytes 3145736 | tf_op jit(solution)/shard_map/ppermute | solution.py:446
  254.0 73.1 %collective-permute-start.37 = (bf16[256,2048]{1,0:T(8,128)(2,1)S(1)}, bf16[256,2048]{1,0:T(8,128)(2,1)}, u32[]{:S(2)}, u32[]{:S(2)}) collective-permute-start(bf16[256,2048]{1,0:T(8,128)(2,1)S(1)} %get-tuple-element.490.refs_0_.refs_7_), channel_id=1, source_target_pairs={{0,1},{1,3},{3,2},{2,0},{4,5},{5,7},{7,6},{6,4},{8,9},{9,11},{11,1... | collective-permute-start | bytes 3145736 | tf_op jit(solution)/shard_map/ppermute | solution.py:446
  255.2 71.9 %collective-permute-start.38 = (bf16[256,2048]{1,0:T(8,128)(2,1)S(1)}, bf16[256,2048]{1,0:T(8,128)(2,1)}, u32[]{:S(2)}, u32[]{:S(2)}) collective-permute-start(bf16[256,2048]{1,0:T(8,128)(2,1)S(1)} %get-tuple-element.490.refs_0_.refs_7_), channel_id=1, source_target_pairs={{0,2},{1,0},{3,1},{2,3},{4,6},{5,4},{7,5},{6,7},{8,10},{9,8},{11,9... | collective-permute-start | bytes 3145736 | tf_op jit(solution)/shard_map/ppermute | solution.py:446
  256.0 46.7 %collective-permute-start.32 = (bf16[256,2048]{1,0:T(8,128)(2,1)}, bf16[256,2048]{1,0:T(8,128)(2,1)}, u32[]{:S(2)}, u32[]{:S(2)}) collective-permute-start(bf16[256,2048]{1,0:T(8,128)(2,1)} %get-tuple-element.539.refs_0_), channel_id=1, source_target_pairs={{0,2},{1,0},{3,1},{2,3},{4,6},{5,4},{7,5},{6,7},{8,10},{9,8},{11,9... | collective-permute-start | bytes 3145736 | tf_op jit(solution)/shard_map/ppermute | solution.py:446
  258.5 53.8 %collective-permute-start.30 = (bf16[128,2048]{1,0:T(8,128)(2,1)S(1)}, bf16[128,2048]{1,0:T(8,128)(2,1)}, u32[]{:S(2)}, u32[]{:S(2)}) collective-permute-start(bf16[128,2048]{1,0:T(8,128)(2,1)S(1)} %add_convert_fusion.12), channel_id=1, source_target_pairs={{0,2},{1,0},{3,1},{2,3},{4,6},{5,4},{7,5},{6,7},{8,10},{9,8},{11,9... | collective-permute-start | bytes 1572872 | tf_op jit(solution)/shard_map/ppermute | solution.py:446
  435.3 201.8 %reduce-scatter.7.cloned.1.call-start = ((), (), s32[]{:S(2)}) async-start(), calls=%async_computation.9 | async-start | bytes 9437184 | tf_op jit(solution)/shard_map/reduce_scatter | solution.py:721
  456.2 42.3 %collective-permute-start.47 = (bf16[256,2048]{1,0:T(8,128)(2,1)}, bf16[256,2048]{1,0:T(8,128)(2,1)S(1)}, u32[]{:S(2)}, u32[]{:S(2)}) collective-permute-start(bf16[256,2048]{1,0:T(8,128)(2,1)} %get-tuple-element.566.refs_0_.refs_2_), channel_id=1, source_target_pairs={{0,1},{1,3},{3,2},{2,0},{4,5},{5,7},{7,6},{6,4},{8,9},{9,11},{11,1... | collective-permute-start | bytes 3145736 | tf_op jit(solution)/shard_map/ppermute | solution.py:446
  458.7 39.8 %collective-permute-start.48 = (bf16[256,2048]{1,0:T(8,128)(2,1)}, bf16[256,2048]{1,0:T(8,128)(2,1)S(1)}, u32[]{:S(2)}, u32[]{:S(2)}) collective-permute-start(bf16[256,2048]{1,0:T(8,128)(2,1)} %get-tuple-element.566.refs_0_.refs_2_), channel_id=1, source_target_pairs={{0,2},{1,0},{3,1},{2,3},{4,6},{5,4},{7,5},{6,7},{8,10},{9,8},{11,9... | collective-permute-start | bytes 3145736 | tf_op jit(solution)/shard_map/ppermute | solution.py:446
  534.6 170.0 %reduce-scatter.9.cloned.1.call-start = ((), (), s32[]{:S(2)}) async-start(), calls=%async_computation.10 | async-start | bytes 2359296 | tf_op jit(solution)/shard_map/reduce_scatter | solution.py:721
  535.3 48.1 %collective-permute-start.55 = (bf16[256,2048]{1,0:T(8,128)(2,1)}, bf16[256,2048]{1,0:T(8,128)(2,1)}, u32[]{:S(2)}, u32[]{:S(2)}) collective-permute-start(bf16[256,2048]{1,0:T(8,128)(2,1)} %get-tuple-element.555), channel_id=1, source_target_pairs={{0,1},{1,3},{3,2},{2,0},{4,5},{5,7},{7,6},{6,4},{8,9},{9,11},{11,1... | collective-permute-start | bytes 3145736 | tf_op jit(solution)/shard_map/ppermute | solution.py:446
  537.3 46.1 %collective-permute-start.56 = (bf16[256,2048]{1,0:T(8,128)(2,1)}, bf16[256,2048]{1,0:T(8,128)(2,1)}, u32[]{:S(2)}, u32[]{:S(2)}) collective-permute-start(bf16[256,2048]{1,0:T(8,128)(2,1)} %get-tuple-element.556), channel_id=1, source_target_pairs={{0,2},{1,0},{3,1},{2,3},{4,6},{5,4},{7,5},{6,7},{8,10},{9,8},{11,9... | collective-permute-start | bytes 3145736 | tf_op jit(solution)/shard_map/ppermute | solution.py:446
  537.4 43.3 %collective-permute-start.57 = (bf16[256,2048]{1,0:T(8,128)(2,1)S(1)}, bf16[256,2048]{1,0:T(8,128)(2,1)S(1)}, u32[]{:S(2)}, u32[]{:S(2)}) collective-permute-start(bf16[256,2048]{1,0:T(8,128)(2,1)S(1)} %copy-done.10), channel_id=1, source_target_pairs={{0,1},{1,3},{3,2},{2,0},{4,5},{5,7},{7,6},{6,4},{8,9},{9,11},{11,1... | collective-permute-start | bytes 3145736 | tf_op jit(solution)/shard_map/ppermute | solution.py:446
  539.3 41.5 %collective-permute-start.58 = (bf16[256,2048]{1,0:T(8,128)(2,1)S(1)}, bf16[256,2048]{1,0:T(8,128)(2,1)S(1)}, u32[]{:S(2)}, u32[]{:S(2)}) collective-permute-start(bf16[256,2048]{1,0:T(8,128)(2,1)S(1)} %copy-done.10), channel_id=1, source_target_pairs={{0,2},{1,0},{3,1},{2,3},{4,6},{5,4},{7,5},{6,7},{8,10},{9,8},{11,9... | collective-permute-start | bytes 3145736 | tf_op jit(solution)/shard_map/ppermute | solution.py:446
  540.0 48.0 %collective-permute-start.59 = (f32[16,512]{1,0:T(8,128)S(1)}, f32[16,512]{1,0:T(8,128)S(1)}, u32[]{:S(2)}, u32[]{:S(2)}) collective-permute-start(f32[16,512]{1,0:T(8,128)S(1)} %get-tuple-element.729), channel_id=1, source_target_pairs={{0,16},{1,17},{2,18},{3,19},{4,20},{5,21},{6,22},{7,23},{8,24},{9,... | collective-permute-start | bytes 98312 | tf_op jit(solution)/shard_map/ppermute | solution.py:554
  585.8 39.9 %collective-permute-start.65 = (bf16[128,2048]{1,0:T(8,128)(2,1)S(1)}, bf16[128,2048]{1,0:T(8,128)(2,1)}, u32[]{:S(2)}, u32[]{:S(2)}) collective-permute-start(bf16[128,2048]{1,0:T(8,128)(2,1)S(1)} %add_convert_fusion.6), channel_id=1, source_target_pairs={{0,2},{1,0},{3,1},{2,3},{4,6},{5,4},{7,5},{6,7},{8,10},{9,8},{11,9... | collective-permute-start | bytes 1572872 | tf_op jit(solution)/shard_map/ppermute | solution.py:446
  637.1 154.5 %reduce-scatter.11.cloned.1.call-start = ((), (), s32[]{:S(2)}) async-start(), calls=%async_computation.11 | async-start | bytes 7077888 | tf_op jit(solution)/shard_map/reduce_scatter | solution.py:721
  (160 other events, 2902.1 us)
Sparse Core Ops, SparseCore 0:
  27.2 66.3 all-gather.4
  95.2 27.4 all-gather.6
  124.7 82.9 all-gather.8
  209.1 80.5 all-gather.10
  435.4 93.4 reduce-scatter.4
  534.7 93.5 reduce-scatter.6
  637.2 33.5 reduce-scatter.8
  704.8 67.9 reduce-scatter.10

commit v3 on v2

--- a/solution.py
+++ b/solution.py
@@ -793,22 +793,16 @@
             return lax.dynamic_update_slice(spread, v.reshape(B, 1, r), (0, s, 0)).reshape(devices, r)
         return lax.dynamic_update_slice(jnp.zeros((D,), f32), v, (s * Dl,)).reshape(devices, r)
 
-    def early_pack():
+    def small_pack():
         own_hidden = lax.dynamic_update_slice(
             jnp.zeros((B, S, rw), f32), sum(sum_pre).reshape(B, 1, rw), (0, s, 0)
         ).reshape(devices, rw)
         parts = (
-            pair_sum(sums_two, 2), pair_sum(sums_two, 0), pair_sum(sums_two, 1), pair_sum(sums_two, 3), own_hidden,
+            pair_sum(sums_two, 2), pair_sum(sums_two, 0), pair_sum(sums_two, 1), pair_sum(sums_two, 3),
+            own_heads(bias_sums[:Dl]), own_heads(bias_sums[2 * Dl :]), own_hidden,
         )
-        return jnp.concatenate(parts, -1)
-
-    def late_pack():
-        bias_sums = tokens(grad_qkv)
-        parts = (
-            pair_sum(sums_one, 0), pair_sum(sums_one, 1), own_heads(bias_sums[:Dl]),
-            own_heads(bias_sums[2 * Dl :]),
-        )
-        return jnp.concatenate(parts, -1)
+        last = pair_sum(sums_one, 0), pair_sum(sums_one, 1)
+        return jnp.concatenate(last + parts, -1)
 
     fresh = lambda: [None] * slots
     normed, qkv, context, lse, middle, normed_two, sums_one, sums_two = (fresh() for _ in range(8))
@@ -828,7 +822,6 @@
     else:
         w_o = lax.all_gather(clock.now(wo), ALL, axis=0, tiled=True)
         w_o = lax.dynamic_slice(w_o, (s * Dl, 0), (Dl, D))
-    in1 = bring(inputs[1])
 
     small = (gain_one, shift_one, bias_q, bias_v, bias_o, gain_two, shift_two, bias_out)
     packed = clock.did(gather_small(clock.now(jnp.concatenate(small + (bias_in,))), devices))
@@ -845,10 +838,11 @@
         .reshape(1, Fl).astype(f32)
     )
 
+    w_2 = gather(clock.now(w_out))
     in0.arrive()
+    in1 = bring(inputs[1])
     start_layer(0, in0.result())
     in1.go()
-    w_2 = gather(clock.now(w_out))
     cot0 = bring(grad_two[0])
     attention(0)
     in1.arrive()
@@ -858,32 +852,34 @@
     cot0.go()
     attention(1)
     br0.go()
-    cot0.arrive()
-    cot1 = bring(grad_two[1])
-    br1 = begin(branch_out(1))
+    part = branch_out(1)
     br0.arrive()
     nt0 = bring(middle_of(0, br0.result()))
-    br1.go()
+    br1 = begin(part)
+    cot0.arrive()
     grad_branch_two[0] = cot0.result()
     hidden_back(0)
     nt0.go()
+    br1.go()
+    cot1 = bring(grad_two[1])
+    nt0.arrive()
     br1.arrive()
     nt1 = bring(middle_of(1, br1.result()))
-    nt0.arrive()
-    cot1.go()
     normed_two[0] = nt0.result()
     hidden_units(0)
+    cot1.go()
     nt1.go()
+    gn0 = begin(normed_two_back(0))
     cot1.arrive()
     grad_branch_two[1] = cot1.result()
     hidden_back(1)
-    gn0 = begin(normed_two_back(0))
     nt1.arrive()
     normed_two[1] = nt1.result()
     hidden_units(1)
     gn0.go()
     sum_w_2 = gradient(hidden, grad_branch_two)
     sum_w_2 = scatter(sum_w_2)
+    part = branch_two_out(0)
     gn0.arrive()
     middle_back(0, gn0.result())
     gb0 = bring(own_grad_branch[0])
@@ -891,7 +887,7 @@
     sum_w_1 = gradient(normed_two, grad_pre)
     gb0.go()
     gn1.go()
-    part = branch_two_out(0)
+    part_one = branch_two_out(1)
     gb0.arrive()
     out0 = begin(part)
     grad_branch[0] = gb0.result()
@@ -899,49 +895,46 @@
     gn1.arrive()
     middle_back(1, gn1.result())
     gb1 = bring(own_grad_branch[1])
-    early = SmallScatter(clock, early_pack())
-    early.step()
     sum_w_1 = scatter(after(clock.now(sum_w_1), sum_w_2))
     attention_back(0)
     gb1.go()
-    out0.go()
-    early.step()
-    gx0 = begin(normed_back(0))
-    part = branch_two_out(1)
+    part = normed_back(0)
     gb1.arrive()
+    gx0 = begin(part)
     grad_branch[1] = gb1.result()
     context_back(1)
+    out0.go()
+    sum_o = gradient(context, grad_branch)
     out0.arrive()
     gx0.go()
-    early.step()
-    sum_o = gradient(context, grad_branch)
-    if whole_heads:
-        sum_o = scatter(after(clock.now(sum_o), sum_w_1))
-    else:
-        sum_o = lax.dynamic_update_slice(jnp.zeros((D, D), bf16), sum_o, (s * Dl, 0))
-        sum_o = lax.psum_scatter(sum_o, ALL, scatter_dimension=0, tiled=True)
-    out1 = begin(part)
+    out1 = begin(part_one)
     attention_back(1)
     gx0.arrive()
     out1.go()
-    gx1 = begin(normed_back(1))
     sum_qkv = gradient(normed, grad_qkv)
-    sum_qkv = scatter(after(clock.now(sum_qkv), sum_o))
+    sum_qkv = scatter(after(clock.now(sum_qkv), sum_w_1))
+    part = normed_back(1)
+    out1.arrive()
+    gx1 = begin(part)
+    finish(0, out0.result())
+    start_back(0, gx0.result())
+    finish(1, out1.result())
+    bias_sums = clock.did(tokens(clock.now(grad_qkv)))
     gx1.go()
-    early.step()
-    start_back(0, gx0.result())
-    finish(0, out0.result())
-    out1.arrive()
-    finish(1, out1.result())
     sum_w_1 = ring.swap(clock.now(sum_w_1).reshape(S, r, Fl))
     gx1.arrive()
     start_back(1, gx1.result())
     sum_w_1 = clock.did(unit_rows(clock.now(sum_w_1), B))
-    late = SmallScatter(clock, late_pack())
-    early, late = early.result(), late.result()
-    clock.did(late)
-
+    sums = SmallScatter(clock, small_pack())
+    for _ in range(3):
+        sums.step()
+    if whole_heads:
+        sum_o = scatter(after(clock.now(sum_o), sum_qkv))
+    else:
+        sum_o = lax.dynamic_update_slice(jnp.zeros((D, D), bf16), sum_o, (s * Dl, 0))
+        sum_o = lax.psum_scatter(after(clock.now(sum_o), sum_qkv), ALL, scatter_dimension=0, tiled=True)
     sum_qkv = ring.swap(clock.now(sum_qkv).reshape(S, r, 3 * Dl))
+    sums = sums.result()
     if whole_heads:
         sum_q, sum_k, sum_v = head_rows(sum_qkv, B)
     else:
@@ -949,12 +942,11 @@
             sum_qkv[:, :, c * Dl : (c + 1) * Dl].transpose(1, 0, 2).reshape(r, D) for c in range(3)
         )
 
-    bo, g2, s2, b2 = (early[k * r : (k + 1) * r] for k in range(4))
-    g1, s1, bq, bv = (late[k * r : (k + 1) * r] for k in range(4))
+    g1, s1, bo, g2, s2, b2, bq, bv = (sums[k * r : (k + 1) * r] for k in range(8))
     wide = lambda v: v.astype(f32)
     return (
         output[-1], input_grad[-1], wide(sum_q), wide(sum_k), wide(sum_v), wide(sum_o),
-        g1, s1, bq, bv, bo, sum_w_1, wide(sum_w_2), g2, s2, early[4 * r :], b2,
+        g1, s1, bq, bv, bo, sum_w_1, wide(sum_w_2), g2, s2, sums[8 * r :], b2,
     )
 
 

time: 826 us -> 805 us (0.975)
  starting transfers between devices: 106 us -> 92.7 us
    ppermute x76, waiting for transfers between devices: 190 us -> 167 us  [send(): lax.ppermute(value, 'seq', [(self.order[i], self.order[(i + steps) % n])...]
    ppermute x10 -> x5, starting transfers between devices: 16 us -> 4.14 us  [step(): lax.ppermute(send, ALL, [(i, i ^ bit) for i in range(self.devices)])]
    reduce_scatter x4, waiting for transfers between devices: 0.04 us -> 10.5 us  [body(): lax.psum_scatter(x, 'batch', scatter_dimension=0, tiled=True)]
  transfers between devices with their start and end apart: 99 -> 94, of which waited for: 45 -> 45; matrix products, arithmetic and copies ran while one was open for 5% -> 5% of each run, Pallas kernels for 48% -> 50%
where the time goes in v3:
time: 805 us; the launch traced here: 795 us
  Pallas kernels  425 us (53%)
  waiting for transfers between devices  204 us (25%)
  starting transfers between devices  92.7 us (12%)
  local copies, waits for them, and re-layouts  34.5 us (4%)
  other arithmetic  21.8 us (3%)
  between operations  16.6 us (2%)
    ppermute x76, waiting for transfers between devices, send(): lax.ppermute(value, 'seq', [(self.order[i], self.order[(i + steps) % n])...  167 us
    pallas_call x12, Pallas kernels, matmul(): pl.pallas_call(kernel, out_shape=tuple((jax.ShapeDtypeStruct((size, width...  127 us
    ppermute x76, starting transfers between devices, send(): lax.ppermute(value, 'seq', [(self.order[i], self.order[(i + steps) % n])...  82 us
    pallas_call x4, Pallas kernels, weight_sum(): pl.pallas_call(kernel, out_shape=jax.ShapeDtypeStruct((rows, width), bf16...  78.3 us
    pallas_call x2, Pallas kernels, attend_back(): pl.pallas_call(partial(attend_back_kernel, blocks, rows), out_shape=jax.S...  63.1 us
    pallas_call x2, Pallas kernels, hidden_both(): pl.pallas_call(kernel, out_shape=(jax.ShapeDtypeStruct((rows, width), bf1...  38 us
    pallas_call x2, Pallas kernels, attend(): pl.pallas_call(partial(attend_kernel, blocks, rows), out_shape=(jax.Shape...  33 us
    pallas_call x2, Pallas kernels, project(): pl.pallas_call(kernel, out_shape=(jax.ShapeDtypeStruct((rows, depth), bf1...  28.1 us
  transfers between devices with their start and end apart: 94, of which 45 were waited for; matrix products, arithmetic and copies ran while one was open for 5% of the time, Pallas kernels for 50%

profile of v3, /device:TPU:0, one launch (start us, length us, event | category | flops | bytes accessed | tf_op | source)
XLA Modules:
  0.0 794.6 jit_solution(7115223344493825285)
XLA Ops:
  37.2 24.1 %collective-permute-done.5 = bf16[1,64,2048]{2,1,0:T(8,128)(2,1)S(1)} collective-permute-done((bf16[1,64,2048]{2,1,0:T(8,128)(2,1)S(1)}, bf16[1,64,2048]{2,1,0:T(8,128)(2,1)S(1)}, u32[]{:S(2)}, u32[]{:S(2)}) %collective-permute-start.5) | collective-permute-done | bytes 262176 | tf_op jit(solution)/shard_map/ppermute | solution.py:446
  93.9 11.3 %collective-permute-done.8.refs_2_ = bf16[128,2048]{1,0:T(8,128)(2,1)} collective-permute-done((bf16[128,2048]{1,0:T(8,128)(2,1)S(1)}, bf16[128,2048]{1,0:T(8,128)(2,1)}, u32[]{:S(2)}, u32[]{:S(2)}) %collective-permute-start.8) | collective-permute-done | bytes 524320 | tf_op jit(solution)/shard_map/ppermute | solution.py:446
  111.0 14.1 %project.2 = (bf16[1024,2048]{1,0:T(8,128)(2,1)}, bf16[1024,1536]{1,0:T(8,128)(2,1)}) custom-call(bf16[256,2048]{1,0:T(8,128)(2,1)} %get-tuple-element.366.refs_0_, bf16[256,2048]{1,0:T(8,128)(2,1)} %collective-permute-done.4.refs_1_, bf16[128,2048]{1,0:T(8,128)(2,1)} %collective-permute-done.8.refs_2_, bf16[128,2048]{1,0:T(8,128)(2,1)} %collective-permute-done.9.refs_3_, ...), custom_call_target="tpu_custom_call" | custom-call | flops 8053063680 | bytes 25165824 | tf_op jit(solution)/shard_map/project/pallas_call | solution.py:171
  134.6 16.5 %attend.2 = (bf16[1024,512]{1,0:T(8,128)(2,1)}, f32[4,2,1024]{2,1,0:T(2,128)}) custom-call(s32[4]{0:T(128)} %subtract_and_fusion.steps, bf16[1024,1536]{1,0:T(8,128)(2,1)} %get-tuple-element.375.q_ref.k_ref.v_ref, bf16[1024,1536]{1,0:T(8,128)(2,1)} %get-tuple-element.375.q_ref.k_ref.v_ref, bf16[1024,1536]{1,0:T(8,128)(2,1)} %get-tuple-element.375.q_ref.k_ref.v_ref), custom_call_target="tpu_custom_call" | custom-call | flops 8589934592 | bytes 26843544 | tf_op jit(solution)/shard_map/attend/pallas_call | solution.py:603
  163.0 14.0 %project.3 = (bf16[1024,2048]{1,0:T(8,128)(2,1)}, bf16[1024,1536]{1,0:T(8,128)(2,1)}) custom-call(bf16[256,2048]{1,0:T(8,128)(2,1)} %get-tuple-element.392.refs_0_, bf16[256,2048]{1,0:T(8,128)(2,1)} %collective-permute-done.16.refs_1_, bf16[128,2048]{1,0:T(8,128)(2,1)} %copy-done.69, bf16[128,2048]{1,0:T(8,128)(2,1)} %copy-done.71, ...), custom_call_target="tpu_custom_call" | custom-call | flops 8053063680 | bytes 25165824 | tf_op jit(solution)/shard_map/project/pallas_call | solution.py:171
  185.8 16.6 %attend.3 = (bf16[1024,512]{1,0:T(8,128)(2,1)}, f32[4,2,1024]{2,1,0:T(2,128)}) custom-call(s32[4]{0:T(128)} %subtract_and_fusion.steps, bf16[1024,1536]{1,0:T(8,128)(2,1)} %get-tuple-element.402.q_ref.k_ref.v_ref, bf16[1024,1536]{1,0:T(8,128)(2,1)} %get-tuple-element.402.q_ref.k_ref.v_ref, bf16[1024,1536]{1,0:T(8,128)(2,1)} %get-tuple-element.402.q_ref.k_ref.v_ref), custom_call_target="tpu_custom_call" | custom-call | flops 8589934592 | bytes 26843544 | tf_op jit(solution)/shard_map/attend/pallas_call | solution.py:603
  232.9 13.7 %matmul.14.refs_5_ = bf16[1024,2048]{1,0:T(8,128)(2,1)} custom-call(bf16[256,2048]{1,0:T(8,128)(2,1)} %copy-done.17, bf16[256,2048]{1,0:T(8,128)(2,1)} %copy-done.45, bf16[128,2048]{1,0:T(8,128)(2,1)} %collective-permute-done.29.refs_2_.refs_4_, bf16[128,2048]{1,0:T(8,128)(2,1)} %collective-permute-done.30.refs_3_.refs_5_, bf16[256,2048]{1,0:T(8,128)(2,1)} %copy-done.44, ...), custom_call_target="tpu_custom_call" | custom-call | flops 7516192768 | bytes 23488102 | tf_op jit(solution)/shard_map/matmul/pallas_call | solution.py:89
  258.8 18.2 %collective-permute-done.23.refs_1_ = bf16[256,2048]{1,0:T(8,128)(2,1)} collective-permute-done((bf16[256,2048]{1,0:T(8,128)(2,1)}, bf16[256,2048]{1,0:T(8,128)(2,1)}, u32[]{:S(2)}, u32[]{:S(2)}) %collective-permute-start.23) | collective-permute-done | bytes 1048608 | tf_op jit(solution)/shard_map/ppermute | solution.py:446
  307.1 19.0 %hidden_both.2 = (bf16[1024,2048]{1,0:T(8,128)(2,1)}, bf16[1024,2048]{1,0:T(8,128)(2,1)}, f32[1,2048]{1,0:T(1,128)}) custom-call(bf16[256,2048]{1,0:T(8,128)(2,1)} %get-tuple-element.537.refs_0_, bf16[256,2048]{1,0:T(8,128)(2,1)} %collective-permute-done.28.refs_1_, bf16[128,2048]{1,0:T(8,128)(2,1)} %collective-permute-done.33.refs_2_, ...), custom_call_target="tpu_custom_call" | custom-call | flops 10737418240 | bytes 33554432 | tf_op jit(solution)/shard_map/hidden_both/pallas_call | solution.py:203
  330.4 13.9 %collective-permute-done.35.refs_4_.refs_9_ = bf16[256,2048]{1,0:T(8,128)(2,1)S(1)} collective-permute-done((bf16[256,2048]{1,0:T(8,128)(2,1)}, bf16[256,2048]{1,0:T(8,128)(2,1)S(1)}, u32[]{:S(2)}, u32[]{:S(2)}) %collective-permute-start.35) | collective-permute-done | bytes 1048608 | tf_op jit(solution)/shard_map/ppermute | solution.py:446
  346.5 13.3 %matmul.15 = (bf16[256,2048]{1,0:T(8,128)(2,1)}, bf16[256,2048]{1,0:T(8,128)(2,1)}, bf16[256,2048]{1,0:T(8,128)(2,1)}, bf16[128,2048]{1,0:T(8,128)(2,1)}, bf16[128,2048]{1,0:T(8,128)(2,1)}) custom-call(bf16[1024,2048]{1,0:T(8,128)(2,1)} %get-tuple-element.475.refs_0_.refs_10_, bf16[2048,2048]{1,0:T(8,128)(2,1)} %all-gather.11.cloned.1.call-done.refs_6_.refs_1_), custom_call_target="tpu_custom_call" | custom-call | flops 7516192768 | bytes 23488102 | tf_op jit(solution)/shard_map/matmul/pallas_call | solution.py:89
  362.8 13.7 %matmul.16.refs_5_ = bf16[1024,2048]{1,0:T(8,128)(2,1)} custom-call(bf16[256,2048]{1,0:T(8,128)(2,1)} %copy-done.16, bf16[256,2048]{1,0:T(8,128)(2,1)} %collective-permute-done.38.refs_1_.refs_8_, bf16[128,2048]{1,0:T(8,128)(2,1)} %copy-done.70, bf16[128,2048]{1,0:T(8,128)(2,1)} %copy-done.72, bf16[256,2048]{1,0:T(8,128)(2,1)} %collective-permute-done.37.refs_4_.refs_11_, ...), custom_call_target="tpu_custom_call" | custom-call | flops 7516192768 | bytes 23488102 | tf_op jit(solution)/shard_map/matmul/pallas_call | solution.py:89
  378.1 19.0 %hidden_both.3 = (bf16[1024,2048]{1,0:T(8,128)(2,1)}, bf16[1024,2048]{1,0:T(8,128)(2,1)}, f32[1,2048]{1,0:T(1,128)}) custom-call(bf16[256,2048]{1,0:T(8,128)(2,1)} %get-tuple-element.542.refs_0_.refs_5_, bf16[256,2048]{1,0:T(8,128)(2,1)} %copy-done.47, bf16[128,2048]{1,0:T(8,128)(2,1)} %copy-done.65, bf16[128,2048]{1,0:T(8,128)(2,1)} %copy-done.66, ...), custom_call_target="tpu_custom_call" | custom-call | flops 10737418240 | bytes 33554432 | tf_op jit(solution)/shard_map/hidden_both/pallas_call | solution.py:203
  397.4 24.8 %weight_sum.4 = bf16[2048,2048]{1,0:T(8,128)(2,1)} custom-call(bf16[1024,2048]{1,0:T(8,128)(2,1)} %get-tuple-element.512.refs_0_, bf16[1024,2048]{1,0:T(8,128)(2,1)} %get-tuple-element.551.refs_1_.refs_0_, bf16[256,2048]{1,0:T(8,128)(2,1)} %copy-done.17, bf16[256,2048]{1,0:T(8,128)(2,1)} %copy-done.45, ...), custom_call_target="tpu_custom_call" | custom-call | flops 14173391872 | bytes 44291848 | tf_op jit(solution)/shard_map/weight_sum/pallas_call | solution.py:127
  424.4 13.8 %matmul.17 = (bf16[256,2048]{1,0:T(8,128)(2,1)}, bf16[256,2048]{1,0:T(8,128)(2,1)}, bf16[256,2048]{1,0:T(8,128)(2,1)}, bf16[128,2048]{1,0:T(8,128)(2,1)}, bf16[128,2048]{1,0:T(8,128)(2,1)}) custom-call(bf16[1024,2048]{1,0:T(8,128)(2,1)} %get-tuple-element.512.refs_0_, bf16[2048,2048]{1,0:T(8,128)(2,1)} %all-gather.9.cloned.1.call-done.refs_5_.refs_1_), custom_call_target="tpu_custom_call" | custom-call | flops 7516192768 | bytes 23488102 | tf_op jit(solution)/shard_map/matmul/pallas_call | solution.py:89
  448.2 13.4 %matmul.18 = (bf16[256,2048]{1,0:T(8,128)(2,1)}, bf16[256,2048]{1,0:T(8,128)(2,1)}, bf16[256,2048]{1,0:T(8,128)(2,1)}, bf16[128,2048]{1,0:T(8,128)(2,1)}, bf16[128,2048]{1,0:T(8,128)(2,1)}) custom-call(bf16[1024,2048]{1,0:T(8,128)(2,1)} %get-tuple-element.530.refs_0_.refs_11_, bf16[2048,2048]{1,0:T(8,128)(2,1)} %all-gather.11.cloned.1.call-done.refs_6_.refs_1_), custom_call_target="tpu_custom_call" | custom-call | flops 7516192768 | bytes 23488102 | tf_op jit(solution)/shard_map/matmul/pallas_call | solution.py:89
  464.0 24.4 %weight_sum.5 = bf16[2048,2048]{1,0:T(8,128)(2,1)} custom-call(bf16[256,2048]{1,0:T(8,128)(2,1)} %get-tuple-element.537.refs_0_, bf16[256,2048]{1,0:T(8,128)(2,1)} %collective-permute-done.28.refs_1_, bf16[128,2048]{1,0:T(8,128)(2,1)} %collective-permute-done.33.refs_2_, bf16[128,2048]{1,0:T(8,128)(2,1)} %collective-permute-done.34.refs_3_, ...), custom_call_target="tpu_custom_call" | custom-call | flops 14173391872 | bytes 44291848 | tf_op jit(solution)/shard_map/weight_sum/pallas_call | solution.py:127
  496.6 13.1 %matmul.19 = (bf16[256,2048]{1,0:T(8,128)(2,1)}, bf16[256,2048]{1,0:T(8,128)(2,1)}, bf16[256,2048]{1,0:T(8,128)(2,1)}, bf16[128,2048]{1,0:T(8,128)(2,1)}, bf16[128,2048]{1,0:T(8,128)(2,1)}) custom-call(bf16[1024,2048]{1,0:T(8,128)(2,1)} %get-tuple-element.551.refs_1_.refs_0_, bf16[2048,2048]{1,0:T(8,128)(2,1)} %all-gather.9.cloned.1.call-done.refs_5_.refs_1_), custom_call_target="tpu_custom_call" | custom-call | flops 7516192768 | bytes 23488102 | tf_op jit(solution)/shard_map/matmul/pallas_call | solution.py:89
  529.6 31.5 %attend_back.2.refs_0_.refs_2_ = bf16[1024,1536]{1,0:T(8,128)(2,1)} custom-call(s32[4]{0:T(128)} %subtract_and_fusion.steps, bf16[1024,1536]{1,0:T(8,128)(2,1)} %get-tuple-element.375.q_ref.k_ref.v_ref, bf16[1024,1536]{1,0:T(8,128)(2,1)} %get-tuple-element.375.q_ref.k_ref.v_ref, bf16[1024,1536]{1,0:T(8,128)(2,1)} %get-tuple-element.375.q_ref.k_ref.v_ref, ...), custom_call_target="tpu_custom_call" | custom-call | flops 17179869184 | bytes 53687092 | tf_op jit(solution)/shard_map/attend_back/pallas_call | solution.py:678
  569.2 10.6 %matmul.21 = (bf16[256,2048]{1,0:T(8,128)(2,1)}, bf16[256,2048]{1,0:T(8,128)(2,1)}, bf16[256,2048]{1,0:T(8,128)(2,1)}, bf16[128,2048]{1,0:T(8,128)(2,1)}, bf16[128,2048]{1,0:T(8,128)(2,1)}) custom-call(bf16[1024,1536]{1,0:T(8,128)(2,1)} %attend_back.2.refs_0_.refs_2_, bf16[2048,1536]{1,0:T(8,128)(2,1)} %all-gather.5.cloned.1.call-done.refs_7_.refs_1_), custom_call_target="tpu_custom_call" | custom-call | flops 5637144576 | bytes 17616076 | tf_op jit(solution)/shard_map/matmul/pallas_call | solution.py:89
  604.9 11.5 %collective-permute-done.66.refs_4_ = bf16[128,2048]{1,0:T(8,128)(2,1)} collective-permute-done((bf16[128,2048]{1,0:T(8,128)(2,1)S(1)}, bf16[128,2048]{1,0:T(8,128)(2,1)}, u32[]{:S(2)}, u32[]{:S(2)}) %collective-permute-start.66) | collective-permute-done | bytes 524320 | tf_op jit(solution)/shard_map/ppermute | solution.py:446
  622.1 31.6 %attend_back.3.refs_3_.refs_0_ = bf16[1024,1536]{1,0:T(8,128)(2,1)} custom-call(s32[4]{0:T(128)} %subtract_and_fusion.steps, bf16[1024,1536]{1,0:T(8,128)(2,1)} %get-tuple-element.402.q_ref.k_ref.v_ref, bf16[1024,1536]{1,0:T(8,128)(2,1)} %get-tuple-element.402.q_ref.k_ref.v_ref, bf16[1024,1536]{1,0:T(8,128)(2,1)} %get-tuple-element.402.q_ref.k_ref.v_ref, ...), custom_call_target="tpu_custom_call" | custom-call | flops 17179869184 | bytes 53687092 | tf_op jit(solution)/shard_map/attend_back/pallas_call | solution.py:678
  655.4 18.9 %weight_sum.7 = bf16[2048,1536]{1,0:T(8,128)(2,1)} custom-call(bf16[1024,2048]{1,0:T(8,128)(2,1)} %get-tuple-element.616.refs_0_, bf16[1024,2048]{1,0:T(8,128)(2,1)} %get-tuple-element.617.refs_1_, bf16[1024,1536]{1,0:T(8,128)(2,1)} %attend_back.2.refs_0_.refs_2_, bf16[1024,1536]{1,0:T(8,128)(2,1)} %attend_back.3.refs_3_.refs_0_), custom_call_target="tpu_custom_call" | custom-call | flops 10630043648 | bytes 33218888 | tf_op jit(solution)/shard_map/weight_sum/pallas_call | solution.py:127
  676.6 11.1 %matmul.23 = (bf16[256,2048]{1,0:T(8,128)(2,1)}, bf16[256,2048]{1,0:T(8,128)(2,1)}, bf16[256,2048]{1,0:T(8,128)(2,1)}, bf16[128,2048]{1,0:T(8,128)(2,1)}, bf16[128,2048]{1,0:T(8,128)(2,1)}) custom-call(bf16[1024,1536]{1,0:T(8,128)(2,1)} %attend_back.3.refs_3_.refs_0_, bf16[2048,1536]{1,0:T(8,128)(2,1)} %all-gather.5.cloned.1.call-done.refs_7_.refs_1_), custom_call_target="tpu_custom_call" | custom-call | flops 5637144576 | bytes 17616076 | tf_op jit(solution)/shard_map/matmul/pallas_call | solution.py:89
  (496 shorter events, 366.0 us)
Async XLA Ops:
  7.2 103.8 %all-gather.5.cloned.1.call-start = ((), (), s32[]{:S(2)}) async-start(), calls=%async_computation.4 | async-start | bytes 7077888 | tf_op jit(solution)/shard_map/all_gather | solution.py:720
  27.1 124.1 %all-gather.7.cloned.1.call-start = ((), (), s32[]{:S(2)}) async-start(), calls=%async_computation.5 | async-start | bytes 2359296 | tf_op jit(solution)/shard_map/all_gather | solution.py:720
  70.1 162.7 %all-gather.9.cloned.1.call-start = ((), (), s32[]{:S(2)}) async-start(), calls=%async_computation.6 | async-start | bytes 9437184 | tf_op jit(solution)/shard_map/all_gather | solution.py:720
  91.2 215.9 %all-gather.11.cloned.1.call-start = ((), (), s32[]{:S(2)}) async-start(), calls=%async_computation.7 | async-start | bytes 9437184 | tf_op jit(solution)/shard_map/all_gather | solution.py:720
  157.4 368.0 %reduce-scatter.5.cloned.1.call-start = ((), (), s32[]{:S(2)}) async-start(), calls=%async_computation.8 | async-start | bytes 9437184 | tf_op jit(solution)/shard_map/reduce_scatter | solution.py:721
  161.0 42.6 %collective-permute-start.21 = (bf16[256,2048]{1,0:T(8,128)(2,1)}, bf16[256,2048]{1,0:T(8,128)(2,1)S(1)}, u32[]{:S(2)}, u32[]{:S(2)}) collective-permute-start(bf16[256,2048]{1,0:T(8,128)(2,1)} %get-tuple-element.383), channel_id=1, source_target_pairs={{0,1},{1,3},{3,2},{2,0},{4,5},{5,7},{7,6},{6,4},{8,9},{9,11},{11,1... | collective-permute-start | bytes 3145736 | tf_op jit(solution)/shard_map/ppermute | solution.py:446
  161.6 43.3 %collective-permute-start.22 = (bf16[256,2048]{1,0:T(8,128)(2,1)}, bf16[256,2048]{1,0:T(8,128)(2,1)S(1)}, u32[]{:S(2)}, u32[]{:S(2)}) collective-permute-start(bf16[256,2048]{1,0:T(8,128)(2,1)} %get-tuple-element.384), channel_id=1, source_target_pairs={{0,2},{1,0},{3,1},{2,3},{4,6},{5,4},{7,5},{6,7},{8,10},{9,8},{11,9... | collective-permute-start | bytes 3145736 | tf_op jit(solution)/shard_map/ppermute | solution.py:446
  227.9 49.0 %collective-permute-start.23 = (bf16[256,2048]{1,0:T(8,128)(2,1)}, bf16[256,2048]{1,0:T(8,128)(2,1)}, u32[]{:S(2)}, u32[]{:S(2)}) collective-permute-start(bf16[256,2048]{1,0:T(8,128)(2,1)} %get-tuple-element.409), channel_id=1, source_target_pairs={{0,1},{1,3},{3,2},{2,0},{4,5},{5,7},{7,6},{6,4},{8,9},{9,11},{11,1... | collective-permute-start | bytes 3145736 | tf_op jit(solution)/shard_map/ppermute | solution.py:446
  232.1 44.9 %collective-permute-start.24 = (bf16[256,2048]{1,0:T(8,128)(2,1)}, bf16[256,2048]{1,0:T(8,128)(2,1)}, u32[]{:S(2)}, u32[]{:S(2)}) collective-permute-start(bf16[256,2048]{1,0:T(8,128)(2,1)} %get-tuple-element.410), channel_id=1, source_target_pairs={{0,2},{1,0},{3,1},{2,3},{4,6},{5,4},{7,5},{6,7},{8,10},{9,8},{11,9... | collective-permute-start | bytes 3145736 | tf_op jit(solution)/shard_map/ppermute | solution.py:446
  282.3 43.9 %collective-permute-start.37 = (bf16[256,2048]{1,0:T(8,128)(2,1)S(1)}, bf16[256,2048]{1,0:T(8,128)(2,1)}, u32[]{:S(2)}, u32[]{:S(2)}) collective-permute-start(bf16[256,2048]{1,0:T(8,128)(2,1)S(1)} %get-tuple-element.488.refs_0_.refs_7_), channel_id=1, source_target_pairs={{0,1},{1,3},{3,2},{2,0},{4,5},{5,7},{7,6},{6,4},{8,9},{9,11},{11,1... | collective-permute-start | bytes 3145736 | tf_op jit(solution)/shard_map/ppermute | solution.py:446
  288.2 37.9 %collective-permute-start.38 = (bf16[256,2048]{1,0:T(8,128)(2,1)S(1)}, bf16[256,2048]{1,0:T(8,128)(2,1)}, u32[]{:S(2)}, u32[]{:S(2)}) collective-permute-start(bf16[256,2048]{1,0:T(8,128)(2,1)S(1)} %get-tuple-element.488.refs_0_.refs_7_), channel_id=1, source_target_pairs={{0,2},{1,0},{3,1},{2,3},{4,6},{5,4},{7,5},{6,7},{8,10},{9,8},{11,9... | collective-permute-start | bytes 3145736 | tf_op jit(solution)/shard_map/ppermute | solution.py:446
  304.5 39.8 %collective-permute-start.35 = (bf16[256,2048]{1,0:T(8,128)(2,1)}, bf16[256,2048]{1,0:T(8,128)(2,1)S(1)}, u32[]{:S(2)}, u32[]{:S(2)}) collective-permute-start(bf16[256,2048]{1,0:T(8,128)(2,1)} %get-tuple-element.542.refs_0_.refs_5_), channel_id=1, source_target_pairs={{0,1},{1,3},{3,2},{2,0},{4,5},{5,7},{7,6},{6,4},{8,9},{9,11},{11,1... | collective-permute-start | bytes 3145736 | tf_op jit(solution)/shard_map/ppermute | solution.py:446
  305.9 38.4 %collective-permute-start.36 = (bf16[256,2048]{1,0:T(8,128)(2,1)}, bf16[256,2048]{1,0:T(8,128)(2,1)S(1)}, u32[]{:S(2)}, u32[]{:S(2)}) collective-permute-start(bf16[256,2048]{1,0:T(8,128)(2,1)} %get-tuple-element.542.refs_0_.refs_5_), channel_id=1, source_target_pairs={{0,2},{1,0},{3,1},{2,3},{4,6},{5,4},{7,5},{6,7},{8,10},{9,8},{11,9... | collective-permute-start | bytes 3145736 | tf_op jit(solution)/shard_map/ppermute | solution.py:446
  422.3 252.1 %reduce-scatter.7.cloned.1.call-start = ((), (), s32[]{:S(2)}) async-start(), calls=%async_computation.9 | async-start | bytes 9437184 | tf_op jit(solution)/shard_map/reduce_scatter | solution.py:721
  446.1 42.3 %collective-permute-start.49 = (bf16[256,2048]{1,0:T(8,128)(2,1)}, bf16[256,2048]{1,0:T(8,128)(2,1)S(1)}, u32[]{:S(2)}, u32[]{:S(2)}) collective-permute-start(bf16[256,2048]{1,0:T(8,128)(2,1)} %get-tuple-element.564.refs_0_.refs_2_), channel_id=1, source_target_pairs={{0,1},{1,3},{3,2},{2,0},{4,5},{5,7},{7,6},{6,4},{8,9},{9,11},{11,1... | collective-permute-start | bytes 3145736 | tf_op jit(solution)/shard_map/ppermute | solution.py:446
  447.6 40.8 %collective-permute-start.50 = (bf16[256,2048]{1,0:T(8,128)(2,1)}, bf16[256,2048]{1,0:T(8,128)(2,1)S(1)}, u32[]{:S(2)}, u32[]{:S(2)}) collective-permute-start(bf16[256,2048]{1,0:T(8,128)(2,1)} %get-tuple-element.564.refs_0_.refs_2_), channel_id=1, source_target_pairs={{0,2},{1,0},{3,1},{2,3},{4,6},{5,4},{7,5},{6,7},{8,10},{9,8},{11,9... | collective-permute-start | bytes 3145736 | tf_op jit(solution)/shard_map/ppermute | solution.py:446
  525.4 226.3 %reduce-scatter.9.cloned.1.call-start = ((), (), s32[]{:S(2)}) async-start(), calls=%async_computation.10 | async-start | bytes 7077888 | tf_op jit(solution)/shard_map/reduce_scatter | solution.py:721
  525.5 64.0 %collective-permute-start.61 = (bf16[256,2048]{1,0:T(8,128)(2,1)}, bf16[256,2048]{1,0:T(8,128)(2,1)S(1)}, u32[]{:S(2)}, u32[]{:S(2)}) collective-permute-start(bf16[256,2048]{1,0:T(8,128)(2,1)} %get-tuple-element.514), channel_id=1, source_target_pairs={{0,1},{1,3},{3,2},{2,0},{4,5},{5,7},{7,6},{6,4},{8,9},{9,11},{11,1... | collective-permute-start | bytes 3145736 | tf_op jit(solution)/shard_map/ppermute | solution.py:446
  526.6 62.9 %collective-permute-start.62 = (bf16[256,2048]{1,0:T(8,128)(2,1)S(1)}, bf16[256,2048]{1,0:T(8,128)(2,1)}, u32[]{:S(2)}, u32[]{:S(2)}) collective-permute-start(bf16[256,2048]{1,0:T(8,128)(2,1)S(1)} %copy-done.64), channel_id=1, source_target_pairs={{0,2},{1,0},{3,1},{2,3},{4,6},{5,4},{7,5},{6,7},{8,10},{9,8},{11,9... | collective-permute-start | bytes 3145736 | tf_op jit(solution)/shard_map/ppermute | solution.py:446
  527.6 39.3 %collective-permute-start.57 = (bf16[256,2048]{1,0:T(8,128)(2,1)S(1)}, bf16[256,2048]{1,0:T(8,128)(2,1)S(1)}, u32[]{:S(2)}, u32[]{:S(2)}) collective-permute-start(bf16[256,2048]{1,0:T(8,128)(2,1)S(1)} %copy-done.11), channel_id=1, source_target_pairs={{0,1},{1,3},{3,2},{2,0},{4,5},{5,7},{7,6},{6,4},{8,9},{9,11},{11,1... | collective-permute-start | bytes 3145736 | tf_op jit(solution)/shard_map/ppermute | solution.py:446
  528.6 38.2 %collective-permute-start.58 = (bf16[256,2048]{1,0:T(8,128)(2,1)S(1)}, bf16[256,2048]{1,0:T(8,128)(2,1)S(1)}, u32[]{:S(2)}, u32[]{:S(2)}) collective-permute-start(bf16[256,2048]{1,0:T(8,128)(2,1)S(1)} %copy-done.11), channel_id=1, source_target_pairs={{0,2},{1,0},{3,1},{2,3},{4,6},{5,4},{7,5},{6,7},{8,10},{9,8},{11,9... | collective-permute-start | bytes 3145736 | tf_op jit(solution)/shard_map/ppermute | solution.py:446
  579.9 37.7 %collective-permute-start.59 = (bf16[256,2048]{1,0:T(8,128)(2,1)}, bf16[256,2048]{1,0:T(8,128)(2,1)}, u32[]{:S(2)}, u32[]{:S(2)}) collective-permute-start(bf16[256,2048]{1,0:T(8,128)(2,1)} %get-tuple-element.587), channel_id=1, source_target_pairs={{0,1},{1,3},{3,2},{2,0},{4,5},{5,7},{7,6},{6,4},{8,9},{9,11},{11,1... | collective-permute-start | bytes 3145736 | tf_op jit(solution)/shard_map/ppermute | solution.py:446
  593.3 60.4 %collective-permute-start.51 = (bf16[256,2048]{1,0:T(8,128)(2,1)}, bf16[256,2048]{1,0:T(8,128)(2,1)}, u32[]{:S(2)}, u32[]{:S(2)}) collective-permute-start(bf16[256,2048]{1,0:T(8,128)(2,1)} %get-tuple-element.553), channel_id=1, source_target_pairs={{0,1},{1,3},{3,2},{2,0},{4,5},{5,7},{7,6},{6,4},{8,9},{9,11},{11,1... | collective-permute-start | bytes 3145736 | tf_op jit(solution)/shard_map/ppermute | solution.py:446
  674.4 111.3 %reduce-scatter.11.cloned.1.call-start = ((), (), s32[]{:S(2)}) async-start(), calls=%async_computation.11 | async-start | bytes 2359296 | tf_op jit(solution)/shard_map/reduce_scatter | solution.py:721
  (151 other events, 2827.6 us)
Sparse Core Ops, SparseCore 0:
  27.2 66.3 all-gather.4
  95.2 27.5 all-gather.6
  124.4 81.4 all-gather.8
  207.3 80.6 all-gather.10
  422.4 87.0 reduce-scatter.4
  525.6 85.7 reduce-scatter.6
  674.5 68.4 reduce-scatter.8
  751.9 33.8 reduce-scatter.10

commit v4 on v3

--- a/solution.py
+++ b/solution.py
@@ -903,15 +903,15 @@
     gx0 = begin(part)
     grad_branch[1] = gb1.result()
     context_back(1)
+    sum_o = gradient(context, grad_branch)
+    gx0.go()
     out0.go()
-    sum_o = gradient(context, grad_branch)
-    out0.arrive()
-    gx0.go()
-    out1 = begin(part_one)
     attention_back(1)
     gx0.arrive()
+    out0.arrive()
+    out1 = begin(part_one)
+    sum_qkv = gradient(normed, grad_qkv)
     out1.go()
-    sum_qkv = gradient(normed, grad_qkv)
     sum_qkv = scatter(after(clock.now(sum_qkv), sum_w_1))
     part = normed_back(1)
     out1.arrive()

time: 805 us -> 843 us (1.047)
  waiting for transfers between devices: 204 us -> 243 us
    ppermute x76, waiting for transfers between devices: 167 us -> 206 us  [send(): lax.ppermute(value, 'seq', [(self.order[i], self.order[(i + steps) % n])...]
  transfers between devices with their start and end apart: 94 -> 94, of which waited for: 45 -> 45; matrix products, arithmetic and copies ran while one was open for 5% -> 5% of each run, Pallas kernels for 50% -> 48%
where the time goes in v4:
time: 843 us; the launch traced here: 832 us
  Pallas kernels  426 us (51%)
  waiting for transfers between devices  243 us (29%)
  starting transfers between devices  89.4 us (11%)
  local copies, waits for them, and re-layouts  35.5 us (4%)
  other arithmetic  22.2 us (3%)
  between operations  16.6 us (2%)
    ppermute x76, waiting for transfers between devices, send(): lax.ppermute(value, 'seq', [(self.order[i], self.order[(i + steps) % n])...  206 us
    pallas_call x12, Pallas kernels, matmul(): pl.pallas_call(kernel, out_shape=tuple((jax.ShapeDtypeStruct((size, width...  128 us
    ppermute x76, starting transfers between devices, send(): lax.ppermute(value, 'seq', [(self.order[i], self.order[(i + steps) % n])...  79.1 us
    pallas_call x4, Pallas kernels, weight_sum(): pl.pallas_call(kernel, out_shape=jax.ShapeDtypeStruct((rows, width), bf16...  78.2 us
    pallas_call x2, Pallas kernels, attend_back(): pl.pallas_call(partial(attend_back_kernel, blocks, rows), out_shape=jax.S...  63.1 us
    pallas_call x2, Pallas kernels, hidden_both(): pl.pallas_call(kernel, out_shape=(jax.ShapeDtypeStruct((rows, width), bf1...  38.1 us
    pallas_call x2, Pallas kernels, attend(): pl.pallas_call(partial(attend_kernel, blocks, rows), out_shape=(jax.Shape...  33 us
    pallas_call x2, Pallas kernels, project(): pl.pallas_call(kernel, out_shape=(jax.ShapeDtypeStruct((rows, depth), bf1...  28.1 us
  transfers between devices with their start and end apart: 94, of which 45 were waited for; matrix products, arithmetic and copies ran while one was open for 5% of the time, Pallas kernels for 48%

profile of v4, /device:TPU:0, one launch (start us, length us, event | category | flops | bytes accessed | tf_op | source)
XLA Modules:
  0.0 832.1 jit_solution(18050107495554605751)
XLA Ops:
  37.2 24.1 %collective-permute-done.5 = bf16[1,64,2048]{2,1,0:T(8,128)(2,1)S(1)} collective-permute-done((bf16[1,64,2048]{2,1,0:T(8,128)(2,1)S(1)}, bf16[1,64,2048]{2,1,0:T(8,128)(2,1)S(1)}, u32[]{:S(2)}, u32[]{:S(2)}) %collective-permute-start.5) | collective-permute-done | bytes 262176 | tf_op jit(solution)/shard_map/ppermute | solution.py:446
  93.9 11.3 %collective-permute-done.8.refs_2_ = bf16[128,2048]{1,0:T(8,128)(2,1)} collective-permute-done((bf16[128,2048]{1,0:T(8,128)(2,1)S(1)}, bf16[128,2048]{1,0:T(8,128)(2,1)}, u32[]{:S(2)}, u32[]{:S(2)}) %collective-permute-start.8) | collective-permute-done | bytes 524320 | tf_op jit(solution)/shard_map/ppermute | solution.py:446
  111.0 14.1 %project.2 = (bf16[1024,2048]{1,0:T(8,128)(2,1)}, bf16[1024,1536]{1,0:T(8,128)(2,1)}) custom-call(bf16[256,2048]{1,0:T(8,128)(2,1)} %get-tuple-element.366.refs_0_, bf16[256,2048]{1,0:T(8,128)(2,1)} %collective-permute-done.4.refs_1_, bf16[128,2048]{1,0:T(8,128)(2,1)} %collective-permute-done.8.refs_2_, bf16[128,2048]{1,0:T(8,128)(2,1)} %collective-permute-done.9.refs_3_, ...), custom_call_target="tpu_custom_call" | custom-call | flops 8053063680 | bytes 25165824 | tf_op jit(solution)/shard_map/project/pallas_call | solution.py:171
  134.6 16.5 %attend.2 = (bf16[1024,512]{1,0:T(8,128)(2,1)}, f32[4,2,1024]{2,1,0:T(2,128)}) custom-call(s32[4]{0:T(128)} %subtract_and_fusion.steps, bf16[1024,1536]{1,0:T(8,128)(2,1)} %get-tuple-element.375.q_ref.k_ref.v_ref, bf16[1024,1536]{1,0:T(8,128)(2,1)} %get-tuple-element.375.q_ref.k_ref.v_ref, bf16[1024,1536]{1,0:T(8,128)(2,1)} %get-tuple-element.375.q_ref.k_ref.v_ref), custom_call_target="tpu_custom_call" | custom-call | flops 8589934592 | bytes 26843544 | tf_op jit(solution)/shard_map/attend/pallas_call | solution.py:603
  163.0 14.0 %project.3 = (bf16[1024,2048]{1,0:T(8,128)(2,1)}, bf16[1024,1536]{1,0:T(8,128)(2,1)}) custom-call(bf16[256,2048]{1,0:T(8,128)(2,1)} %get-tuple-element.392.refs_0_, bf16[256,2048]{1,0:T(8,128)(2,1)} %collective-permute-done.16.refs_1_, bf16[128,2048]{1,0:T(8,128)(2,1)} %copy-done.69, bf16[128,2048]{1,0:T(8,128)(2,1)} %copy-done.71, ...), custom_call_target="tpu_custom_call" | custom-call | flops 8053063680 | bytes 25165824 | tf_op jit(solution)/shard_map/project/pallas_call | solution.py:171
  185.8 16.6 %attend.3 = (bf16[1024,512]{1,0:T(8,128)(2,1)}, f32[4,2,1024]{2,1,0:T(2,128)}) custom-call(s32[4]{0:T(128)} %subtract_and_fusion.steps, bf16[1024,1536]{1,0:T(8,128)(2,1)} %get-tuple-element.402.q_ref.k_ref.v_ref, bf16[1024,1536]{1,0:T(8,128)(2,1)} %get-tuple-element.402.q_ref.k_ref.v_ref, bf16[1024,1536]{1,0:T(8,128)(2,1)} %get-tuple-element.402.q_ref.k_ref.v_ref), custom_call_target="tpu_custom_call" | custom-call | flops 8589934592 | bytes 26843544 | tf_op jit(solution)/shard_map/attend/pallas_call | solution.py:603
  232.9 13.7 %matmul.14.refs_5_ = bf16[1024,2048]{1,0:T(8,128)(2,1)} custom-call(bf16[256,2048]{1,0:T(8,128)(2,1)} %copy-done.17, bf16[256,2048]{1,0:T(8,128)(2,1)} %copy-done.44, bf16[128,2048]{1,0:T(8,128)(2,1)} %collective-permute-done.29.refs_2_.refs_4_, bf16[128,2048]{1,0:T(8,128)(2,1)} %collective-permute-done.30.refs_3_.refs_5_, bf16[256,2048]{1,0:T(8,128)(2,1)} %copy-done.43, ...), custom_call_target="tpu_custom_call" | custom-call | flops 7516192768 | bytes 23488102 | tf_op jit(solution)/shard_map/matmul/pallas_call | solution.py:89
  258.8 18.2 %collective-permute-done.23.refs_1_ = bf16[256,2048]{1,0:T(8,128)(2,1)} collective-permute-done((bf16[256,2048]{1,0:T(8,128)(2,1)}, bf16[256,2048]{1,0:T(8,128)(2,1)}, u32[]{:S(2)}, u32[]{:S(2)}) %collective-permute-start.23) | collective-permute-done | bytes 1048608 | tf_op jit(solution)/shard_map/ppermute | solution.py:446
  307.1 19.0 %hidden_both.2 = (bf16[1024,2048]{1,0:T(8,128)(2,1)}, bf16[1024,2048]{1,0:T(8,128)(2,1)}, f32[1,2048]{1,0:T(1,128)}) custom-call(bf16[256,2048]{1,0:T(8,128)(2,1)} %get-tuple-element.537.refs_0_, bf16[256,2048]{1,0:T(8,128)(2,1)} %collective-permute-done.28.refs_1_, bf16[128,2048]{1,0:T(8,128)(2,1)} %collective-permute-done.33.refs_2_, ...), custom_call_target="tpu_custom_call" | custom-call | flops 10737418240 | bytes 33554432 | tf_op jit(solution)/shard_map/hidden_both/pallas_call | solution.py:203
  330.4 13.8 %collective-permute-done.35.refs_4_.refs_9_ = bf16[256,2048]{1,0:T(8,128)(2,1)S(1)} collective-permute-done((bf16[256,2048]{1,0:T(8,128)(2,1)}, bf16[256,2048]{1,0:T(8,128)(2,1)S(1)}, u32[]{:S(2)}, u32[]{:S(2)}) %collective-permute-start.35) | collective-permute-done | bytes 1048608 | tf_op jit(solution)/shard_map/ppermute | solution.py:446
  346.4 13.3 %matmul.15 = (bf16[256,2048]{1,0:T(8,128)(2,1)}, bf16[256,2048]{1,0:T(8,128)(2,1)}, bf16[256,2048]{1,0:T(8,128)(2,1)}, bf16[128,2048]{1,0:T(8,128)(2,1)}, bf16[128,2048]{1,0:T(8,128)(2,1)}) custom-call(bf16[1024,2048]{1,0:T(8,128)(2,1)} %get-tuple-element.475.refs_0_.refs_10_, bf16[2048,2048]{1,0:T(8,128)(2,1)} %all-gather.11.cloned.1.call-done.refs_6_.refs_1_), custom_call_target="tpu_custom_call" | custom-call | flops 7516192768 | bytes 23488102 | tf_op jit(solution)/shard_map/matmul/pallas_call | solution.py:89
  362.8 13.7 %matmul.16.refs_5_ = bf16[1024,2048]{1,0:T(8,128)(2,1)} custom-call(bf16[256,2048]{1,0:T(8,128)(2,1)} %copy-done.16, bf16[256,2048]{1,0:T(8,128)(2,1)} %collective-permute-done.38.refs_1_.refs_8_, bf16[128,2048]{1,0:T(8,128)(2,1)} %copy-done.70, bf16[128,2048]{1,0:T(8,128)(2,1)} %copy-done.72, bf16[256,2048]{1,0:T(8,128)(2,1)} %collective-permute-done.37.refs_4_.refs_11_, ...), custom_call_target="tpu_custom_call" | custom-call | flops 7516192768 | bytes 23488102 | tf_op jit(solution)/shard_map/matmul/pallas_call | solution.py:89
  378.0 19.1 %hidden_both.3 = (bf16[1024,2048]{1,0:T(8,128)(2,1)}, bf16[1024,2048]{1,0:T(8,128)(2,1)}, f32[1,2048]{1,0:T(1,128)}) custom-call(bf16[256,2048]{1,0:T(8,128)(2,1)} %get-tuple-element.542.refs_0_.refs_5_, bf16[256,2048]{1,0:T(8,128)(2,1)} %copy-done.46, bf16[128,2048]{1,0:T(8,128)(2,1)} %copy-done.63, bf16[128,2048]{1,0:T(8,128)(2,1)} %copy-done.64, ...), custom_call_target="tpu_custom_call" | custom-call | flops 10737418240 | bytes 33554432 | tf_op jit(solution)/shard_map/hidden_both/pallas_call | solution.py:203
  397.4 24.8 %weight_sum.4 = bf16[2048,2048]{1,0:T(8,128)(2,1)} custom-call(bf16[1024,2048]{1,0:T(8,128)(2,1)} %get-tuple-element.512.refs_0_, bf16[1024,2048]{1,0:T(8,128)(2,1)} %get-tuple-element.551.refs_1_.refs_0_, bf16[256,2048]{1,0:T(8,128)(2,1)} %copy-done.17, bf16[256,2048]{1,0:T(8,128)(2,1)} %copy-done.44, ...), custom_call_target="tpu_custom_call" | custom-call | flops 14173391872 | bytes 44291848 | tf_op jit(solution)/shard_map/weight_sum/pallas_call | solution.py:127
  424.4 13.9 %matmul.17 = (bf16[256,2048]{1,0:T(8,128)(2,1)}, bf16[256,2048]{1,0:T(8,128)(2,1)}, bf16[256,2048]{1,0:T(8,128)(2,1)}, bf16[128,2048]{1,0:T(8,128)(2,1)}, bf16[128,2048]{1,0:T(8,128)(2,1)}) custom-call(bf16[1024,2048]{1,0:T(8,128)(2,1)} %get-tuple-element.512.refs_0_, bf16[2048,2048]{1,0:T(8,128)(2,1)} %all-gather.9.cloned.1.call-done.refs_5_.refs_1_), custom_call_target="tpu_custom_call" | custom-call | flops 7516192768 | bytes 23488102 | tf_op jit(solution)/shard_map/matmul/pallas_call | solution.py:89
  448.2 13.4 %matmul.18 = (bf16[256,2048]{1,0:T(8,128)(2,1)}, bf16[256,2048]{1,0:T(8,128)(2,1)}, bf16[256,2048]{1,0:T(8,128)(2,1)}, bf16[128,2048]{1,0:T(8,128)(2,1)}, bf16[128,2048]{1,0:T(8,128)(2,1)}) custom-call(bf16[1024,2048]{1,0:T(8,128)(2,1)} %get-tuple-element.530.refs_0_.refs_11_, bf16[2048,2048]{1,0:T(8,128)(2,1)} %all-gather.11.cloned.1.call-done.refs_6_.refs_1_), custom_call_target="tpu_custom_call" | custom-call | flops 7516192768 | bytes 23488102 | tf_op jit(solution)/shard_map/matmul/pallas_call | solution.py:89
  463.9 24.4 %weight_sum.5 = bf16[2048,2048]{1,0:T(8,128)(2,1)} custom-call(bf16[256,2048]{1,0:T(8,128)(2,1)} %get-tuple-element.537.refs_0_, bf16[256,2048]{1,0:T(8,128)(2,1)} %collective-permute-done.28.refs_1_, bf16[128,2048]{1,0:T(8,128)(2,1)} %collective-permute-done.33.refs_2_, bf16[128,2048]{1,0:T(8,128)(2,1)} %collective-permute-done.34.refs_3_, ...), custom_call_target="tpu_custom_call" | custom-call | flops 14173391872 | bytes 44291848 | tf_op jit(solution)/shard_map/weight_sum/pallas_call | solution.py:127
  496.6 13.1 %matmul.19 = (bf16[256,2048]{1,0:T(8,128)(2,1)}, bf16[256,2048]{1,0:T(8,128)(2,1)}, bf16[256,2048]{1,0:T(8,128)(2,1)}, bf16[128,2048]{1,0:T(8,128)(2,1)}, bf16[128,2048]{1,0:T(8,128)(2,1)}) custom-call(bf16[1024,2048]{1,0:T(8,128)(2,1)} %get-tuple-element.551.refs_1_.refs_0_, bf16[2048,2048]{1,0:T(8,128)(2,1)} %all-gather.9.cloned.1.call-done.refs_5_.refs_1_), custom_call_target="tpu_custom_call" | custom-call | flops 7516192768 | bytes 23488102 | tf_op jit(solution)/shard_map/matmul/pallas_call | solution.py:89
  528.6 31.5 %attend_back.2.refs_0_.refs_2_ = bf16[1024,1536]{1,0:T(8,128)(2,1)} custom-call(s32[4]{0:T(128)} %subtract_and_fusion.steps, bf16[1024,1536]{1,0:T(8,128)(2,1)} %get-tuple-element.375.q_ref.k_ref.v_ref, bf16[1024,1536]{1,0:T(8,128)(2,1)} %get-tuple-element.375.q_ref.k_ref.v_ref, bf16[1024,1536]{1,0:T(8,128)(2,1)} %get-tuple-element.375.q_ref.k_ref.v_ref, ...), custom_call_target="tpu_custom_call" | custom-call | flops 17179869184 | bytes 53687092 | tf_op jit(solution)/shard_map/attend_back/pallas_call | solution.py:678
  560.2 11.4 %matmul.21 = (bf16[256,2048]{1,0:T(8,128)(2,1)}, bf16[256,2048]{1,0:T(8,128)(2,1)}, bf16[256,2048]{1,0:T(8,128)(2,1)}, bf16[128,2048]{1,0:T(8,128)(2,1)}, bf16[128,2048]{1,0:T(8,128)(2,1)}) custom-call(bf16[1024,1536]{1,0:T(8,128)(2,1)} %attend_back.2.refs_0_.refs_2_, bf16[2048,1536]{1,0:T(8,128)(2,1)} %all-gather.5.cloned.1.call-done.refs_7_.refs_1_), custom_call_target="tpu_custom_call" | custom-call | flops 5637144576 | bytes 17616076 | tf_op jit(solution)/shard_map/matmul/pallas_call | solution.py:89
  576.1 33.1 %collective-permute-done.63.refs_2_.refs_9_ = bf16[128,2048]{1,0:T(8,128)(2,1)S(1)} collective-permute-done((bf16[128,2048]{1,0:T(8,128)(2,1)S(1)}, bf16[128,2048]{1,0:T(8,128)(2,1)S(1)}, u32[]{:S(2)}, u32[]{:S(2)}) %collective-permute-start.63) | collective-permute-done | bytes 524320 | tf_op jit(solution)/shard_map/ppermute | solution.py:446
  638.3 16.3 %collective-permute-done.68.refs_4_ = bf16[128,2048]{1,0:T(8,128)(2,1)S(1)} collective-permute-done((bf16[128,2048]{1,0:T(8,128)(2,1)S(1)}, bf16[128,2048]{1,0:T(8,128)(2,1)S(1)}, u32[]{:S(2)}, u32[]{:S(2)}) %collective-permute-start.68) | collective-permute-done | bytes 524320 | tf_op jit(solution)/shard_map/ppermute | solution.py:446
  655.4 31.6 %attend_back.3.refs_3_.refs_0_ = bf16[1024,1536]{1,0:T(8,128)(2,1)} custom-call(s32[4]{0:T(128)} %subtract_and_fusion.steps, bf16[1024,1536]{1,0:T(8,128)(2,1)} %get-tuple-element.402.q_ref.k_ref.v_ref, bf16[1024,1536]{1,0:T(8,128)(2,1)} %get-tuple-element.402.q_ref.k_ref.v_ref, bf16[1024,1536]{1,0:T(8,128)(2,1)} %get-tuple-element.402.q_ref.k_ref.v_ref, ...), custom_call_target="tpu_custom_call" | custom-call | flops 17179869184 | bytes 53687092 | tf_op jit(solution)/shard_map/attend_back/pallas_call | solution.py:678
  688.7 18.9 %weight_sum.7 = bf16[2048,1536]{1,0:T(8,128)(2,1)} custom-call(bf16[1024,2048]{1,0:T(8,128)(2,1)} %get-tuple-element.614.refs_0_, bf16[1024,2048]{1,0:T(8,128)(2,1)} %get-tuple-element.615.refs_1_, bf16[1024,1536]{1,0:T(8,128)(2,1)} %attend_back.2.refs_0_.refs_2_, bf16[1024,1536]{1,0:T(8,128)(2,1)} %attend_back.3.refs_3_.refs_0_), custom_call_target="tpu_custom_call" | custom-call | flops 10630043648 | bytes 33218888 | tf_op jit(solution)/shard_map/weight_sum/pallas_call | solution.py:127
  (496 shorter events, 376.1 us)
Async XLA Ops:
  7.2 103.8 %all-gather.5.cloned.1.call-start = ((), (), s32[]{:S(2)}) async-start(), calls=%async_computation.4 | async-start | bytes 7077888 | tf_op jit(solution)/shard_map/all_gather | solution.py:720
  27.1 124.1 %all-gather.7.cloned.1.call-start = ((), (), s32[]{:S(2)}) async-start(), calls=%async_computation.5 | async-start | bytes 2359296 | tf_op jit(solution)/shard_map/all_gather | solution.py:720
  70.1 162.7 %all-gather.9.cloned.1.call-start = ((), (), s32[]{:S(2)}) async-start(), calls=%async_computation.6 | async-start | bytes 9437184 | tf_op jit(solution)/shard_map/all_gather | solution.py:720
  91.2 216.0 %all-gather.11.cloned.1.call-start = ((), (), s32[]{:S(2)}) async-start(), calls=%async_computation.7 | async-start | bytes 9437184 | tf_op jit(solution)/shard_map/all_gather | solution.py:720
  157.4 367.9 %reduce-scatter.5.cloned.1.call-start = ((), (), s32[]{:S(2)}) async-start(), calls=%async_computation.8 | async-start | bytes 9437184 | tf_op jit(solution)/shard_map/reduce_scatter | solution.py:721
  161.0 42.5 %collective-permute-start.21 = (bf16[256,2048]{1,0:T(8,128)(2,1)}, bf16[256,2048]{1,0:T(8,128)(2,1)S(1)}, u32[]{:S(2)}, u32[]{:S(2)}) collective-permute-start(bf16[256,2048]{1,0:T(8,128)(2,1)} %get-tuple-element.383), channel_id=1, source_target_pairs={{0,1},{1,3},{3,2},{2,0},{4,5},{5,7},{7,6},{6,4},{8,9},{9,11},{11,1... | collective-permute-start | bytes 3145736 | tf_op jit(solution)/shard_map/ppermute | solution.py:446
  161.6 43.3 %collective-permute-start.22 = (bf16[256,2048]{1,0:T(8,128)(2,1)}, bf16[256,2048]{1,0:T(8,128)(2,1)S(1)}, u32[]{:S(2)}, u32[]{:S(2)}) collective-permute-start(bf16[256,2048]{1,0:T(8,128)(2,1)} %get-tuple-element.384), channel_id=1, source_target_pairs={{0,2},{1,0},{3,1},{2,3},{4,6},{5,4},{7,5},{6,7},{8,10},{9,8},{11,9... | collective-permute-start | bytes 3145736 | tf_op jit(solution)/shard_map/ppermute | solution.py:446
  227.9 49.0 %collective-permute-start.23 = (bf16[256,2048]{1,0:T(8,128)(2,1)}, bf16[256,2048]{1,0:T(8,128)(2,1)}, u32[]{:S(2)}, u32[]{:S(2)}) collective-permute-start(bf16[256,2048]{1,0:T(8,128)(2,1)} %get-tuple-element.409), channel_id=1, source_target_pairs={{0,1},{1,3},{3,2},{2,0},{4,5},{5,7},{7,6},{6,4},{8,9},{9,11},{11,1... | collective-permute-start | bytes 3145736 | tf_op jit(solution)/shard_map/ppermute | solution.py:446
  232.0 44.9 %collective-permute-start.24 = (bf16[256,2048]{1,0:T(8,128)(2,1)}, bf16[256,2048]{1,0:T(8,128)(2,1)}, u32[]{:S(2)}, u32[]{:S(2)}) collective-permute-start(bf16[256,2048]{1,0:T(8,128)(2,1)} %get-tuple-element.410), channel_id=1, source_target_pairs={{0,2},{1,0},{3,1},{2,3},{4,6},{5,4},{7,5},{6,7},{8,10},{9,8},{11,9... | collective-permute-start | bytes 3145736 | tf_op jit(solution)/shard_map/ppermute | solution.py:446
  282.2 43.9 %collective-permute-start.37 = (bf16[256,2048]{1,0:T(8,128)(2,1)S(1)}, bf16[256,2048]{1,0:T(8,128)(2,1)}, u32[]{:S(2)}, u32[]{:S(2)}) collective-permute-start(bf16[256,2048]{1,0:T(8,128)(2,1)S(1)} %get-tuple-element.488.refs_0_.refs_7_), channel_id=1, source_target_pairs={{0,1},{1,3},{3,2},{2,0},{4,5},{5,7},{7,6},{6,4},{8,9},{9,11},{11,1... | collective-permute-start | bytes 3145736 | tf_op jit(solution)/shard_map/ppermute | solution.py:446
  304.5 39.8 %collective-permute-start.35 = (bf16[256,2048]{1,0:T(8,128)(2,1)}, bf16[256,2048]{1,0:T(8,128)(2,1)S(1)}, u32[]{:S(2)}, u32[]{:S(2)}) collective-permute-start(bf16[256,2048]{1,0:T(8,128)(2,1)} %get-tuple-element.542.refs_0_.refs_5_), channel_id=1, source_target_pairs={{0,1},{1,3},{3,2},{2,0},{4,5},{5,7},{7,6},{6,4},{8,9},{9,11},{11,1... | collective-permute-start | bytes 3145736 | tf_op jit(solution)/shard_map/ppermute | solution.py:446
  305.9 38.3 %collective-permute-start.36 = (bf16[256,2048]{1,0:T(8,128)(2,1)}, bf16[256,2048]{1,0:T(8,128)(2,1)S(1)}, u32[]{:S(2)}, u32[]{:S(2)}) collective-permute-start(bf16[256,2048]{1,0:T(8,128)(2,1)} %get-tuple-element.542.refs_0_.refs_5_), channel_id=1, source_target_pairs={{0,2},{1,0},{3,1},{2,3},{4,6},{5,4},{7,5},{6,7},{8,10},{9,8},{11,9... | collective-permute-start | bytes 3145736 | tf_op jit(solution)/shard_map/ppermute | solution.py:446
  422.3 287.7 %reduce-scatter.7.cloned.1.call-start = ((), (), s32[]{:S(2)}) async-start(), calls=%async_computation.9 | async-start | bytes 9437184 | tf_op jit(solution)/shard_map/reduce_scatter | solution.py:721
  446.1 42.3 %collective-permute-start.49 = (bf16[256,2048]{1,0:T(8,128)(2,1)}, bf16[256,2048]{1,0:T(8,128)(2,1)S(1)}, u32[]{:S(2)}, u32[]{:S(2)}) collective-permute-start(bf16[256,2048]{1,0:T(8,128)(2,1)} %get-tuple-element.564.refs_0_.refs_2_), channel_id=1, source_target_pairs={{0,1},{1,3},{3,2},{2,0},{4,5},{5,7},{7,6},{6,4},{8,9},{9,11},{11,1... | collective-permute-start | bytes 3145736 | tf_op jit(solution)/shard_map/ppermute | solution.py:446
  447.5 40.8 %collective-permute-start.50 = (bf16[256,2048]{1,0:T(8,128)(2,1)}, bf16[256,2048]{1,0:T(8,128)(2,1)S(1)}, u32[]{:S(2)}, u32[]{:S(2)}) collective-permute-start(bf16[256,2048]{1,0:T(8,128)(2,1)} %get-tuple-element.564.refs_0_.refs_2_), channel_id=1, source_target_pairs={{0,2},{1,0},{3,1},{2,3},{4,6},{5,4},{7,5},{6,7},{8,10},{9,8},{11,9... | collective-permute-start | bytes 3145736 | tf_op jit(solution)/shard_map/ppermute | solution.py:446
  525.4 264.2 %reduce-scatter.9.cloned.1.call-start = ((), (), s32[]{:S(2)}) async-start(), calls=%async_computation.10 | async-start | bytes 7077888 | tf_op jit(solution)/shard_map/reduce_scatter | solution.py:721
  571.6 55.9 %collective-permute-start.61 = (bf16[256,2048]{1,0:T(8,128)(2,1)}, bf16[256,2048]{1,0:T(8,128)(2,1)S(1)}, u32[]{:S(2)}, u32[]{:S(2)}) collective-permute-start(bf16[256,2048]{1,0:T(8,128)(2,1)} %get-tuple-element.587), channel_id=1, source_target_pairs={{0,1},{1,3},{3,2},{2,0},{4,5},{5,7},{7,6},{6,4},{8,9},{9,11},{11,1... | collective-permute-start | bytes 3145736 | tf_op jit(solution)/shard_map/ppermute | solution.py:446
  572.1 55.9 %collective-permute-start.62 = (bf16[256,2048]{1,0:T(8,128)(2,1)}, bf16[256,2048]{1,0:T(8,128)(2,1)}, u32[]{:S(2)}, u32[]{:S(2)}) collective-permute-start(bf16[256,2048]{1,0:T(8,128)(2,1)} %get-tuple-element.588), channel_id=1, source_target_pairs={{0,2},{1,0},{3,1},{2,3},{4,6},{5,4},{7,5},{6,7},{8,10},{9,8},{11,9... | collective-permute-start | bytes 3145736 | tf_op jit(solution)/shard_map/ppermute | solution.py:446
  575.7 55.9 %collective-permute-start.53 = (bf16[256,2048]{1,0:T(8,128)(2,1)}, bf16[256,2048]{1,0:T(8,128)(2,1)}, u32[]{:S(2)}, u32[]{:S(2)}) collective-permute-start(bf16[256,2048]{1,0:T(8,128)(2,1)} %get-tuple-element.514), channel_id=1, source_target_pairs={{0,1},{1,3},{3,2},{2,0},{4,5},{5,7},{7,6},{6,4},{8,9},{9,11},{11,1... | collective-permute-start | bytes 3145736 | tf_op jit(solution)/shard_map/ppermute | solution.py:446
  609.5 98.0 %collective-permute-start.51 = (bf16[256,2048]{1,0:T(8,128)(2,1)}, bf16[256,2048]{1,0:T(8,128)(2,1)}, u32[]{:S(2)}, u32[]{:S(2)}) collective-permute-start(bf16[256,2048]{1,0:T(8,128)(2,1)} %get-tuple-element.553), channel_id=1, source_target_pairs={{0,1},{1,3},{3,2},{2,0},{4,5},{5,7},{7,6},{6,4},{8,9},{9,11},{11,1... | collective-permute-start | bytes 3145736 | tf_op jit(solution)/shard_map/ppermute | solution.py:446
  627.5 80.0 %collective-permute-start.52 = (bf16[256,2048]{1,0:T(8,128)(2,1)}, bf16[256,2048]{1,0:T(8,128)(2,1)}, u32[]{:S(2)}, u32[]{:S(2)}) collective-permute-start(bf16[256,2048]{1,0:T(8,128)(2,1)} %get-tuple-element.554), channel_id=1, source_target_pairs={{0,2},{1,0},{3,1},{2,3},{4,6},{5,4},{7,5},{6,7},{8,10},{9,8},{11,9... | collective-permute-start | bytes 3145736 | tf_op jit(solution)/shard_map/ppermute | solution.py:446
  631.6 55.4 %collective-permute-start.67 = (bf16[128,2048]{1,0:T(8,128)(2,1)S(1)}, bf16[128,2048]{1,0:T(8,128)(2,1)S(1)}, u32[]{:S(2)}, u32[]{:S(2)}) collective-permute-start(bf16[128,2048]{1,0:T(8,128)(2,1)S(1)} %add_convert_fusion.7), channel_id=1, source_target_pairs={{0,1},{1,3},{3,2},{2,0},{4,5},{5,7},{7,6},{6,4},{8,9},{9,11},{11,1... | collective-permute-start | bytes 1572872 | tf_op jit(solution)/shard_map/ppermute | solution.py:446
  636.8 50.3 %collective-permute-start.66 = (bf16[128,2048]{1,0:T(8,128)(2,1)S(1)}, bf16[128,2048]{1,0:T(8,128)(2,1)S(1)}, u32[]{:S(2)}, u32[]{:S(2)}) collective-permute-start(bf16[128,2048]{1,0:T(8,128)(2,1)S(1)} %add_convert_fusion.4), channel_id=1, source_target_pairs={{0,2},{1,0},{3,1},{2,3},{4,6},{5,4},{7,5},{6,7},{8,10},{9,8},{11,9... | collective-permute-start | bytes 1572872 | tf_op jit(solution)/shard_map/ppermute | solution.py:446
  710.0 113.3 %reduce-scatter.11.cloned.1.call-start = ((), (), s32[]{:S(2)}) async-start(), calls=%async_computation.11 | async-start | bytes 2359296 | tf_op jit(solution)/shard_map/reduce_scatter | solution.py:721
  (151 other events, 2871.8 us)
Sparse Core Ops, SparseCore 0:
  27.2 66.3 all-gather.4
  95.2 27.5 all-gather.6
  124.4 81.4 all-gather.8
  207.3 80.6 all-gather.10
  422.4 87.0 reduce-scatter.4
  525.5 85.8 reduce-scatter.6
  710.1 68.6 reduce-scatter.8
  789.8 33.4 reduce-scatter.10
